TPU v7x, 32 devices: a whole 2x2x4 slice. The times are simulated.
32 devices in a mesh: group: 2 (over y), tensor: 4 (over z), seq: 4 (over x, core).
Axes of the slice: x: 2, y: 2, z: 4, core: 2. Of those that a mesh axis runs over, the one named last changes fastest.
Arguments:
- tokens: bfloat16 [5120, 3584], P(('group', 'seq', 'tensor')), parts along dimension 0, may hold values from -24 to 24
- cotangent: bfloat16 [5120, 3584], P(('group', 'seq', 'tensor')), parts along dimension 0, may hold values from -6 to 6
- modulation: float32 [6, 3584], P('group'), parts along dimension 0, may hold values from -1 to 1
- w_qkv: bfloat16 [3584, 3, 512], P(None, None, 'tensor'), may hold values from -0.09375 to 0.09375
- w_out: bfloat16 [512, 3584], P('tensor'), may hold values from -0.25 to 0.25
- qk_gain: float32 [2, 128], replicated, may hold values from 0.5 to 3
Outputs:
- input_grad: float32 [5120, 3584], P(('group', 'seq', 'tensor')), parts along dimension 0
There are 2 independent parts, one for each index of `group`. A program takes and returns all parts, laid end to end along the dimension named above; an argument that names none is the same for every part. Nothing has to cross between parts.
All inputs are finite; a program needn't handle non-finite values.
Results may differ from a plain program's by a relative error of at most 0.019.
Values may be sent and summed in bfloat16 or wider, within the bound.
No kernel may reach another device: no remote copies, remote signals or barrier semaphores. Data moves between devices by JAX's collectives and lax.ppermute only.
A program may use at most 64 MiB of HBM per device.

v0:
```python
import math

import jax
import jax.numpy as jnp
from jax import lax
from jax.sharding import PartitionSpec as P


def head_norm(raw, gain):
    scale_back = lax.rsqrt(jnp.mean(raw * raw, axis=-1, keepdims=True) + 1e-06)
    return (raw * scale_back * gain, scale_back)


def head_norm_back(raw, scale_back, gain, upstream):
    scaled_up = upstream * gain
    return scale_back * scaled_up - raw * scale_back**3 * jnp.mean(
        raw * scaled_up, axis=-1, keepdims=True
    )


def body(tokens, cotangent, modulation, w_qkv, w_out, qk_gain):
    head_dim = qk_gain.shape[1]
    width = w_out.shape[0]
    nheads = width // head_dim
    model_width = tokens.shape[1]
    inv_sqrt = 1.0 / math.sqrt(head_dim)
    modulation_shift = modulation[0]
    modulation_scale = modulation[1]
    gate = modulation[2]
    input_rows_all = tokens.astype(jnp.float32)
    inverse_stddev = lax.rsqrt(
        jnp.mean(input_rows_all * input_rows_all, axis=-1, keepdims=True) + 1e-06
    )
    centered_normalized = input_rows_all * inverse_stddev
    layer_normed = (centered_normalized * (1.0 + modulation_scale) + modulation_shift).astype(
        jnp.bfloat16
    )
    cotangent_rows_all = cotangent.astype(jnp.float32)
    scaled_grad = (cotangent_rows_all * gate).astype(jnp.bfloat16)
    flat_in = w_qkv.reshape(model_width, 3 * width)
    qkv = jnp.dot(
        lax.all_gather(layer_normed, "tensor", axis=0, tiled=True),
        flat_in,
        preferred_element_type=jnp.float32,
    )
    rows = qkv.shape[0]
    query = qkv[:, :width].reshape(rows, nheads, head_dim)
    keys = qkv[:, width : 2 * width].reshape(rows, nheads, head_dim)
    values = qkv[:, 2 * width :].reshape(rows, nheads, head_dim)
    query_n, query_rs = head_norm(query, qk_gain[0])
    keys_n, keys_rs = head_norm(keys, qk_gain[1])
    query_b = query_n.astype(jnp.bfloat16)
    keys_b = keys_n.astype(jnp.bfloat16).reshape(rows, width)
    values_b = values.astype(jnp.bfloat16).reshape(rows, width)
    keys_all, values_all = (
        lax.all_gather(keys_b, "seq", axis=0, tiled=True),
        lax.all_gather(values_b, "seq", axis=0, tiled=True),
    )
    total = keys_all.shape[0]
    block = min(total, 512)
    count_blocks = total // block
    key_stack = keys_all.reshape(count_blocks, block, nheads, head_dim)
    value_stack = values_all.reshape(count_blocks, block, nheads, head_dim)

    def block_scores(queries, block_keys):
        return (
            jnp.einsum("qhd,khd->hqk", queries, block_keys, preferred_element_type=jnp.float32)
            * inv_sqrt
        )

    def stats_step(carry, block_keys):
        row_max, row_sum = carry
        scores = block_scores(query_b, block_keys)
        new_max = jnp.maximum(row_max, jnp.max(scores, axis=-1))
        row_sum = row_sum * jnp.exp(row_max - new_max) + jnp.sum(
            jnp.exp(scores - new_max[..., None]), axis=-1
        )
        return ((new_max, row_sum), None)

    start_max = jnp.full((nheads, rows), -jnp.inf, jnp.float32)
    start_sum = jnp.zeros((nheads, rows), jnp.float32)
    (row_max, row_sum), _ = lax.scan(stats_step, (start_max, start_sum), key_stack)

    def probs_of(scores, bmax, bsum):
        return jnp.exp(scores - bmax[..., None]) / bsum[..., None]

    def output_step(acc, pair):
        weights_b = probs_of(block_scores(query_b, pair[0]), row_max, row_sum).astype(jnp.bfloat16)
        return (
            acc
            + jnp.einsum("hqk,khd->hqd", weights_b, pair[1], preferred_element_type=jnp.float32),
            None,
        )

    attn_acc, _ = lax.scan(
        output_step, jnp.zeros((nheads, rows, head_dim), jnp.float32), (key_stack, value_stack)
    )
    attn_b = attn_acc.astype(jnp.bfloat16)
    dout = lax.dot_general(
        lax.all_gather(scaled_grad, "tensor", axis=0, tiled=True),
        w_out,
        (((1,), (1,)), ((), ())),
        preferred_element_type=jnp.float32,
    )
    grad_b = dout.astype(jnp.bfloat16)
    grad_q = grad_b.reshape(rows, nheads, head_dim)
    delta = jnp.sum(
        jnp.transpose(grad_q, (1, 0, 2)).astype(jnp.float32) * attn_b.astype(jnp.float32), axis=-1
    )

    def grad_terms(queries, grads, block_keys, block_values, bmax, bsum, bdelta):
        weights = probs_of(block_scores(queries, block_keys), bmax, bsum)
        dprob = jnp.einsum("qhd,khd->hqk", grads, block_values, preferred_element_type=jnp.float32)
        dscore = (weights * (dprob - bdelta[..., None])).astype(jnp.bfloat16)
        return (weights.astype(jnp.bfloat16), dscore)

    zeros_heads = jnp.zeros((nheads, rows, head_dim), jnp.float32)

    def both_step(acc, pair):
        weights_b, dscore = grad_terms(query_b, grad_q, pair[0], pair[1], row_max, row_sum, delta)
        acc = (
            acc
            + jnp.einsum("hqk,khd->hqd", dscore, pair[0], preferred_element_type=jnp.float32)
            * inv_sqrt
        )
        dkey_part = (
            jnp.einsum("hqk,qhd->khd", dscore, query_b, preferred_element_type=jnp.float32)
            * inv_sqrt
        )
        dvalue_part = jnp.einsum(
            "hqk,qhd->khd", weights_b, grad_q, preferred_element_type=jnp.float32
        )
        return (
            acc,
            jnp.concatenate(
                [dkey_part.reshape(block, width), dvalue_part.reshape(block, width)], axis=1
            ),
        )

    dquery, key_terms = lax.scan(both_step, zeros_heads, (key_stack, value_stack))
    own_terms = lax.psum_scatter(
        key_terms.reshape(total, 2 * width).astype(jnp.bfloat16),
        "seq",
        scatter_dimension=0,
        tiled=True,
    ).astype(jnp.float32)
    dkey = own_terms[:, :width].reshape(rows, nheads, head_dim)
    dvalue = own_terms[:, width:].reshape(rows, nheads, head_dim)
    dquery = jnp.transpose(dquery, (1, 0, 2))
    dq_raw = head_norm_back(query, query_rs, qk_gain[0], dquery)
    dk_raw = head_norm_back(keys, keys_rs, qk_gain[1], dkey)
    dqkv = jnp.concatenate(
        [dq_raw.reshape(rows, width), dk_raw.reshape(rows, width), dvalue.reshape(rows, width)],
        axis=1,
    ).astype(jnp.bfloat16)
    dnormed = lax.psum_scatter(
        lax.dot_general(
            dqkv, flat_in, (((1,), (1,)), ((), ())), preferred_element_type=jnp.float32
        ).astype(jnp.bfloat16),
        "tensor",
        scatter_dimension=0,
        tiled=True,
    ).astype(jnp.float32)
    normalized_grad = dnormed * (1.0 + modulation_scale)
    final_output = cotangent_rows_all + inverse_stddev * (
        normalized_grad
        - centered_normalized
        * jnp.mean(normalized_grad * centered_normalized, axis=-1, keepdims=True)
    )
    return final_output


def solution(mesh):
    placed = (
        P(("group", "seq", "tensor"), None),
        P(("group", "seq", "tensor"), None),
        P("group", None),
        P(None, None, "tensor"),
        P("tensor", None),
        P(),
    )
    return jax.shard_map(
        body,
        mesh=mesh,
        in_specs=placed,
        out_specs=P(("group", "seq", "tensor"), None),
        check_vma=False,
    )
```

profile of v0, /device:TPU:0, one launch (start us, length us, event | category | flops | bytes accessed | tf_op | source)
XLA Modules:
  0.0 351.8 jit_solution(12158047451510148496)
XLA Ops:
  6.5 1.1 slice_reduce_fusion
  7.7 1.6 fusion.58
  9.3 1.5 fusion.54
  10.8 1.2 copy-done.7
  12.0 1.2 fusion.52
  13.4 4.6 %copy.35 = bf16[3584,3,128]{0,2,1:T(8,128)(2,1)} copy(bf16[3584,3,128]{2,0,1:T(8,128)(2,1)} %param.15) | data formatting | bytes 5505024 | tf_op args[3]
  18.0 82.9 %all-gather.3.cloned.1.call-done = bf16[640,3584]{1,0:T(8,128)(2,1)} async-done(((bf16[160,3584]{1,0:T(8,128)(2,1)}), bf16[640,3584]{1,0:T(8,128)(2,1)}) %all-gather.3.cloned.1.call-update) | async-done | bytes 4587536 | tf_op jit(solution)/shard_map/all_gather | solution.py:42
  100.9 5.5 %fusion.70 = f32[640,384]{0,1:T(8,128)S(1)} fusion(bf16[640,3584]{1,0:T(8,128)(2,1)} %all-gather.3.cloned.1.call-done, bf16[3584,384]{0,1:T(8,128)(2,1)} %bitcast.119), kind=kOutput, calls=%fused_computation.110 | convolution fusion | flops 1761607680 | bytes 8323072 | tf_op jit(solution)/shard_map/dot_general | solution.py:41
  106.5 0.7 multiply_multiply_fusion
  107.4 8.3 %all_gather.13 = bf16[2560,128]{0,1:T(8,128)(2,1)} all-gather(bf16[640,128]{0,1:T(8,128)(2,1)S(1)} %get-tuple-element.327), channel_id=1, replica_groups=mesh['group'=2,'tensor'=4,'seq'=4] {'seq'}, dimensions={0}, use_global_device_ids=true | all-gather | bytes 819200 | tf_op jit(solution)/shard_map/all_gather | solution.py:56
  115.7 1.4 copy.36
  117.3 8.0 %all_gather.14 = bf16[2560,128]{0,1:T(8,128)(2,1)S(1)} all-gather(bf16[640,128]{0,1:T(8,128)(2,1)S(1)} %slice.74), channel_id=1, replica_groups=mesh['group'=2,'tensor'=4,'seq'=4] {'seq'}, dimensions={0}, use_global_device_ids=true | all-gather | bytes 819200 | tf_op jit(solution)/shard_map/all_gather | solution.py:57
  125.3 1.1 copy.39
  126.4 3.2 while.37
  129.6 12.0 %while.38 = (s32[]{:T(128)}, f32[1,640,128]{2,1,0:T(8,128)}, bf16[5,512,1,128]{3,1,2,0:T(8,128)(2,1)S(1)}, bf16[640,1,128]{2,0,1:T(8,128)(2,1)S(1)}, f32[1,640]{...) while((s32[]{:T(128)}, f32[1,640,128]{2,1,0:T(8,128)}, ...), condition=%wide.region_8.9_spmd.clone, body=%wide.region_7.8_spmd.clone.sunk | while | flops 169246720 | bytes 1100919 | solution.py:95
  129.7 2.3 fusion.105
  131.9 2.4 fusion.105
  134.4 2.4 fusion.105
  136.8 2.4 fusion.105
  139.2 2.4 fusion.105
  141.6 1.1 copy.43
  142.8 45.5 %all-gather.5.cloned.1.call-done = bf16[640,3584]{1,0:T(8,128)(2,1)} async-done(((bf16[160,3584]{1,0:T(8,128)(2,1)}), bf16[640,3584]{1,0:T(8,128)(2,1)}) %all-gather.5.cloned.1.call-update) | async-done | bytes 4587536 | tf_op jit(solution)/shard_map/all_gather | solution.py:100
  188.2 3.8 %fusion.64 = (f32[640]{0:T(1024)S(1)}, bf16[640,128]{0,1:T(8,128)(2,1)S(1)}) fusion(bf16[1,640,128]{1,2,0:T(8,128)(2,1)S(1)} %copy.43, bf16[640,3584]{1,0:T(8,128)(2,1)} %all-gather.5.cloned.1.call-done, bf16[128,3584]{1,0:T(8,128)(2,1)S(1)} %copy-done), kind=kOutput, calls=%fused_computation.81 | convolution fusion | flops 587611520 | bytes 5835264 | tf_op jit(solution)/shard_map/dot_general | solution.py:99
  192.2 32.2 %while.39 = (s32[]{:T(128)}, f32[1,640,128]{2,1,0:T(8,128)S(1)}, bf16[5,512,256]{2,1,0:T(8,128)(2,1)}, bf16[5,512,1,128]{3,1,2,0:T(8,128)(2,1)S(1)}, bf16[640,1,...) while((s32[]{:T(128)}, f32[1,640,128]{2,1,0:T(8,128)S(1)}, ...), condition=%wide.region_11.12_spmd.clone, body=%wide.region_10.11_spmd.clone.sunk | while | flops 422625280 | bytes 14705355 | solution.py:140
  192.3 0.8 copy-done.5
  193.1 1.3 fusion.116
  194.4 1.2 fusion.117
  195.7 0.4 convolution_multiply_fusion.6
  196.0 0.4 fusion.119
  196.6 0.7 constant_dynamic-update-slice_fusion.2
  197.3 1.4 fusion.118
  198.7 0.8 copy-done.5
  199.5 1.3 fusion.116
  200.9 1.2 fusion.117
  202.1 0.4 convolution_multiply_fusion.6
  202.5 0.4 fusion.119
  203.0 0.7 constant_dynamic-update-slice_fusion.2
  203.7 1.4 fusion.118
  205.2 0.8 copy-done.5
  206.0 1.3 fusion.116
  207.3 1.2 fusion.117
  208.5 0.4 convolution_multiply_fusion.6
  208.9 0.4 fusion.119
  209.4 0.7 constant_dynamic-update-slice_fusion.2
  210.2 1.4 fusion.118
  211.6 0.8 copy-done.5
  212.4 1.3 fusion.116
  213.7 1.2 fusion.117
  215.0 0.4 convolution_multiply_fusion.6
  215.3 0.4 fusion.119
  215.9 0.7 constant_dynamic-update-slice_fusion.2
  216.6 1.4 fusion.118
  218.0 0.8 copy-done.5
  218.8 1.3 fusion.116
  220.2 1.2 fusion.117
  221.8 0.4 fusion.119
  222.3 0.7 constant_dynamic-update-slice_fusion.2
  223.0 1.4 fusion.118
  224.9 24.7 %reduce-scatter.7.cloned.1.call-done = bf16[640,256]{1,0:T(8,128)(2,1)} async-done(((bf16[2560,256]{1,0:T(8,128)(2,1)}), bf16[640,256]{1,0:T(8,128)(2,1)}) %reduce-scatter.7.cloned.1.call-update) | async-done | bytes 327696
  249.6 1.0 fusion.69
  251.4 6.4 %convolution_convert_fusion = bf16[640,3584]{1,0:T(8,128)(2,1)} fusion(bf16[3584,384]{0,1:T(8,128)(2,1)} %bitcast.120, bf16[640,128]{0,1:T(8,128)(2,1)S(1)} %copy.56, bf16[640,128]{0,1:T(8,128)(2,1)S(1)} %get-tuple-element.325, bf16[640,128]{0,1:T(8,128)(2,1)S(1)} %get-tuple-element.324), kind=kOutput, calls=%fused_computation.57 | convolution fusion | flops 1765376000 | bytes 7831552 | tf_op jit(solution)/shard_map/dot_general | solution.py:157
  257.8 83.3 %reduce-scatter.5.cloned.1.call-done = bf16[160,3584]{1,0:T(8,128)(2,1)} async-done(((bf16[640,3584]{1,0:T(8,128)(2,1)}), bf16[160,3584]{1,0:T(8,128)(2,1)}) %reduce-scatter.5.cloned.1.call-update) | async-done | bytes 1146896 | tf_op jit(solution)/shard_map/reduce_scatter | solution.py:156
  341.1 2.0 fusion.55
  343.1 2.1 convert_add_fusion
  (150 shorter events, 6.4 us)
Async XLA Ops:
  6.5 181.7 %copy-start = (bf16[128,3584]{1,0:T(8,128)(2,1)S(1)}, bf16[128,3584]{1,0:T(8,128)(2,1)}, u32[]{:S(2)}) copy-start(bf16[128,3584]{1,0:T(8,128)(2,1)} %param.16) | copy-start | bytes 2752516
  6.5 2.7 copy-start.1
  6.5 94.3 %all-gather.3.cloned.1.call-start = ((), (), s32[]{:S(2)}) async-start(), calls=%async_computation.2 | async-start | bytes 5734400 | tf_op jit(solution)/shard_map/all_gather | solution.py:42
  7.7 3.1 copy-start.10
  9.3 1.5 copy-start.18
  10.8 1.3 copy-start.7
  10.8 177.4 %all-gather.5.cloned.1.call-start = ((), (), s32[]{:S(2)}) async-start(), calls=%async_computation.3 | async-start | bytes 5734400 | tf_op jit(solution)/shard_map/all_gather | solution.py:100
  13.3 236.4 %reduce-scatter.7.cloned.1.call-start = ((), (), s32[]{:S(2)}) async-start(), calls=%async_computation.5 | async-start | bytes 1638400
  13.3 4.6 %copy-start.24 = (f32[2,128]{1,0:T(2,128)S(1)}, f32[2,128]{1,0:T(2,128)}, u32[]{:S(2)}) copy-start(f32[2,128]{1,0:T(2,128)} %param.17) | copy-start | bytes 3076
  18.0 89.2 %copy-start.20 = (f32[128]{0:T(128)}, f32[128]{0:T(128)S(1)}, u32[]{:S(2)}) copy-start(f32[128]{0:T(128)S(1)} %get-tuple-element.334) | copy-start | bytes 1540
  18.0 89.2 %copy-start.22 = (f32[128]{0:T(128)}, f32[128]{0:T(128)S(1)}, u32[]{:S(2)}) copy-start(f32[128]{0:T(128)S(1)} %get-tuple-element.335) | copy-start | bytes 1540
  106.4 9.3 %copy-start.3 = (f32[640,384]{0,1:T(8,128)}, f32[640,384]{0,1:T(8,128)S(1)}, u32[]{:S(2)}) copy-start(f32[640,384]{0,1:T(8,128)S(1)} %fusion.70) | copy-start | bytes 2949124
  107.2 9.9 %copy-start.12 = (f32[640]{0:T(1024)}, f32[640]{0:T(1024)S(1)}, u32[]{:S(2)}) copy-start(f32[640]{0:T(1024)S(1)} %get-tuple-element.333) | copy-start | bytes 7684
  107.2 9.9 %copy-start.14 = (f32[640]{0:T(1024)}, f32[640]{0:T(1024)S(1)}, u32[]{:S(2)}) copy-start(f32[640]{0:T(1024)S(1)} %get-tuple-element.338) | copy-start | bytes 7684
  192.2 0.8 copy-start.5
  196.6 2.1 copy-start.6
  198.7 0.8 copy-start.5
  203.0 2.1 copy-start.6
  205.1 0.8 copy-start.5
  209.4 2.1 copy-start.6
  211.6 0.8 copy-start.5
  215.9 2.1 copy-start.6
  218.0 0.8 copy-start.5
  222.3 2.1 copy-start.6
  224.4 26.4 %copy-start.4 = (f32[640,384]{0,1:T(8,128)S(1)}, f32[640,384]{0,1:T(8,128)}, u32[]{:S(2)}) copy-start(f32[640,384]{0,1:T(8,128)} %copy-done.3) | copy-start | bytes 2949124
  224.4 26.4 %copy-start.21 = (f32[128]{0:T(128)S(1)}, f32[128]{0:T(128)}, u32[]{:S(2)}) copy-start(f32[128]{0:T(128)} %copy-done.20) | copy-start | bytes 1540
  224.4 26.4 %copy-start.23 = (f32[128]{0:T(128)S(1)}, f32[128]{0:T(128)}, u32[]{:S(2)}) copy-start(f32[128]{0:T(128)} %copy-done.22) | copy-start | bytes 1540
  224.5 116.6 %reduce-scatter.5.cloned.1.call-start = ((), (), s32[]{:S(2)}) async-start(), calls=%async_computation.4 | async-start | bytes 5734400 | tf_op jit(solution)/shard_map/reduce_scatter | solution.py:156
  224.9 26.3 %copy-start.13 = (f32[640]{0:T(1024)S(1)}, f32[640]{0:T(1024)}, u32[]{:S(2)}) copy-start(f32[640]{0:T(1024)} %copy-done.12) | copy-start | bytes 7684
  224.9 26.3 %copy-start.15 = (f32[640]{0:T(1024)S(1)}, f32[640]{0:T(1024)}, u32[]{:S(2)}) copy-start(f32[640]{0:T(1024)} %copy-done.14) | copy-start | bytes 7684
  224.9 26.3 %copy-start.16 = (f32[640]{0:T(1024)S(1)}, f32[640]{0:T(1024)}, u32[]{:S(2)}) copy-start(f32[640]{0:T(1024)} %get-tuple-element.332) | copy-start | bytes 7684
  224.9 26.3 %copy-start.17 = (f32[640]{0:T(1024)S(1)}, f32[640]{0:T(1024)}, u32[]{:S(2)}) copy-start(f32[640]{0:T(1024)} %get-tuple-element.339) | copy-start | bytes 7684
  257.8 83.3 %copy-start.2 = (bf16[160,3584]{1,0:T(8,128)(2,1)S(1)}, bf16[160,3584]{1,0:T(8,128)(2,1)}, u32[]{:S(2)}) copy-start(bf16[160,3584]{1,0:T(8,128)(2,1)} %param.12) | copy-start | bytes 3440644
  257.8 83.3 %copy-start.11 = (f32[3584]{0:T(1024)S(1)}, f32[3584]{0:T(1024)}, u32[]{:S(2)}) copy-start(f32[3584]{0:T(1024)} %copy-done.10) | copy-start | bytes 43012
  257.8 83.3 %copy-start.19 = (f32[160]{0:T(256)S(1)}, f32[160]{0:T(256)}, u32[]{:S(2)}) copy-start(f32[160]{0:T(256)} %copy-done.18) | copy-start | bytes 1924
  341.1 2.0 copy-start.8
  341.1 2.0 copy-start.9
Sparse Core Ops, SparseCore 0:
  10.9 89.9 all-gather.2
  102.4 85.7 all-gather.4
  224.6 24.9 reduce-scatter.6
  257.9 83.1 reduce-scatter.4
where the time goes:
time: 353 us; the launch traced here: 352 us
  waiting for transfers between devices  236 us (67%)
  matrix products  52.3 us (15%)
  local copies, waits for them, and re-layouts  19.7 us (6%)
  blocking collectives  16.4 us (5%)
  between operations  13.5 us (4%)
  other arithmetic  12.5 us (4%)
    reduce_scatter x1, waiting for transfers between devices, body(): lax.psum_scatter(lax.dot_general(dqkv, flat_in, (((1,), (1,)), ((), ())),...  83.3 us
    all_gather x1, waiting for transfers between devices, body(): lax.all_gather(layer_normed, 'tensor', axis=0, tiled=True)  82.9 us
    all_gather x1, waiting for transfers between devices, body(): lax.all_gather(scaled_grad, 'tensor', axis=0, tiled=True)  45.5 us
    unnamed x5, waiting for transfers between devices  24.8 us
    dot_general x5, matrix products, output_step(): jnp.einsum('hqk,khd->hqd', weights_b, pair[1], preferred_element_type=jnp...  11.8 us
    all_gather x1, blocking collectives, body(): lax.all_gather(keys_b, 'seq', axis=0, tiled=True)  8.35 us
    dot_general x10, matrix products, block_scores(): jnp.einsum('qhd,khd->hqk', queries, block_keys, preferred_element_type=jn...  8.19 us
    all_gather x1, blocking collectives, body(): lax.all_gather(values_b, 'seq', axis=0, tiled=True)  8.01 us
  transfers between devices with their start and end apart: 4, of which 4 were waited for; matrix products, arithmetic and copies ran while one was open for 9% of the time, Pallas kernels for 0%

commit v1 on v0

--- a/solution.py
+++ b/solution.py
@@ -1,8 +1,11 @@
 import math
+from functools import partial
 
 import jax
 import jax.numpy as jnp
 from jax import lax
+from jax.experimental import pallas as pl
+from jax.experimental.pallas import tpu as pltpu
 from jax.sharding import PartitionSpec as P
 
 
@@ -18,7 +21,7 @@
     )
 
 
-def body(tokens, cotangent, modulation, w_qkv, w_out, qk_gain):
+def token_gather_body(tokens, cotangent, modulation, w_qkv, w_out, qk_gain):
     head_dim = qk_gain.shape[1]
     width = w_out.shape[0]
     nheads = width // head_dim
@@ -170,6 +173,226 @@
     return final_output
 
 
+CORE_SWAP = [(0, 1), (1, 0), (2, 3), (3, 2)]
+CHIP_SWAP = [(0, 2), (2, 0), (1, 3), (3, 1)]
+PLANE = ("group", "seq")
+
+
+def plane_swap(first):
+    pairs = []
+    for group in range(2):
+        for seq in range(4):
+            along_chip = (seq % 2 == 0) == first
+            to = group * 4 + (seq ^ 2) if along_chip else (1 - group) * 4 + seq
+            pairs.append((group * 4 + seq, to))
+    return pairs
+
+
+def around(value, step, count):
+    return lax.ppermute(value, "tensor", [(i, (i + step) % count) for i in range(count)])
+
+
+def attention_kernel(
+    scale, block, q_ref, g_ref, k_ref, v_ref, dq_ref, dk_ref, dv_ref, score_ref, prob_ref, dprob_ref
+):
+    total = k_ref.shape[0]
+    rows, dim = q_ref.shape
+    steps = total // block
+    nt = (((1,), (1,)), ((), ()))
+    tn = (((0,), (0,)), ((), ()))
+
+    def scores(i, top):
+        here = pl.ds(pl.multiple_of(i * block, block), block)
+        s = lax.dot_general(k_ref[here, :], q_ref[...], nt, preferred_element_type=jnp.float32) * scale
+        score_ref[here, :] = s
+        dprob_ref[here, :] = lax.dot_general(
+            v_ref[here, :], g_ref[...], nt, preferred_element_type=jnp.float32
+        )
+        return jnp.maximum(top, jnp.max(s, axis=0, keepdims=True))
+
+    top = lax.fori_loop(0, steps, scores, jnp.full((1, rows), -jnp.inf, jnp.float32))
+
+    def weigh(i, carry):
+        norm, cross = carry
+        here = pl.ds(pl.multiple_of(i * block, block), block)
+        e = jnp.exp(score_ref[here, :] - top)
+        prob_ref[here, :] = e
+        return (
+            norm + jnp.sum(e, axis=0, keepdims=True),
+            cross + jnp.sum(e * dprob_ref[here, :], axis=0, keepdims=True),
+        )
+
+    none = jnp.zeros((1, rows), jnp.float32)
+    norm, cross = lax.fori_loop(0, steps, weigh, (none, none))
+    inverse = 1.0 / norm
+    delta = cross * inverse
+
+    def back(i, dq):
+        here = pl.ds(pl.multiple_of(i * block, block), block)
+        p = prob_ref[here, :] * inverse
+        ds = (p * (dprob_ref[here, :] - delta)).astype(jnp.bfloat16)
+        dk_ref[here, :] = (
+            jnp.dot(ds, q_ref[...], preferred_element_type=jnp.float32) * scale
+        )
+        dv_ref[here, :] = jnp.dot(
+            p.astype(jnp.bfloat16), g_ref[...], preferred_element_type=jnp.float32
+        )
+        return dq + lax.dot_general(k_ref[here, :], ds, tn, preferred_element_type=jnp.float32)
+
+    dq = lax.fori_loop(0, steps, back, jnp.zeros((dim, rows), jnp.float32))
+    dq_ref[...] = dq.T * scale
+
+
+def attention(q, g, k, v):
+    rows, dim = q.shape
+    total = k.shape[0]
+    f32 = jnp.float32
+    vmem = pl.BlockSpec(memory_space=pltpu.VMEM)
+    work = rows * total * dim
+    return pl.pallas_call(
+        partial(attention_kernel, 1.0 / math.sqrt(dim), 256),
+        out_shape=(
+            jax.ShapeDtypeStruct((rows, dim), f32),
+            jax.ShapeDtypeStruct((total, dim), f32),
+            jax.ShapeDtypeStruct((total, dim), f32),
+        ),
+        in_specs=[vmem] * 4,
+        out_specs=(vmem,) * 3,
+        scratch_shapes=[pltpu.VMEM((total, rows), f32)] * 3,
+        compiler_params=pltpu.CompilerParams(vmem_limit_bytes=48 * 1024 * 1024),
+        cost_estimate=pl.CostEstimate(
+            flops=10 * work, bytes_accessed=16 * total * dim, transcendentals=rows * total
+        ),
+        name="attention",
+    )(q, g, k, v)
+
+
+def weight_gather_body(count, tokens, cotangent, modulation, w_qkv, w_out, qk_gain):
+    bf16, f32 = jnp.bfloat16, jnp.float32
+    dim = qk_gain.shape[1]
+    rows, width = tokens.shape
+    half = width // 2
+    part = half // 4
+    seq = lax.axis_index("seq")
+    core, chip, group = seq % 2, seq // 2, lax.axis_index("group")
+    this = core * half
+    other = half - this
+    mine = 2 * group + chip
+    across = 2 * group + (1 - chip)
+    over = 2 * (1 - group) + chip
+    far = 3 - mine
+    first = jnp.where(core == 0, across, over)
+    second = jnp.where(core == 0, over, across)
+
+    def assemble(pieces):
+        whole = jnp.zeros((half, pieces[0].shape[1]), bf16)
+        for place, piece in pieces_at(pieces):
+            whole = lax.dynamic_update_slice(whole, piece, (place * part, 0))
+        return whole
+
+    def pieces_at(pieces):
+        own, one, pair = pieces
+        return ((mine, own), (first, one), (second, pair[:part]), (far, pair[part:]))
+
+    def hand_round(own):
+        one = lax.ppermute(own, PLANE, plane_swap(True))
+        pair = lax.ppermute(jnp.concatenate([own, one], axis=0), PLANE, plane_swap(False))
+        return assemble((own, one, pair))
+
+    own_in = lax.dynamic_slice(w_qkv, (this + mine * part, 0, 0), (part, 3, dim)).reshape(part, 3 * dim)
+    own_out = lax.dynamic_slice(w_out, (0, this + mine * part), (dim, part)).T
+    w_in_half = lax.dynamic_slice(w_qkv, (this, 0, 0), (half, 3, dim)).reshape(half, 3 * dim)
+    w_out_half = lax.dynamic_slice(w_out, (0, this), (dim, half)).T
+    order = [1, count - 1] + list(range(2, count - 1))
+    w_in = {0: w_in_half}
+    w_o = {0: w_out_half}
+    for step in order:
+        w_in[step] = hand_round(around(own_in, step, count))
+    for step in order:
+        w_o[step] = hand_round(around(own_out, step, count))
+
+    shift, scale, gate = modulation[0], 1.0 + modulation[1], modulation[2]
+    x = tokens.astype(f32)
+    inv = lax.rsqrt(jnp.mean(x * x, axis=-1, keepdims=True) + 1e-06)
+    xhat = x * inv
+    normed = (xhat * scale + shift).astype(bf16)
+    cot = cotangent.astype(f32)
+    scaled = (cot * gate).astype(bf16)
+
+    def both_cores(value):
+        keep = lax.dynamic_slice(value, (0, this), (rows, half))
+        send = lax.dynamic_slice(value, (0, other), (rows, half))
+        return jnp.concatenate([keep, lax.ppermute(send, "seq", CORE_SWAP)], axis=0)
+
+    normed_half = both_cores(normed)
+    scaled_half = both_cores(scaled)
+
+    def project(values, weights):
+        out = jnp.dot(values, weights, preferred_element_type=f32)
+        return out[:rows] + lax.ppermute(out[rows:], "seq", CORE_SWAP)
+
+    gain_q, gain_k = qk_gain[0], qk_gain[1]
+
+    def unit(raw):
+        back = lax.rsqrt(jnp.mean(raw * raw, axis=-1, keepdims=True) + 1e-06)
+        return raw * back, back
+
+    units = {}
+    arrived = {}
+    slots = [0] + order
+    for step in slots:
+        qkv = project(normed_half, w_in[step])
+        qh, qs = unit(qkv[:, :dim])
+        kh, ks = unit(qkv[:, dim : 2 * dim])
+        units[step] = (qh, qs, kh, ks)
+        ready = jnp.concatenate([qh * gain_q, kh * gain_k, qkv[:, 2 * dim :]], axis=1).astype(bf16)
+        arrived[step] = around(ready, -step, count) if step else ready
+    heads = jnp.concatenate([arrived[i] for i in range(count)], axis=0)
+    grads = {}
+    for step in slots:
+        ready = project(scaled_half, w_o[step]).astype(bf16)
+        grads[step] = around(ready, -step, count) if step else ready
+    g = jnp.concatenate([grads[i] for i in range(count)], axis=0)
+
+    kv = heads[:, dim:]
+    kv_chip = lax.ppermute(kv, "seq", CHIP_SWAP)
+    kv_all = jnp.concatenate(
+        [kv, lax.ppermute(kv, "seq", CORE_SWAP), kv_chip, lax.ppermute(kv_chip, "seq", CORE_SWAP)], axis=0
+    )
+    dq, dk, dv = attention(heads[:, :dim], g, kv_all[:, :dim], kv_all[:, dim:])
+    dkv = jnp.concatenate([dk, dv], axis=1).reshape(4, count * rows, 2 * dim)
+    summed = dkv[0::2] + lax.ppermute(dkv[1::2], "seq", CORE_SWAP)
+    dkv = summed[0] + lax.ppermute(summed[1].astype(bf16), "seq", CHIP_SWAP).astype(f32)
+    back = jnp.concatenate([dq, dkv], axis=1).astype(bf16).reshape(count, rows, 3 * dim)
+
+    def unit_back(hat, scale_back, gain, upstream):
+        up = upstream * gain
+        return scale_back * (up - hat * jnp.mean(up * hat, axis=-1, keepdims=True))
+
+    grads_in = []
+    weights = []
+    for step in slots:
+        d = around(back[step], step, count) if step else back[0]
+        qh, qs, kh, ks = units[step]
+        dqn, dkn = d[:, :dim].astype(f32), d[:, dim : 2 * dim].astype(f32)
+        grads_in += [
+            unit_back(qh, qs, gain_q, dqn).astype(bf16),
+            unit_back(kh, ks, gain_k, dkn).astype(bf16),
+            d[:, 2 * dim :],
+        ]
+        weights.append(w_in[step])
+    dqkv = jnp.concatenate(grads_in, axis=1)
+    dqkv = jnp.concatenate([dqkv, lax.ppermute(dqkv, "seq", CORE_SWAP)], axis=0)
+    dn = lax.dot_general(
+        dqkv, jnp.concatenate(weights, axis=1), (((1,), (1,)), ((), ())), preferred_element_type=f32
+    )
+    away = lax.ppermute(dn[rows:].astype(bf16), "seq", CORE_SWAP).astype(f32)
+    low = jnp.where(core == 0, dn[:rows], away)
+    high = jnp.where(core == 0, away, dn[:rows])
+    dhat = jnp.concatenate([low, high], axis=1) * scale
+    return cot + inv * (dhat - xhat * jnp.mean(dhat * xhat, axis=-1, keepdims=True))
+
+
 def solution(mesh):
     placed = (
         P(("group", "seq", "tensor"), None),
@@ -179,6 +402,15 @@
         P("tensor", None),
         P(),
     )
+    sizes = dict(mesh.shape)
+
+    def body(*args):
+        weight_elements = args[3].size + args[4].size
+        token_elements = 2 * 3 * args[0].size
+        if sizes["group"] == 2 and sizes["seq"] == 4 and weight_elements < token_elements:
+            return weight_gather_body(sizes["tensor"], *args)
+        return token_gather_body(*args)
+
     return jax.shard_map(
         body,
         mesh=mesh,

time: 353 us -> 264 us (0.75)
  waiting for transfers between devices: 236 us -> 47.5 us
  local copies, waits for them, and re-layouts: 19.7 us -> 111 us
  starting transfers between devices: 0.31 us -> 45.6 us
  matrix products: 52.3 us -> 17.9 us
  other arithmetic: 12.5 us -> 29.8 us
  blocking collectives: 16.4 us -> 0 us
  between operations: 13.5 us -> 0.94 us
  Pallas kernels: 0 us -> 9.1 us
    all_gather x2 -> x0, waiting for transfers between devices: 128 us -> none  [the longest x1 82.9 us: body(): lax.all_gather(layer_normed, 'tensor', axis=0, tiled=True)]
    reduce_scatter x1 -> x0, waiting for transfers between devices: 83.3 us -> none  [body(): lax.psum_scatter(lax.dot_general(dqkv, flat_in, (((1,), (1,)), ((), ())),...]
    dynamic_update_slice x10 -> x24, local copies, waits for them, and re-layouts: 4.29 us -> 78 us  [assemble(): whole = lax.dynamic_update_slice(whole, piece, (place * part, 0))]
    ppermute x0 -> x44, waiting for transfers between devices: none -> 47.5 us  [the longest x15 16 us: around(): lax.ppermute(value, 'tensor', [(i, (i + step) % count) for i in range(cou...]
    ppermute x0 -> x44, starting transfers between devices: none -> 45.6 us  [the longest x15 29.4 us: around(): lax.ppermute(value, 'tensor', [(i, (i + step) % count) for i in range(cou...]
    dot_general x38 -> x9, matrix products: 52.3 us -> 17.9 us  [the longest x8 16 us: project(): out = jnp.dot(values, weights, preferred_element_type=f32)]
    unnamed x5 -> x0, waiting for transfers between devices: 24.8 us -> none
    all_gather x2 -> x0, blocking collectives: 16.4 us -> none  [the longest x1 8.35 us: body(): lax.all_gather(keys_b, 'seq', axis=0, tiled=True)]
  transfers between devices with their start and end apart: 4 -> 44, of which waited for: 4 -> 12; matrix products, arithmetic and copies ran while one was open for 9% -> 57% of each run, Pallas kernels for 0% -> 0%
where the time goes in v1:
time: 264 us; the launch traced here: 262 us
  local copies, waits for them, and re-layouts  111 us (42%)
  waiting for transfers between devices  47.5 us (18%)
  starting transfers between devices  45.6 us (17%)
  other arithmetic  29.8 us (11%)
  matrix products  17.9 us (7%)
  Pallas kernels  9.1 us (3%)
    dynamic_update_slice x24, local copies, waits for them, and re-layouts, assemble(): whole = lax.dynamic_update_slice(whole, piece, (place * part, 0))  78 us
    ppermute x15, starting transfers between devices, around(): lax.ppermute(value, 'tensor', [(i, (i + step) % count) for i in range(cou...  29.4 us
    dot_general x8, matrix products, project(): out = jnp.dot(values, weights, preferred_element_type=f32)  16 us
    ppermute x15, waiting for transfers between devices, around(): lax.ppermute(value, 'tensor', [(i, (i + step) % count) for i in range(cou...  16 us
    concatenate x6, other arithmetic, hand_round(): jnp.concatenate([own, one], axis=0)  11 us
    slice x6, local copies, waits for them, and re-layouts, pieces_at(): pair[part:]  10.2 us
    ppermute x1, waiting for transfers between devices, weight_gather_body(): lax.ppermute(summed[1].astype(bf16), 'seq', CHIP_SWAP).astype(f32)  9.45 us
    pallas_call x1, Pallas kernels, attention(): pl.pallas_call(partial(attention_kernel, 1.0 / math.sqrt(dim), 256), out_...  9.1 us
  transfers between devices with their start and end apart: 44, of which 12 were waited for; matrix products, arithmetic and copies ran while one was open for 57% of the time, Pallas kernels for 0%

profile of v1, /device:TPU:0, one launch (start us, length us, event | category | flops | bytes accessed | tf_op | source)
XLA Modules:
  0.0 261.6 jit_solution(16988030896621971634)
XLA Ops:
  0.0 1.8 dynamic-slice_bitcast_fusion
  1.8 5.0 %collective-permute-start.29 = (bf16[448,128]{0,1:T(8,128)(2,1)}, bf16[448,128]{0,1:T(8,128)(2,1)}, u32[]{:S(2)}, u32[]{:S(2)}) collective-permute-start(bf16[448,128]{0,1:T(8,128)(2,1)} %dynamic-slice_bitcast_fusion), channel_id=1, source_target_pairs={{0,12},{4,0},{8,4},{12,8},{1,13},{5,1},{9,5},{13,9},{2,14},{6,2},{... | collective-permute-start | bytes 344072 | tf_op jit(solution)/shard_map/ppermute | solution.py:192
  8.8 2.8 %collective-permute-start.12 = (bf16[448,384]{0,1:T(8,128)(2,1)}, bf16[448,384]{0,1:T(8,128)(2,1)S(1)}, u32[]{:S(2)}, u32[]{:S(2)}) collective-permute-start(bf16[448,384]{0,1:T(8,128)(2,1)} %bitcast.3), channel_id=1, source_target_pairs={{0,12},{4,0},{8,4},{12,8},{1,13},{5,1},{9,5},{13,9},{2,14},{6,2},{... | collective-permute-start | bytes 1032200 | tf_op jit(solution)/shard_map/ppermute | solution.py:192
  17.8 2.2 fusion.11
  22.2 2.6 copy.9
  29.0 1.8 dynamic_update_slice.88
  31.6 1.8 dynamic_update_slice.92
  33.5 3.4 %collective-permute-start.2 = (bf16[448,384]{0,1:T(8,128)(2,1)}, bf16[448,384]{0,1:T(8,128)(2,1)}, u32[]{:S(2)}, u32[]{:S(2)}) collective-permute-start(bf16[448,384]{0,1:T(8,128)(2,1)} %bitcast.3), channel_id=1, source_target_pairs={{0,4},{4,8},{8,12},{12,0},{1,5},{5,9},{9,13},{13,1},{2,6},{6,10},{... | collective-permute-start | bytes 1032200 | tf_op jit(solution)/shard_map/ppermute | solution.py:192
  37.6 1.8 dynamic_update_slice.84
  39.4 2.1 dynamic_update_slice.89
  43.1 2.1 dynamic_update_slice.93
  45.3 1.8 pad_maximum_fusion.13
  48.1 2.1 dynamic_update_slice.85
  50.3 1.8 pad_maximum_fusion.12
  52.1 1.8 pad_maximum_fusion.14
  55.0 4.4 %dynamic_update_slice.80 = bf16[1792,384]{0,1:T(8,128)(2,1)} dynamic-update-slice(bf16[1792,384]{0,1:T(8,128)(2,1)} %broadcast.174.clone.1, bf16[448,384]{0,1:T(8,128)(2,1)S(1)} %collective-permute-done.12, s32[]{:T(128)S(6)} %select_n.81, s32[]{:T(128)} %constant.63.clone.1) | dynamic-update-slice | bytes 688132 | tf_op jit(solution)/shard_map/dynamic_update_slice | solution.py:290
  61.4 4.4 %dynamic_update_slice.76 = bf16[1792,384]{0,1:T(8,128)(2,1)} dynamic-update-slice(bf16[1792,384]{0,1:T(8,128)(2,1)} %broadcast.174.clone, bf16[448,384]{0,1:T(8,128)(2,1)S(1)} %collective-permute-done.7, s32[]{:T(128)S(6)} %select_n.81, s32[]{:T(128)} %constant.63.clone.1) | dynamic-update-slice | bytes 688132 | tf_op jit(solution)/shard_map/dynamic_update_slice | solution.py:290
  68.2 4.6 %dynamic_update_slice.72 = bf16[1792,384]{0,1:T(8,128)(2,1)} dynamic-update-slice(bf16[1792,384]{0,1:T(8,128)(2,1)} %broadcast.174.clone.2, bf16[448,384]{0,1:T(8,128)(2,1)} %collective-permute-done.2, s32[]{:T(128)S(6)} %select_n.81, s32[]{:T(128)} %constant.63.clone.1) | dynamic-update-slice | bytes 688132 | tf_op jit(solution)/shard_map/dynamic_update_slice | solution.py:290
  72.8 2.0 collective-permute-start.13
  74.8 1.7 fusion.52
  76.5 1.8 dynamic_update_slice.90
  78.5 1.7 fusion.53
  80.2 1.8 dynamic_update_slice.94
  82.0 1.9 dynamic_update_slice.91
  83.9 1.9 dynamic_update_slice.95
  85.7 1.8 collective-permute-start.3
  87.5 1.7 fusion.51
  89.2 1.8 dynamic_update_slice.86
  91.0 1.9 dynamic_update_slice.87
  92.9 1.9 fusion.42
  98.1 1.7 fusion.23
  102.9 1.8 fusion.46
  105.6 5.0 %dynamic_update_slice.81 = bf16[1792,384]{0,1:T(8,128)(2,1)} dynamic-update-slice(bf16[1792,384]{0,1:T(8,128)(2,1)} %dynamic_update_slice.80, bf16[448,384]{0,1:T(8,128)(2,1)} %collective-permute-done.13, s32[]{:T(128)S(6)} %select_n.83, s32[]{:T(128)} %constant.63.clone.1) | dynamic-update-slice | bytes 688132 | tf_op jit(solution)/shard_map/dynamic_update_slice | solution.py:290
  110.7 5.0 %dynamic_update_slice.77 = bf16[1792,384]{0,1:T(8,128)(2,1)} dynamic-update-slice(bf16[1792,384]{0,1:T(8,128)(2,1)} %dynamic_update_slice.76, bf16[448,384]{0,1:T(8,128)(2,1)} %collective-permute-done.8, s32[]{:T(128)S(6)} %select_n.83, s32[]{:T(128)} %constant.63.clone.1) | dynamic-update-slice | bytes 688132 | tf_op jit(solution)/shard_map/dynamic_update_slice | solution.py:290
  115.8 2.2 pad_maximum_fusion.5
  118.3 5.0 %dynamic_update_slice.73 = bf16[1792,384]{0,1:T(8,128)(2,1)} dynamic-update-slice(bf16[1792,384]{0,1:T(8,128)(2,1)} %dynamic_update_slice.72, bf16[448,384]{0,1:T(8,128)(2,1)} %collective-permute-done.3, s32[]{:T(128)S(6)} %select_n.83, s32[]{:T(128)} %constant.63.clone.1) | dynamic-update-slice | bytes 688132 | tf_op jit(solution)/shard_map/dynamic_update_slice | solution.py:290
  124.7 2.1 pad_maximum_fusion.6
  130.2 7.6 %collective-permute-done.4 = bf16[896,384]{0,1:T(8,128)(2,1)S(1)} collective-permute-done((bf16[896,384]{0,1:T(8,128)(2,1)S(1)}, bf16[896,384]{0,1:T(8,128)(2,1)S(1)}, u32[]{:S(2)}, u32[]{:S(2)}) %collective-permute-start.4) | collective-permute-done | bytes 688160 | tf_op jit(solution)/shard_map/ppermute | solution.py:299
  139.8 4.6 %dynamic_update_slice.74 = bf16[1792,384]{0,1:T(8,128)(2,1)} dynamic-update-slice(bf16[1792,384]{0,1:T(8,128)(2,1)} %dynamic_update_slice.73, bf16[448,384]{0,1:T(8,128)(2,1)} %get-tuple-element.43, s32[]{:T(128)S(6)} %select_n.85, s32[]{:T(128)} %constant.63.clone.1) | dynamic-update-slice | bytes 688132 | tf_op jit(solution)/shard_map/dynamic_update_slice | solution.py:290
  144.4 4.3 %dynamic_update_slice.75 = bf16[1792,384]{0,1:T(8,128)(2,1)} dynamic-update-slice(bf16[1792,384]{0,1:T(8,128)(2,1)} %dynamic_update_slice.74, bf16[448,384]{0,1:T(8,128)(2,1)S(1)} %get-tuple-element.42, s32[]{:T(128)S(6)} %select_n.86, s32[]{:T(128)} %constant.63.clone.1) | dynamic-update-slice | bytes 688132 | tf_op jit(solution)/shard_map/dynamic_update_slice | solution.py:290
  148.6 2.5 fusion.45
  152.0 2.1 fusion.50
  154.1 4.6 %dynamic_update_slice.78 = bf16[1792,384]{0,1:T(8,128)(2,1)} dynamic-update-slice(bf16[1792,384]{0,1:T(8,128)(2,1)} %dynamic_update_slice.77, bf16[448,384]{0,1:T(8,128)(2,1)} %get-tuple-element.47, s32[]{:T(128)S(6)} %select_n.85, s32[]{:T(128)} %constant.63.clone.1) | dynamic-update-slice | bytes 688132 | tf_op jit(solution)/shard_map/dynamic_update_slice | solution.py:290
  158.6 4.3 %dynamic_update_slice.79 = bf16[1792,384]{0,1:T(8,128)(2,1)} dynamic-update-slice(bf16[1792,384]{0,1:T(8,128)(2,1)} %dynamic_update_slice.78, bf16[448,384]{0,1:T(8,128)(2,1)S(1)} %get-tuple-element.46, s32[]{:T(128)S(6)} %select_n.86, s32[]{:T(128)} %constant.63.clone.1) | dynamic-update-slice | bytes 688132 | tf_op jit(solution)/shard_map/dynamic_update_slice | solution.py:290
  162.9 2.5 fusion.44
  167.3 2.0 fusion.49
  169.3 4.6 %dynamic_update_slice.82 = bf16[1792,384]{0,1:T(8,128)(2,1)} dynamic-update-slice(bf16[1792,384]{0,1:T(8,128)(2,1)} %dynamic_update_slice.81, bf16[448,384]{0,1:T(8,128)(2,1)} %get-tuple-element.45, s32[]{:T(128)S(6)} %select_n.85, s32[]{:T(128)} %constant.63.clone.1) | dynamic-update-slice | bytes 688132 | tf_op jit(solution)/shard_map/dynamic_update_slice | solution.py:290
  173.9 4.3 %dynamic_update_slice.83 = bf16[1792,384]{0,1:T(8,128)(2,1)} dynamic-update-slice(bf16[1792,384]{0,1:T(8,128)(2,1)} %dynamic_update_slice.82, bf16[448,384]{0,1:T(8,128)(2,1)S(1)} %get-tuple-element.44, s32[]{:T(128)S(6)} %select_n.86, s32[]{:T(128)} %constant.63.clone.1) | dynamic-update-slice | bytes 688132 | tf_op jit(solution)/shard_map/dynamic_update_slice | solution.py:290
  178.3 2.5 fusion.43
  184.3 8.0 %collective-permute-start.11 = (bf16[160,384]{1,0:T(8,128)(2,1)S(1)}, bf16[160,384]{1,0:T(8,128)(2,1)S(1)}, u32[]{:S(2)}, u32[]{:S(2)}) collective-permute-start(bf16[160,384]{1,0:T(8,128)(2,1)S(1)} %pad_maximum_fusion.21), channel_id=1, source_target_pairs={{0,8},{4,12},{8,0},{12,4},{1,9},{5,13},{9,1},{13,5},{2,10},{6,14},... | collective-permute-start | bytes 368648 | tf_op jit(solution)/shard_map/ppermute | solution.py:192
  192.4 2.1 collective-permute-start.16
  195.4 3.2 %collective-permute-done.11 = bf16[160,384]{1,0:T(8,128)(2,1)S(1)} collective-permute-done((bf16[160,384]{1,0:T(8,128)(2,1)S(1)}, bf16[160,384]{1,0:T(8,128)(2,1)S(1)}, u32[]{:S(2)}, u32[]{:S(2)}) %collective-permute-start.11) | collective-permute-done | bytes 122912 | tf_op jit(solution)/shard_map/ppermute | solution.py:192
  198.6 3.9 %collective-permute-done.6 = bf16[160,384]{1,0:T(8,128)(2,1)S(1)} collective-permute-done((bf16[160,384]{1,0:T(8,128)(2,1)S(1)}, bf16[160,384]{1,0:T(8,128)(2,1)S(1)}, u32[]{:S(2)}, u32[]{:S(2)}) %collective-permute-start.6) | collective-permute-done | bytes 122912 | tf_op jit(solution)/shard_map/ppermute | solution.py:192
  207.8 6.3 %collective-permute-done.35 = bf16[640,256]{1,0:T(8,128)(2,1)S(1)} collective-permute-done((bf16[640,256]{1,0:T(8,128)(2,1)S(1)}, bf16[640,256]{1,0:T(8,128)(2,1)S(1)}, u32[]{:S(2)}, u32[]{:S(2)}) %collective-permute-start.35) | collective-permute-done | bytes 327712 | tf_op jit(solution)/shard_map/ppermute | solution.py:358
  215.8 9.1 %attention.1 = (f32[640,128]{1,0:T(8,128)S(1)}, f32[2560,128]{1,0:T(8,128)S(1)}, f32[2560,128]{1,0:T(8,128)S(1)}) custom-call(bf16[640,128]{1,0:T(8,128)(2,1)S(1)} %pad_maximum_fusion.15.q_ref, bf16[640,128]{1,0:T(8,128)(2,1)S(1)} %pad_maximum_fusion.16.g_ref, bf16[2560,128]{1,0:T(8,128)(2,1)S(1)} %get-tuple-element.37.k_ref, ...), custom_call_target="tpu_custom_call" | custom-call | flops 2097152000 | bytes 5242880 | tf_op jit(solution)/shard_map/attention/pallas_call | solution.py:252
  225.4 2.9 %collective-permute-done.37 = f32[2,640,256]{2,1,0:T(8,128)S(1)} collective-permute-done((f32[2,640,256]{2,1,0:T(8,128)S(1)}, f32[2,640,256]{2,1,0:T(8,128)S(1)}, u32[]{:S(2)}, u32[]{:S(2)}) %collective-permute-start.37) | collective-permute-done | bytes 1310752 | tf_op jit(solution)/shard_map/ppermute | solution.py:364
  228.9 9.4 %collective-permute-done.38 = bf16[640,256]{1,0:T(8,128)(2,1)S(1)} collective-permute-done((bf16[640,256]{1,0:T(8,128)(2,1)S(1)}, bf16[640,256]{1,0:T(8,128)(2,1)S(1)}, u32[]{:S(2)}, u32[]{:S(2)}) %collective-permute-start.38) | collective-permute-done | bytes 327712 | tf_op jit(solution)/shard_map/ppermute | solution.py:365
  238.9 1.7 collective-permute-start.39
  241.3 5.3 %collective-permute-done.40 = bf16[160,384]{1,0:T(8,128)(2,1)S(1)} collective-permute-done((bf16[160,384]{1,0:T(8,128)(2,1)S(1)}, bf16[160,384]{1,0:T(8,128)(2,1)S(1)}, u32[]{:S(2)}, u32[]{:S(2)}) %collective-permute-start.40) | collective-permute-done | bytes 122912 | tf_op jit(solution)/shard_map/ppermute | solution.py:192
  247.9 2.6 collective-permute-done.41
  252.1 1.9 collective-permute-done.42
  254.0 1.9 fusion
  256.2 1.9 collective-permute-done.43
  259.5 2.1 convert_add_fusion
  (229 shorter events, 59.5 us)
Async XLA Ops:
  0.0 7.9 %copy-start = (bf16[3584,3,128]{2,0,1:T(8,128)(2,1)S(1)}, bf16[3584,3,128]{2,0,1:T(8,128)(2,1)}, u32[]{:S(2)}) copy-start(bf16[3584,3,128]{2,0,1:T(8,128)(2,1)} %param.9) | copy-start | bytes 8257540
  1.8 22.9 %collective-permute-start.29 = (bf16[448,128]{0,1:T(8,128)(2,1)}, bf16[448,128]{0,1:T(8,128)(2,1)}, u32[]{:S(2)}, u32[]{:S(2)}) collective-permute-start(bf16[448,128]{0,1:T(8,128)(2,1)} %dynamic-slice_bitcast_fusion), channel_id=1, source_target_pairs={{0,12},{4,0},{8,4},{12,8},{1,13},{5,1},{9,5},{13,9},{2,14},{6,2},{... | collective-permute-start | bytes 344072 | tf_op jit(solution)/shard_map/ppermute | solution.py:192
  6.9 19.4 %collective-permute-start.24 = (bf16[448,128]{0,1:T(8,128)(2,1)}, bf16[448,128]{0,1:T(8,128)(2,1)}, u32[]{:S(2)}, u32[]{:S(2)}) collective-permute-start(bf16[448,128]{0,1:T(8,128)(2,1)} %dynamic-slice_bitcast_fusion), channel_id=1, source_target_pairs={{0,8},{4,12},{8,0},{12,4},{1,9},{5,13},{9,1},{13,5},{2,10},{6,14},... | collective-permute-start | bytes 344072 | tf_op jit(solution)/shard_map/ppermute | solution.py:192
  6.9 26.6 %collective-permute-start.19 = (bf16[448,128]{0,1:T(8,128)(2,1)}, bf16[448,128]{0,1:T(8,128)(2,1)}, u32[]{:S(2)}, u32[]{:S(2)}) collective-permute-start(bf16[448,128]{0,1:T(8,128)(2,1)} %dynamic-slice_bitcast_fusion), channel_id=1, source_target_pairs={{0,4},{4,8},{8,12},{12,0},{1,5},{5,9},{9,13},{13,1},{2,6},{6,10},{... | collective-permute-start | bytes 344072 | tf_op jit(solution)/shard_map/ppermute | solution.py:192
  8.8 45.0 %collective-permute-start.12 = (bf16[448,384]{0,1:T(8,128)(2,1)}, bf16[448,384]{0,1:T(8,128)(2,1)S(1)}, u32[]{:S(2)}, u32[]{:S(2)}) collective-permute-start(bf16[448,384]{0,1:T(8,128)(2,1)} %bitcast.3), channel_id=1, source_target_pairs={{0,12},{4,0},{8,4},{12,8},{1,13},{5,1},{9,5},{13,9},{2,14},{6,2},{... | collective-permute-start | bytes 1032200 | tf_op jit(solution)/shard_map/ppermute | solution.py:192
  11.7 47.8 %collective-permute-start.7 = (bf16[448,384]{0,1:T(8,128)(2,1)}, bf16[448,384]{0,1:T(8,128)(2,1)S(1)}, u32[]{:S(2)}, u32[]{:S(2)}) collective-permute-start(bf16[448,384]{0,1:T(8,128)(2,1)} %bitcast.3), channel_id=1, source_target_pairs={{0,8},{4,12},{8,0},{12,4},{1,9},{5,13},{9,1},{13,5},{2,10},{6,14},... | collective-permute-start | bytes 1032200 | tf_op jit(solution)/shard_map/ppermute | solution.py:192
  24.7 16.8 %collective-permute-start.30 = (bf16[448,128]{0,1:T(8,128)(2,1)}, bf16[448,128]{0,1:T(8,128)(2,1)}, u32[]{:S(2)}, u32[]{:S(2)}) collective-permute-start(bf16[448,128]{0,1:T(8,128)(2,1)} %collective-permute-done.29), channel_id=1, source_target_pairs={{0,2},{1,17},{2,0},{3,19},{16,18},{17,1},{18,16},{19,3},{4,6},{5,2... | collective-permute-start | bytes 344072 | tf_op jit(solution)/shard_map/ppermute | solution.py:298
  26.2 13.2 %collective-permute-start.25 = (bf16[448,128]{0,1:T(8,128)(2,1)}, bf16[448,128]{0,1:T(8,128)(2,1)}, u32[]{:S(2)}, u32[]{:S(2)}) collective-permute-start(bf16[448,128]{0,1:T(8,128)(2,1)} %collective-permute-done.24), channel_id=1, source_target_pairs={{0,2},{1,17},{2,0},{3,19},{16,18},{17,1},{18,16},{19,3},{4,6},{5,2... | collective-permute-start | bytes 344072 | tf_op jit(solution)/shard_map/ppermute | solution.py:298
  33.5 32.4 %collective-permute-start.2 = (bf16[448,384]{0,1:T(8,128)(2,1)}, bf16[448,384]{0,1:T(8,128)(2,1)}, u32[]{:S(2)}, u32[]{:S(2)}) collective-permute-start(bf16[448,384]{0,1:T(8,128)(2,1)} %bitcast.3), channel_id=1, source_target_pairs={{0,4},{4,8},{8,12},{12,0},{1,5},{5,9},{9,13},{13,1},{2,6},{6,10},{... | collective-permute-start | bytes 1032200 | tf_op jit(solution)/shard_map/ppermute | solution.py:192
  39.4 53.5 %collective-permute-start.17 = (bf16[160,1792]{1,0:T(8,128)(2,1)}, bf16[160,1792]{1,0:T(8,128)(2,1)}, u32[]{:S(2)}, u32[]{:S(2)}) collective-permute-start(bf16[160,1792]{1,0:T(8,128)(2,1)} %get-tuple-element.39), channel_id=1, source_target_pairs={{0,1},{1,0},{2,3},{3,2},{4,5},{5,4},{6,7},{7,6},{8,9},{9,8},{10,11... | collective-permute-start | bytes 1720328 | tf_op jit(solution)/shard_map/ppermute | solution.py:325
  41.6 5.5 %collective-permute-start.20 = (bf16[448,128]{0,1:T(8,128)(2,1)}, bf16[448,128]{0,1:T(8,128)(2,1)}, u32[]{:S(2)}, u32[]{:S(2)}) collective-permute-start(bf16[448,128]{0,1:T(8,128)(2,1)} %collective-permute-done.19), channel_id=1, source_target_pairs={{0,2},{1,17},{2,0},{3,19},{16,18},{17,1},{18,16},{19,3},{4,6},{5,2... | collective-permute-start | bytes 344072 | tf_op jit(solution)/shard_map/ppermute | solution.py:298
  47.0 25.8 %collective-permute-start.26 = (bf16[896,128]{0,1:T(8,128)(2,1)}, bf16[896,128]{0,1:T(8,128)(2,1)}, u32[]{:S(2)}, u32[]{:S(2)}) collective-permute-start(bf16[896,128]{0,1:T(8,128)(2,1)} %pad_maximum_fusion.13), channel_id=1, source_target_pairs={{0,16},{1,3},{2,18},{3,1},{16,0},{17,19},{18,2},{19,17},{4,20},{5,... | collective-permute-start | bytes 688136 | tf_op jit(solution)/shard_map/ppermute | solution.py:299
  53.8 48.6 %collective-permute-start = (bf16[160,1792]{1,0:T(8,128)(2,1)}, bf16[160,1792]{1,0:T(8,128)(2,1)}, u32[]{:S(2)}, u32[]{:S(2)}) collective-permute-start(bf16[160,1792]{1,0:T(8,128)(2,1)} %get-tuple-element.41), channel_id=1, source_target_pairs={{0,1},{1,0},{2,3},{3,2},{4,5},{5,4},{6,7},{7,6},{8,9},{9,8},{10,11... | collective-permute-start | bytes 1720328 | tf_op jit(solution)/shard_map/ppermute | solution.py:325
  59.4 18.9 %collective-permute-start.31 = (bf16[896,128]{0,1:T(8,128)(2,1)}, bf16[896,128]{0,1:T(8,128)(2,1)}, u32[]{:S(2)}, u32[]{:S(2)}) collective-permute-start(bf16[896,128]{0,1:T(8,128)(2,1)} %pad_maximum_fusion.14), channel_id=1, source_target_pairs={{0,16},{1,3},{2,18},{3,1},{16,0},{17,19},{18,2},{19,17},{4,20},{5,... | collective-permute-start | bytes 688136 | tf_op jit(solution)/shard_map/ppermute | solution.py:299
  65.8 19.9 %collective-permute-start.21 = (bf16[896,128]{0,1:T(8,128)(2,1)}, bf16[896,128]{0,1:T(8,128)(2,1)}, u32[]{:S(2)}, u32[]{:S(2)}) collective-permute-start(bf16[896,128]{0,1:T(8,128)(2,1)} %pad_maximum_fusion.12), channel_id=1, source_target_pairs={{0,16},{1,3},{2,18},{3,1},{16,0},{17,19},{18,2},{19,17},{4,20},{5,... | collective-permute-start | bytes 688136 | tf_op jit(solution)/shard_map/ppermute | solution.py:299
  72.8 32.7 %collective-permute-start.13 = (bf16[448,384]{0,1:T(8,128)(2,1)S(1)}, bf16[448,384]{0,1:T(8,128)(2,1)}, u32[]{:S(2)}, u32[]{:S(2)}) collective-permute-start(bf16[448,384]{0,1:T(8,128)(2,1)S(1)} %collective-permute-done.12), channel_id=1, source_target_pairs={{0,2},{1,17},{2,0},{3,19},{16,18},{17,1},{18,16},{19,3},{4,6},{5,2... | collective-permute-start | bytes 1032200 | tf_op jit(solution)/shard_map/ppermute | solution.py:298
  78.3 32.4 %collective-permute-start.8 = (bf16[448,384]{0,1:T(8,128)(2,1)S(1)}, bf16[448,384]{0,1:T(8,128)(2,1)}, u32[]{:S(2)}, u32[]{:S(2)}) collective-permute-start(bf16[448,384]{0,1:T(8,128)(2,1)S(1)} %collective-permute-done.7), channel_id=1, source_target_pairs={{0,2},{1,17},{2,0},{3,19},{16,18},{17,1},{18,16},{19,3},{4,6},{5,2... | collective-permute-start | bytes 1032200 | tf_op jit(solution)/shard_map/ppermute | solution.py:298
  85.7 32.2 %collective-permute-start.3 = (bf16[448,384]{0,1:T(8,128)(2,1)}, bf16[448,384]{0,1:T(8,128)(2,1)}, u32[]{:S(2)}, u32[]{:S(2)}) collective-permute-start(bf16[448,384]{0,1:T(8,128)(2,1)} %collective-permute-done.2), channel_id=1, source_target_pairs={{0,2},{1,17},{2,0},{3,19},{16,18},{17,1},{18,16},{19,3},{4,6},{5,2... | collective-permute-start | bytes 1032200 | tf_op jit(solution)/shard_map/ppermute | solution.py:298
  94.8 6.9 %copy-start.24 = (f32[320,128]{1,0:T(8,128)}, f32[320,128]{1,0:T(8,128)S(1)}, u32[]{:S(2)}) copy-start(f32[320,128]{1,0:T(8,128)S(1)} %fusion.42) | copy-start | bytes 491524
  96.5 4.7 %copy-start.22 = (f32[320,128]{1,0:T(8,128)}, f32[320,128]{1,0:T(8,128)S(1)}, u32[]{:S(2)}) copy-start(f32[320,128]{1,0:T(8,128)S(1)} %fusion.41) | copy-start | bytes 491524
  98.1 4.8 %copy-start.3 = (bf16[1792,3,128]{0,2,1:T(8,128)(2,1)S(1)}, bf16[1792,3,128]{0,2,1:T(8,128)(2,1)}, u32[]{:S(2)}) copy-start(bf16[1792,3,128]{0,2,1:T(8,128)(2,1)} %copy.9) | copy-start | bytes 4128772
  98.1 4.8 %copy-start.8 = (bf16[160,1792]{1,0:T(8,128)(2,1)S(1)}, bf16[160,1792]{1,0:T(8,128)(2,1)}, u32[]{:S(2)}) copy-start(bf16[160,1792]{1,0:T(8,128)(2,1)} %get-tuple-element.40) | copy-start | bytes 1720324
  99.8 3.1 %copy-start.18 = (f32[320,128]{1,0:T(8,128)}, f32[320,128]{1,0:T(8,128)S(1)}, u32[]{:S(2)}) copy-start(f32[320,128]{1,0:T(8,128)S(1)} %fusion.23) | copy-start | bytes 491524
  102.4 90.0 %collective-permute-start.22 = (f32[160,128]{1,0:T(8,128)}, f32[160,128]{1,0:T(8,128)}, u32[]{:S(2)}, u32[]{:S(2)}) collective-permute-start(f32[160,128]{1,0:T(8,128)} %slice.329), channel_id=1, source_target_pairs={{0,1},{1,0},{2,3},{3,2},{4,5},{5,4},{6,7},{7,6},{8,9},{9,8},{10,11... | collective-permute-start | bytes 245768 | tf_op jit(solution)/shard_map/ppermute | solution.py:332
  102.4 101.9 %collective-permute-start.27 = (f32[160,128]{1,0:T(8,128)}, f32[160,128]{1,0:T(8,128)}, u32[]{:S(2)}, u32[]{:S(2)}) collective-permute-start(f32[160,128]{1,0:T(8,128)} %slice.333), channel_id=1, source_target_pairs={{0,1},{1,0},{2,3},{3,2},{4,5},{5,4},{6,7},{7,6},{8,9},{9,8},{10,11... | collective-permute-start | bytes 245768 | tf_op jit(solution)/shard_map/ppermute | solution.py:332
  105.6 101.1 %collective-permute-start.32 = (f32[160,128]{1,0:T(8,128)}, f32[160,128]{1,0:T(8,128)}, u32[]{:S(2)}, u32[]{:S(2)}) collective-permute-start(f32[160,128]{1,0:T(8,128)} %slice.337), channel_id=1, source_target_pairs={{0,1},{1,0},{2,3},{3,2},{4,5},{5,4},{6,7},{7,6},{8,9},{9,8},{10,11... | collective-permute-start | bytes 245768 | tf_op jit(solution)/shard_map/ppermute | solution.py:332
  110.7 16.2 %collective-permute-start.1 = (f32[160,384]{1,0:T(8,128)}, f32[160,384]{1,0:T(8,128)}, u32[]{:S(2)}, u32[]{:S(2)}) collective-permute-start(f32[160,384]{1,0:T(8,128)} %slice.299), channel_id=1, source_target_pairs={{0,1},{1,0},{2,3},{3,2},{4,5},{5,4},{6,7},{7,6},{8,9},{9,8},{10,11... | collective-permute-start | bytes 737288 | tf_op jit(solution)/shard_map/ppermute | solution.py:332
  117.9 34.0 %collective-permute-start.9 = (bf16[896,384]{0,1:T(8,128)(2,1)}, bf16[896,384]{0,1:T(8,128)(2,1)}, u32[]{:S(2)}, u32[]{:S(2)}) collective-permute-start(bf16[896,384]{0,1:T(8,128)(2,1)} %pad_maximum_fusion.5), channel_id=1, source_target_pairs={{0,16},{1,3},{2,18},{3,1},{16,0},{17,19},{18,2},{19,17},{4,20},{5,... | collective-permute-start | bytes 2064392 | tf_op jit(solution)/shard_map/ppermute | solution.py:299
  123.3 4.6 %copy-start.13 = (f32[320,384]{1,0:T(8,128)S(1)}, f32[320,384]{1,0:T(8,128)}, u32[]{:S(2)}) copy-start(f32[320,384]{1,0:T(8,128)} %copy-done.12) | copy-start | bytes 1474564
  126.9 10.9 %collective-permute-start.4 = (bf16[896,384]{0,1:T(8,128)(2,1)S(1)}, bf16[896,384]{0,1:T(8,128)(2,1)S(1)}, u32[]{:S(2)}, u32[]{:S(2)}) collective-permute-start(bf16[896,384]{0,1:T(8,128)(2,1)S(1)} %pad_maximum_fusion.4), channel_id=1, source_target_pairs={{0,16},{1,3},{2,18},{3,1},{16,0},{17,19},{18,2},{19,17},{4,20},{5,... | collective-permute-start | bytes 2064392 | tf_op jit(solution)/shard_map/ppermute | solution.py:299
  137.8 28.4 %collective-permute-start.14 = (bf16[896,384]{0,1:T(8,128)(2,1)}, bf16[896,384]{0,1:T(8,128)(2,1)}, u32[]{:S(2)}, u32[]{:S(2)}) collective-permute-start(bf16[896,384]{0,1:T(8,128)(2,1)} %pad_maximum_fusion.6), channel_id=1, source_target_pairs={{0,16},{1,3},{2,18},{3,1},{16,0},{17,19},{18,2},{19,17},{4,20},{5,... | collective-permute-start | bytes 2064392 | tf_op jit(solution)/shard_map/ppermute | solution.py:299
  152.0 28.8 %collective-permute-start.5 = (f32[160,384]{1,0:T(8,128)}, f32[160,384]{1,0:T(8,128)}, u32[]{:S(2)}, u32[]{:S(2)}) collective-permute-start(f32[160,384]{1,0:T(8,128)} %slice.306), channel_id=1, source_target_pairs={{0,1},{1,0},{2,3},{3,2},{4,5},{5,4},{6,7},{7,6},{8,9},{9,8},{10,11... | collective-permute-start | bytes 737288 | tf_op jit(solution)/shard_map/ppermute | solution.py:332
  166.3 16.0 %collective-permute-start.10 = (f32[160,384]{1,0:T(8,128)}, f32[160,384]{1,0:T(8,128)}, u32[]{:S(2)}, u32[]{:S(2)}) collective-permute-start(f32[160,384]{1,0:T(8,128)} %slice.313), channel_id=1, source_target_pairs={{0,1},{1,0},{2,3},{3,2},{4,5},{5,4},{6,7},{7,6},{8,9},{9,8},{10,11... | collective-permute-start | bytes 737288 | tf_op jit(solution)/shard_map/ppermute | solution.py:332
  180.8 3.2 %copy-start.27 = (f32[128]{0:T(128)S(1)}, f32[128]{0:T(128)}, u32[]{:S(2)}) copy-start(f32[128]{0:T(128)} %get-tuple-element.72) | copy-start | bytes 1540
  180.8 3.2 %copy-start.28 = (f32[128]{0:T(128)S(1)}, f32[128]{0:T(128)}, u32[]{:S(2)}) copy-start(f32[128]{0:T(128)} %get-tuple-element.71) | copy-start | bytes 1540
  180.8 3.2 %copy-start.31 = (f32[160]{0:T(256)S(1)}, f32[160]{0:T(256)}, u32[]{:S(2)}) copy-start(f32[160]{0:T(256)} %add_rsqrt_fusion.6) | copy-start | bytes 1924
  180.8 3.2 %copy-start.32 = (f32[160]{0:T(256)S(1)}, f32[160]{0:T(256)}, u32[]{:S(2)}) copy-start(f32[160]{0:T(256)} %add_rsqrt_fusion.7) | copy-start | bytes 1924
  180.9 2.8 %collective-permute-start.15 = (f32[160,384]{1,0:T(8,128)S(1)}, f32[160,384]{1,0:T(8,128)S(1)}, u32[]{:S(2)}, u32[]{:S(2)}) collective-permute-start(f32[160,384]{1,0:T(8,128)S(1)} %slice.320), channel_id=1, source_target_pairs={{0,1},{1,0},{2,3},{3,2},{4,5},{5,4},{6,7},{7,6},{8,9},{9,8},{10,11... | collective-permute-start | bytes 737288 | tf_op jit(solution)/shard_map/ppermute | solution.py:332
  183.7 10.8 %copy-start.25 = (f32[320,128]{1,0:T(8,128)S(1)}, f32[320,128]{1,0:T(8,128)}, u32[]{:S(2)}) copy-start(f32[320,128]{1,0:T(8,128)} %copy-done.24) | copy-start | bytes 491524
  183.7 14.9 %copy-start.26 = (f32[160,128]{1,0:T(8,128)S(1)}, f32[160,128]{1,0:T(8,128)}, u32[]{:S(2)}) copy-start(f32[160,128]{1,0:T(8,128)} %slice.325) | copy-start | bytes 245764
  184.0 20.3 %copy-start.23 = (f32[320,128]{1,0:T(8,128)S(1)}, f32[320,128]{1,0:T(8,128)}, u32[]{:S(2)}) copy-start(f32[320,128]{1,0:T(8,128)} %copy-done.22) | copy-start | bytes 491524
  184.0 22.7 %copy-start.21 = (f32[320,128]{1,0:T(8,128)S(1)}, f32[320,128]{1,0:T(8,128)}, u32[]{:S(2)}) copy-start(f32[320,128]{1,0:T(8,128)} %copy-done.20) | copy-start | bytes 491524
  184.3 29.7 %copy-start.19 = (f32[320,128]{1,0:T(8,128)S(1)}, f32[320,128]{1,0:T(8,128)}, u32[]{:S(2)}) copy-start(f32[320,128]{1,0:T(8,128)} %copy-done.18) | copy-start | bytes 491524
  184.3 14.3 %collective-permute-start.11 = (bf16[160,384]{1,0:T(8,128)(2,1)S(1)}, bf16[160,384]{1,0:T(8,128)(2,1)S(1)}, u32[]{:S(2)}, u32[]{:S(2)}) collective-permute-start(bf16[160,384]{1,0:T(8,128)(2,1)S(1)} %pad_maximum_fusion.21), channel_id=1, source_target_pairs={{0,8},{4,12},{8,0},{12,4},{1,9},{5,13},{9,1},{13,5},{2,10},{6,14},... | collective-permute-start | bytes 368648 | tf_op jit(solution)/shard_map/ppermute | solution.py:192
  192.3 10.2 %collective-permute-start.6 = (bf16[160,384]{1,0:T(8,128)(2,1)S(1)}, bf16[160,384]{1,0:T(8,128)(2,1)S(1)}, u32[]{:S(2)}, u32[]{:S(2)}) collective-permute-start(bf16[160,384]{1,0:T(8,128)(2,1)S(1)} %pad_maximum_fusion.20), channel_id=1, source_target_pairs={{0,12},{4,0},{8,4},{12,8},{1,13},{5,1},{9,5},{13,9},{2,14},{6,2},{... | collective-permute-start | bytes 368648 | tf_op jit(solution)/shard_map/ppermute | solution.py:192
  192.4 11.7 %collective-permute-start.16 = (bf16[160,384]{1,0:T(8,128)(2,1)S(1)}, bf16[160,384]{1,0:T(8,128)(2,1)S(1)}, u32[]{:S(2)}, u32[]{:S(2)}) collective-permute-start(bf16[160,384]{1,0:T(8,128)(2,1)S(1)} %pad_maximum_fusion.22), channel_id=1, source_target_pairs={{0,4},{4,8},{8,12},{12,0},{1,5},{5,9},{9,13},{13,1},{2,6},{6,10},{... | collective-permute-start | bytes 368648 | tf_op jit(solution)/shard_map/ppermute | solution.py:192
  198.6 9.1 %collective-permute-start.18 = (f32[160,128]{1,0:T(8,128)S(1)}, f32[160,128]{1,0:T(8,128)S(1)}, u32[]{:S(2)}, u32[]{:S(2)}) collective-permute-start(f32[160,128]{1,0:T(8,128)S(1)} %copy-done.26), channel_id=1, source_target_pairs={{0,1},{1,0},{2,3},{3,2},{4,5},{5,4},{6,7},{7,6},{8,9},{9,8},{10,11... | collective-permute-start | bytes 245768 | tf_op jit(solution)/shard_map/ppermute | solution.py:332
  202.5 11.5 %collective-permute-start.23 = (bf16[160,128]{1,0:T(8,128)(2,1)S(1)}, bf16[160,128]{1,0:T(8,128)(2,1)S(1)}, u32[]{:S(2)}, u32[]{:S(2)}) collective-permute-start(bf16[160,128]{1,0:T(8,128)(2,1)S(1)} %fusion.28), channel_id=1, source_target_pairs={{0,12},{4,0},{8,4},{12,8},{1,13},{5,1},{9,5},{13,9},{2,14},{6,2},{... | collective-permute-start | bytes 122888 | tf_op jit(solution)/shard_map/ppermute | solution.py:192
  204.2 9.9 %collective-permute-start.35 = (bf16[640,256]{1,0:T(8,128)(2,1)S(1)}, bf16[640,256]{1,0:T(8,128)(2,1)S(1)}, u32[]{:S(2)}, u32[]{:S(2)}) collective-permute-start(bf16[640,256]{1,0:T(8,128)(2,1)S(1)} %pad_maximum_fusion.7), channel_id=1, source_target_pairs={{0,2},{2,0},{1,3},{3,1},{4,6},{6,4},{5,7},{7,5},{8,10},{10,8},{9,1... | collective-permute-start | bytes 983048 | tf_op jit(solution)/shard_map/ppermute | solution.py:358
  205.2 8.9 %collective-permute-start.28 = (bf16[160,128]{1,0:T(8,128)(2,1)S(1)}, bf16[160,128]{1,0:T(8,128)(2,1)S(1)}, u32[]{:S(2)}, u32[]{:S(2)}) collective-permute-start(bf16[160,128]{1,0:T(8,128)(2,1)S(1)} %fusion.27), channel_id=1, source_target_pairs={{0,8},{4,12},{8,0},{12,4},{1,9},{5,13},{9,1},{13,5},{2,10},{6,14},... | collective-permute-start | bytes 122888 | tf_op jit(solution)/shard_map/ppermute | solution.py:192
  207.6 6.5 %collective-permute-start.33 = (bf16[160,128]{1,0:T(8,128)(2,1)S(1)}, bf16[160,128]{1,0:T(8,128)(2,1)S(1)}, u32[]{:S(2)}, u32[]{:S(2)}) collective-permute-start(bf16[160,128]{1,0:T(8,128)(2,1)S(1)} %fusion.26), channel_id=1, source_target_pairs={{0,4},{4,8},{8,12},{12,0},{1,5},{5,9},{9,13},{13,1},{2,6},{6,10},{... | collective-permute-start | bytes 122888 | tf_op jit(solution)/shard_map/ppermute | solution.py:192
  207.7 6.4 %collective-permute-start.34 = (bf16[640,256]{1,0:T(8,128)(2,1)S(1)}, bf16[640,256]{1,0:T(8,128)(2,1)S(1)}, u32[]{:S(2)}, u32[]{:S(2)}) collective-permute-start(bf16[640,256]{1,0:T(8,128)(2,1)S(1)} %pad_maximum_fusion.7), channel_id=1, source_target_pairs={{0,1},{1,0},{2,3},{3,2},{4,5},{5,4},{6,7},{7,6},{8,9},{9,8},{10,11... | collective-permute-start | bytes 983048 | tf_op jit(solution)/shard_map/ppermute | solution.py:360
  214.0 1.6 collective-permute-start.36
  225.2 3.1 %collective-permute-start.37 = (f32[2,640,256]{2,1,0:T(8,128)S(1)}, f32[2,640,256]{2,1,0:T(8,128)S(1)}, u32[]{:S(2)}, u32[]{:S(2)}) collective-permute-start(f32[2,640,256]{2,1,0:T(8,128)S(1)} %slice.279), channel_id=1, source_target_pairs={{0,1},{1,0},{2,3},{3,2},{4,5},{5,4},{6,7},{7,6},{8,9},{9,8},{10,11... | collective-permute-start | bytes 3932168 | tf_op jit(solution)/shard_map/ppermute | solution.py:364
  228.5 25.5 %copy-start.7 = (bf16[1792,384]{0,1:T(8,128)(2,1)S(1)}, bf16[1792,384]{0,1:T(8,128)(2,1)}, u32[]{:S(2)}) copy-start(bf16[1792,384]{0,1:T(8,128)(2,1)} %dynamic_update_slice.79) | copy-start | bytes 4128772
  228.5 9.8 %collective-permute-start.38 = (bf16[640,256]{1,0:T(8,128)(2,1)S(1)}, bf16[640,256]{1,0:T(8,128)(2,1)S(1)}, u32[]{:S(2)}, u32[]{:S(2)}) collective-permute-start(bf16[640,256]{1,0:T(8,128)(2,1)S(1)} %fusion.25), channel_id=1, source_target_pairs={{0,2},{2,0},{1,3},{3,1},{4,6},{6,4},{5,7},{7,5},{8,10},{10,8},{9,1... | collective-permute-start | bytes 983048 | tf_op jit(solution)/shard_map/ppermute | solution.py:365
  238.4 15.6 %copy-start.6 = (bf16[1792,384]{0,1:T(8,128)(2,1)S(1)}, bf16[1792,384]{0,1:T(8,128)(2,1)}, u32[]{:S(2)}) copy-start(bf16[1792,384]{0,1:T(8,128)(2,1)} %dynamic_update_slice.83) | copy-start | bytes 4128772
  238.4 15.5 %copy-start.5 = (bf16[1792,384]{0,1:T(8,128)(2,1)S(1)}, bf16[1792,384]{0,1:T(8,128)(2,1)}, u32[]{:S(2)}) copy-start(bf16[1792,384]{0,1:T(8,128)(2,1)} %dynamic_update_slice.75) | copy-start | bytes 4128772
  238.5 15.5 %copy-start.4 = (bf16[1792,3,128]{0,2,1:T(8,128)(2,1)S(1)}, bf16[1792,3,128]{0,2,1:T(8,128)(2,1)}, u32[]{:S(2)}) copy-start(bf16[1792,3,128]{0,2,1:T(8,128)(2,1)} %copy.9) | copy-start | bytes 4128772
  238.5 8.1 %collective-permute-start.40 = (bf16[160,384]{1,0:T(8,128)(2,1)S(1)}, bf16[160,384]{1,0:T(8,128)(2,1)S(1)}, u32[]{:S(2)}, u32[]{:S(2)}) collective-permute-start(bf16[160,384]{1,0:T(8,128)(2,1)S(1)} %get-tuple-element.48), channel_id=1, source_target_pairs={{0,12},{4,0},{8,4},{12,8},{1,13},{5,1},{9,5},{13,9},{2,14},{6,2},{... | collective-permute-start | bytes 368648 | tf_op jit(solution)/shard_map/ppermute | solution.py:192
  238.9 8.7 %collective-permute-start.39 = (bf16[160,384]{1,0:T(8,128)(2,1)S(1)}, bf16[160,384]{1,0:T(8,128)(2,1)S(1)}, u32[]{:S(2)}, u32[]{:S(2)}) collective-permute-start(bf16[160,384]{1,0:T(8,128)(2,1)S(1)} %get-tuple-element.49), channel_id=1, source_target_pairs={{0,4},{4,8},{8,12},{12,0},{1,5},{5,9},{9,13},{13,1},{2,6},{6,10},{... | collective-permute-start | bytes 368648 | tf_op jit(solution)/shard_map/ppermute | solution.py:192
  240.6 9.9 %collective-permute-start.41 = (bf16[160,384]{1,0:T(8,128)(2,1)S(1)}, bf16[160,384]{1,0:T(8,128)(2,1)S(1)}, u32[]{:S(2)}, u32[]{:S(2)}) collective-permute-start(bf16[160,384]{1,0:T(8,128)(2,1)S(1)} %get-tuple-element.50), channel_id=1, source_target_pairs={{0,8},{4,12},{8,0},{12,4},{1,9},{5,13},{9,1},{13,5},{2,10},{6,14},... | collective-permute-start | bytes 368648 | tf_op jit(solution)/shard_map/ppermute | solution.py:192
  252.0 1.9 collective-permute-start.42
  256.0 2.0 collective-permute-start.43
  (13 other events, 22.5 us)

commit v2 on v1

--- a/solution.py
+++ b/solution.py
@@ -267,6 +267,186 @@
     )(q, g, k, v)
 
 
+def project_kernel(pieces, rows, *refs):
+    if pieces:
+        places, values = refs[:2]
+        blocks = refs[2 : 2 + pieces]
+        own_ref, other_ref, whole, sems = refs[2 + pieces :]
+        copies = []
+        for i, block in enumerate(blocks):
+            size = block.shape[0]
+            at = pl.ds(pl.multiple_of(places[i] * size, size), size)
+            copies.append(pltpu.make_async_copy(block, whole.at[at, :], sems.at[i]))
+            copies[-1].start()
+        for copy in copies:
+            copy.wait()
+    else:
+        values, whole, own_ref, other_ref = refs
+    out = jnp.dot(values[...], whole[...], preferred_element_type=jnp.float32)
+    own_ref[...] = out[:rows]
+    other_ref[...] = out[rows:]
+
+
+def project(values, weights, places=None):
+    rows = values.shape[0] // 2
+    half = values.shape[1]
+    f32 = jnp.float32
+    pieces = 0 if places is None else len(weights)
+    columns = weights[0].shape[1]
+    vmem = pl.BlockSpec(memory_space=pltpu.VMEM)
+    smem = pl.BlockSpec(memory_space=pltpu.SMEM)
+    anywhere = pl.BlockSpec(memory_space=pl.ANY)
+    scratch = [pltpu.VMEM((half, columns), jnp.bfloat16), pltpu.SemaphoreType.DMA((pieces,))]
+    return pl.pallas_call(
+        partial(project_kernel, pieces, rows),
+        out_shape=(jax.ShapeDtypeStruct((rows, columns), f32),) * 2,
+        in_specs=[smem, vmem] + [anywhere] * pieces if pieces else [vmem, vmem],
+        out_specs=(vmem, vmem),
+        scratch_shapes=scratch if pieces else [],
+        compiler_params=pltpu.CompilerParams(vmem_limit_bytes=32 * 1024 * 1024),
+        cost_estimate=pl.CostEstimate(
+            flops=4 * rows * half * columns,
+            bytes_accessed=2 * half * (columns + 2 * rows),
+            transcendentals=0,
+        ),
+        name="project",
+    )(*((places,) if pieces else ()), values, *weights)
+
+
+def unit(raw):
+    back = lax.rsqrt(jnp.mean(raw * raw, axis=-1, keepdims=True) + 1e-06)
+    return raw * back, back
+
+
+def finish_kernel(own_ref, come_ref, gain_ref, raw_ref, query_ref, kv_ref):
+    raw = own_ref[...] + come_ref[...]
+    raw_ref[...] = raw
+    dim = query_ref.shape[1]
+    qh, _ = unit(raw[:, :dim])
+    kh, _ = unit(raw[:, dim : 2 * dim])
+    query_ref[...] = (qh * gain_ref[0:1, :]).astype(jnp.bfloat16)
+    kv_ref[:, :dim] = (kh * gain_ref[1:2, :]).astype(jnp.bfloat16)
+    kv_ref[:, dim:] = raw[:, 2 * dim :].astype(jnp.bfloat16)
+
+
+def finish(own, come, gains):
+    rows, dim = own.shape[0], gains.shape[1]
+    vmem = pl.BlockSpec(memory_space=pltpu.VMEM)
+    return pl.pallas_call(
+        finish_kernel,
+        out_shape=(
+            jax.ShapeDtypeStruct(own.shape, jnp.float32),
+            jax.ShapeDtypeStruct((rows, dim), jnp.bfloat16),
+            jax.ShapeDtypeStruct((rows, 2 * dim), jnp.bfloat16),
+        ),
+        in_specs=[vmem] * 3,
+        out_specs=(vmem,) * 3,
+        cost_estimate=pl.CostEstimate(
+            flops=20 * own.size, bytes_accessed=16 * own.size, transcendentals=2 * rows
+        ),
+        name="finish",
+    )(own, come, gains)
+
+
+def unfinish_kernel(count, gain_ref, *refs):
+    raws, dqs, dkvs, out_ref = refs[:count], refs[count : 2 * count], refs[2 * count : 3 * count], refs[-1]
+    dim = gain_ref.shape[1]
+
+    def unit_back(raw, gain, upstream):
+        hat, scale_back = unit(raw)
+        up = upstream.astype(jnp.float32) * gain
+        return scale_back * (up - hat * jnp.mean(up * hat, axis=-1, keepdims=True))
+
+    for i in range(count):
+        at = 3 * dim * i
+        raw, dkv = raws[i], dkvs[i]
+        dq = unit_back(raw[:, :dim], gain_ref[0:1, :], dqs[i][...])
+        dk = unit_back(raw[:, dim : 2 * dim], gain_ref[1:2, :], dkv[:, :dim])
+        out_ref[:, at : at + dim] = dq.astype(jnp.bfloat16)
+        out_ref[:, at + dim : at + 2 * dim] = dk.astype(jnp.bfloat16)
+        out_ref[:, at + 2 * dim : at + 3 * dim] = dkv[:, dim:]
+
+
+def unfinish(gains, raws, dqs, dkvs):
+    count = len(raws)
+    rows, columns = raws[0].shape
+    vmem = pl.BlockSpec(memory_space=pltpu.VMEM)
+    return pl.pallas_call(
+        partial(unfinish_kernel, count),
+        out_shape=jax.ShapeDtypeStruct((rows, count * columns), jnp.bfloat16),
+        in_specs=[vmem] * (1 + 3 * count),
+        out_specs=vmem,
+        cost_estimate=pl.CostEstimate(
+            flops=20 * count * rows * columns,
+            bytes_accessed=8 * count * rows * columns,
+            transcendentals=2 * rows,
+        ),
+        name="unfinish",
+    )(gains, *raws, *dqs, *dkvs)
+
+
+def back_project_kernel(count, places, mine, theirs, *refs):
+    whole_own = refs[0]
+    blocks = [refs[1 + 4 * i : 5 + 4 * i] for i in range(count - 1)]
+    own_ref, other_ref, grads, whole, sems = refs[1 + 4 * (count - 1) :]
+    rows, columns = mine.shape
+    part = blocks[0][0].shape[0]
+    width = columns // count
+    copies = []
+    for i, four in enumerate(blocks):
+        copies.append([])
+        for j, block in enumerate(four):
+            at = pl.ds(pl.multiple_of(places[j] * part, part), part)
+            copies[i].append(pltpu.make_async_copy(block, whole.at[i, at, :], sems.at[4 * i + j]))
+            copies[i][j].start()
+    grads[:rows] = mine[...]
+    grads[rows:] = theirs[...]
+    nt = (((1,), (1,)), ((), ()))
+    total = lax.dot_general(grads[:, :width], whole_own[...], nt, preferred_element_type=jnp.float32)
+    for i, four in enumerate(copies):
+        for copy in four:
+            copy.wait()
+        at = width * (i + 1)
+        total += lax.dot_general(
+            grads[:, at : at + width], whole[i], nt, preferred_element_type=jnp.float32
+        )
+    own_ref[...] = total[:rows]
+    other_ref[...] = total[rows:].astype(jnp.bfloat16)
+
+
+def back_project(mine, theirs, whole_own, blocks, places):
+    count = 1 + len(blocks)
+    rows, columns = mine.shape
+    half, width = whole_own.shape
+    vmem = pl.BlockSpec(memory_space=pltpu.VMEM)
+    smem = pl.BlockSpec(memory_space=pltpu.SMEM)
+    anywhere = pl.BlockSpec(memory_space=pl.ANY)
+    flat = [block for four in blocks for block in four]
+    return pl.pallas_call(
+        partial(back_project_kernel, count),
+        out_shape=(
+            jax.ShapeDtypeStruct((rows, half), jnp.float32),
+            jax.ShapeDtypeStruct((rows, half), jnp.bfloat16),
+        ),
+        in_specs=[smem, vmem, vmem, vmem] + [anywhere] * len(flat),
+        out_specs=(vmem, vmem),
+        scratch_shapes=[
+            pltpu.VMEM((2 * rows, columns), jnp.bfloat16),
+            pltpu.VMEM((count - 1, half, width), jnp.bfloat16),
+            pltpu.SemaphoreType.DMA((len(flat),)),
+        ],
+        compiler_params=pltpu.CompilerParams(vmem_limit_bytes=40 * 1024 * 1024),
+        cost_estimate=pl.CostEstimate(
+            flops=4 * rows * half * columns, bytes_accessed=2 * half * columns, transcendentals=0
+        ),
+        name="back_project",
+    )(places, mine, theirs, whole_own, *flat)
+
+
+def after(value, *earlier):
+    return lax.optimization_barrier((value, *earlier))[0]
+
+
 def weight_gather_body(count, tokens, cotangent, modulation, w_qkv, w_out, qk_gain):
     bf16, f32 = jnp.bfloat16, jnp.float32
     dim = qk_gain.shape[1]
@@ -281,35 +461,28 @@
     across = 2 * group + (1 - chip)
     over = 2 * (1 - group) + chip
     far = 3 - mine
-    first = jnp.where(core == 0, across, over)
-    second = jnp.where(core == 0, over, across)
-
-    def assemble(pieces):
-        whole = jnp.zeros((half, pieces[0].shape[1]), bf16)
-        for place, piece in pieces_at(pieces):
-            whole = lax.dynamic_update_slice(whole, piece, (place * part, 0))
-        return whole
-
-    def pieces_at(pieces):
-        own, one, pair = pieces
-        return ((mine, own), (first, one), (second, pair[:part]), (far, pair[part:]))
+    places = jnp.stack(
+        [mine, jnp.where(core == 0, across, over), jnp.where(core == 0, over, across), far]
+    ).astype(jnp.int32)
+    side = jnp.where(core == 0, chip, group)
+    sides = jnp.stack([side, 1 - side]).astype(jnp.int32)
 
     def hand_round(own):
         one = lax.ppermute(own, PLANE, plane_swap(True))
-        pair = lax.ppermute(jnp.concatenate([own, one], axis=0), PLANE, plane_swap(False))
-        return assemble((own, one, pair))
-
+        two = lax.ppermute(own, PLANE, plane_swap(False))
+        return own, one, two, lax.ppermute(one, PLANE, plane_swap(False))
+
+    order = [1, count - 1] + list(range(2, count - 1))
     own_in = lax.dynamic_slice(w_qkv, (this + mine * part, 0, 0), (part, 3, dim)).reshape(part, 3 * dim)
-    own_out = lax.dynamic_slice(w_out, (0, this + mine * part), (dim, part)).T
-    w_in_half = lax.dynamic_slice(w_qkv, (this, 0, 0), (half, 3, dim)).reshape(half, 3 * dim)
-    w_out_half = lax.dynamic_slice(w_out, (0, this), (dim, half)).T
-    order = [1, count - 1] + list(range(2, count - 1))
-    w_in = {0: w_in_half}
-    w_o = {0: w_out_half}
+    w_in, w_o = {}, {}
+    last = None
     for step in order:
-        w_in[step] = hand_round(around(own_in, step, count))
+        last = around(own_in if last is None else after(own_in, last), step, count)
+        w_in[step] = hand_round(last)
+    own_out = lax.dynamic_slice(w_out, (0, this + side * 2 * part), (dim, 2 * part)).T
     for step in order:
-        w_o[step] = hand_round(around(own_out, step, count))
+        last = around(after(own_out, last), step, count)
+        w_o[step] = (last, lax.ppermute(last, PLANE, plane_swap(True)))
 
     shift, scale, gate = modulation[0], 1.0 + modulation[1], modulation[2]
     x = tokens.astype(f32)
@@ -326,69 +499,51 @@
 
     normed_half = both_cores(normed)
     scaled_half = both_cores(scaled)
-
-    def project(values, weights):
-        out = jnp.dot(values, weights, preferred_element_type=f32)
-        return out[:rows] + lax.ppermute(out[rows:], "seq", CORE_SWAP)
-
-    gain_q, gain_k = qk_gain[0], qk_gain[1]
-
-    def unit(raw):
-        back = lax.rsqrt(jnp.mean(raw * raw, axis=-1, keepdims=True) + 1e-06)
-        return raw * back, back
-
-    units = {}
-    arrived = {}
+    w_in_half = lax.dynamic_slice(w_qkv, (this, 0, 0), (half, 3, dim)).reshape(half, 3 * dim)
+    w_out_half = lax.dynamic_slice(w_out, (0, this), (dim, half)).T
+
     slots = [0] + order
+    raws, queries, kvs, grads = {}, {}, {}, {}
     for step in slots:
-        qkv = project(normed_half, w_in[step])
-        qh, qs = unit(qkv[:, :dim])
-        kh, ks = unit(qkv[:, dim : 2 * dim])
-        units[step] = (qh, qs, kh, ks)
-        ready = jnp.concatenate([qh * gain_q, kh * gain_k, qkv[:, 2 * dim :]], axis=1).astype(bf16)
-        arrived[step] = around(ready, -step, count) if step else ready
-    heads = jnp.concatenate([arrived[i] for i in range(count)], axis=0)
-    grads = {}
+        if step:
+            own, away = project(normed_half, w_in[step], places)
+        else:
+            own, away = project(normed_half, (w_in_half,))
+        raw, query, kv = finish(own, lax.ppermute(away, "seq", CORE_SWAP), qk_gain)
+        raws[step] = raw
+        queries[step] = around(query, -step, count) if step else query
+        kvs[step] = around(kv, -step, count) if step else kv
     for step in slots:
-        ready = project(scaled_half, w_o[step]).astype(bf16)
+        if step:
+            own, away = project(scaled_half, w_o[step], sides)
+        else:
+            own, away = project(scaled_half, (w_out_half,))
+        ready = (own + lax.ppermute(away, "seq", CORE_SWAP)).astype(bf16)
         grads[step] = around(ready, -step, count) if step else ready
-    g = jnp.concatenate([grads[i] for i in range(count)], axis=0)
-
-    kv = heads[:, dim:]
+    q = jnp.concatenate([queries[i] for i in slots], axis=0)
+    g = jnp.concatenate([grads[i] for i in slots], axis=0)
+    kv = jnp.concatenate([kvs[i] for i in slots], axis=0)
+
     kv_chip = lax.ppermute(kv, "seq", CHIP_SWAP)
     kv_all = jnp.concatenate(
         [kv, lax.ppermute(kv, "seq", CORE_SWAP), kv_chip, lax.ppermute(kv_chip, "seq", CORE_SWAP)], axis=0
     )
-    dq, dk, dv = attention(heads[:, :dim], g, kv_all[:, :dim], kv_all[:, dim:])
+    dq, dk, dv = attention(q, g, kv_all[:, :dim], kv_all[:, dim:])
+    dq = dq.astype(bf16).reshape(count, rows, dim)
+    dqs = {step: around(dq[i], step, count) if step else dq[i] for i, step in enumerate(slots)}
     dkv = jnp.concatenate([dk, dv], axis=1).reshape(4, count * rows, 2 * dim)
     summed = dkv[0::2] + lax.ppermute(dkv[1::2], "seq", CORE_SWAP)
     dkv = summed[0] + lax.ppermute(summed[1].astype(bf16), "seq", CHIP_SWAP).astype(f32)
-    back = jnp.concatenate([dq, dkv], axis=1).astype(bf16).reshape(count, rows, 3 * dim)
-
-    def unit_back(hat, scale_back, gain, upstream):
-        up = upstream * gain
-        return scale_back * (up - hat * jnp.mean(up * hat, axis=-1, keepdims=True))
-
-    grads_in = []
-    weights = []
-    for step in slots:
-        d = around(back[step], step, count) if step else back[0]
-        qh, qs, kh, ks = units[step]
-        dqn, dkn = d[:, :dim].astype(f32), d[:, dim : 2 * dim].astype(f32)
-        grads_in += [
-            unit_back(qh, qs, gain_q, dqn).astype(bf16),
-            unit_back(kh, ks, gain_k, dkn).astype(bf16),
-            d[:, 2 * dim :],
-        ]
-        weights.append(w_in[step])
-    dqkv = jnp.concatenate(grads_in, axis=1)
-    dqkv = jnp.concatenate([dqkv, lax.ppermute(dqkv, "seq", CORE_SWAP)], axis=0)
-    dn = lax.dot_general(
-        dqkv, jnp.concatenate(weights, axis=1), (((1,), (1,)), ((), ())), preferred_element_type=f32
-    )
-    away = lax.ppermute(dn[rows:].astype(bf16), "seq", CORE_SWAP).astype(f32)
-    low = jnp.where(core == 0, dn[:rows], away)
-    high = jnp.where(core == 0, away, dn[:rows])
+    dkv = dkv.astype(bf16).reshape(count, rows, 2 * dim)
+    dkvs = {step: around(dkv[i], step, count) if step else dkv[i] for i, step in enumerate(slots)}
+
+    dqkv = unfinish(qk_gain, *[[each[i] for i in slots] for each in (raws, dqs, dkvs)])
+    own, away = back_project(
+        dqkv, lax.ppermute(dqkv, "seq", CORE_SWAP), w_in_half, [w_in[i] for i in order], places
+    )
+    away = lax.ppermute(away, "seq", CORE_SWAP).astype(f32)
+    low = jnp.where(core == 0, own, away)
+    high = jnp.where(core == 0, away, own)
     dhat = jnp.concatenate([low, high], axis=1) * scale
     return cot + inv * (dhat - xhat * jnp.mean(dhat * xhat, axis=-1, keepdims=True))
 

time: 264 us -> 188 us (0.71)
  local copies, waits for them, and re-layouts: 111 us -> 39.3 us
  Pallas kernels: 9.1 us -> 43 us
  matrix products: 17.9 us -> 0 us
  other arithmetic: 29.8 us -> 16.8 us
  waiting for transfers between devices: 47.5 us -> 36.5 us
  starting transfers between devices: 45.6 us -> 50.1 us
    dynamic_update_slice x24 -> x0, local copies, waits for them, and re-layouts: 78 us -> none  [assemble(): whole = lax.dynamic_update_slice(whole, piece, (place * part, 0))]
    pallas_call x0 -> x14, Pallas kernels: none -> 33.9 us  [the longest x8 18.5 us: project(): pl.pallas_call(partial(project_kernel, pieces, rows), out_shape=(jax.Shap...]
    unnamed x70 -> x86, local copies, waits for them, and re-layouts: 3.8 us -> 22.9 us
    dot_general x9 -> x0, matrix products: 17.9 us -> none  [the longest x8 16 us: project(): out = jnp.dot(values, weights, preferred_element_type=f32)]
    slice x20 -> x3, local copies, waits for them, and re-layouts: 15.3 us -> 1.37 us  [the longest x1 0.66 us: weight_gather_body(): dkv[i]]
    ppermute x16 -> x19, waiting for transfers between devices: 11.3 us -> 3.96 us  [the longest x1 2.07 us: weight_gather_body(): lax.ppermute(dqkv, 'seq', CORE_SWAP)]
    concatenate x12 -> x4, other arithmetic: 11.1 us -> 4.27 us  [the longest x2 3.45 us: both_cores(): return jnp.concatenate([keep, lax.ppermute(send, 'seq', CORE_SWAP)], axis=0)]
    another operation x6 -> x0, local copies, waits for them, and re-layouts: 6.01 us -> none
  transfers between devices with their start and end apart: 44 -> 50, of which waited for: 12 -> 11; matrix products, arithmetic and copies ran while one was open for 57% -> 20% of each run, Pallas kernels for 0% -> 14%
where the time goes in v2:
time: 188 us; the launch traced here: 186 us
  starting transfers between devices  50.1 us (27%)
  Pallas kernels  43 us (23%)
  local copies, waits for them, and re-layouts  39.3 us (21%)
  waiting for transfers between devices  36.5 us (19%)
  other arithmetic  16.8 us (9%)
    ppermute x21, starting transfers between devices, around(): lax.ppermute(value, 'tensor', [(i, (i + step) % count) for i in range(cou...  30.6 us
    unnamed x86, local copies, waits for them, and re-layouts  22.9 us
    pallas_call x8, Pallas kernels, project(): pl.pallas_call(partial(project_kernel, pieces, rows), out_shape=(jax.Shap...  18.5 us
    ppermute x21, waiting for transfers between devices, around(): lax.ppermute(value, 'tensor', [(i, (i + step) % count) for i in range(cou...  16.4 us
    pallas_call x1, Pallas kernels, attention(): pl.pallas_call(partial(attention_kernel, 1.0 / math.sqrt(dim), 256), out_...  9.1 us
    pallas_call x4, Pallas kernels, finish(): pl.pallas_call(finish_kernel, out_shape=(jax.ShapeDtypeStruct(own.shape,...  7.46 us
    ppermute x1, waiting for transfers between devices, weight_gather_body(): lax.ppermute(summed[1].astype(bf16), 'seq', CHIP_SWAP).astype(f32)  6.92 us
    ppermute x3, starting transfers between devices, hand_round(): one = lax.ppermute(own, PLANE, plane_swap(True))  5.59 us
  transfers between devices with their start and end apart: 50, of which 11 were waited for; matrix products, arithmetic and copies ran while one was open for 20% of the time, Pallas kernels for 14%

profile of v2, /device:TPU:0, one launch (start us, length us, event | category | flops | bytes accessed | tf_op | source)
XLA Modules:
  0.0 186.3 jit_solution(3941190476878486157)
XLA Ops:
  0.0 1.8 copy-done
  2.9 3.0 %collective-permute-start.2 = (bf16[448,384]{1,0:T(8,128)(2,1)}, bf16[448,384]{1,0:T(8,128)(2,1)S(1)}, u32[]{:S(2)}, u32[]{:S(2)}) collective-permute-start(bf16[448,384]{1,0:T(8,128)(2,1)} %copy.14), channel_id=1, source_target_pairs={{0,4},{4,8},{8,12},{12,0},{1,5},{5,9},{9,13},{13,1},{2,6},{6,10},{... | collective-permute-start | bytes 1032200 | tf_op jit(solution)/shard_map/ppermute | solution.py:192
  5.9 1.6 fusion.9
  8.6 2.2 %fusion.3 = (bf16[160,3584]{1,0:T(8,128)(2,1)S(1)}, bf16[160,3584]{1,0:T(8,128)(2,1)S(1)}) fusion(bf16[160,3584]{1,0:T(8,128)(2,1)} %param.7, f32[3584]{0:T(1024)S(1)} %get-tuple-element.81, f32[3584]{0:T(1024)S(1)} %get-tuple-element.83, f32[3584]{0:T(1024)S(1)} %get-tuple-element.82, f32[160]{0:T(256)S(1)} %add_rsqrt_fusion, bf16[160,3584]{1,0:T(8,128)(2,1)} %param.6), kind=kLoop, calls=%fused_computation.8 | loop fusion | flops 4587520 | bytes 4631168 | tf_op jit(solution)/shard_map/convert_element_type | solution.py:493
  13.5 1.8 constant_dynamic-slice_fusion.1
  15.3 1.3 copy.21
  16.6 1.6 collective-permute-start.3
  19.3 2.5 %copy.20 = bf16[1792,3,128]{0,2,1:T(8,128)(2,1)} copy(bf16[1792,3,128]{2,0,1:T(8,128)(2,1)} %constant_dynamic-slice_fusion.5) | data formatting | bytes 2752512
  21.9 2.5 %copy.12.refs_1_.refs_0_ = bf16[1792,384]{1,0:T(8,128)(2,1)} copy(bf16[1792,384]{0,1:T(8,128)(2,1)} %bitcast.25) | data formatting | bytes 2752512 | tf_op jit(solution)/shard_map/reshape | solution.py:502
  24.4 1.9 %copy.15 = bf16[448,384]{1,0:T(8,128)(2,1)} copy(bf16[448,384]{0,1:T(8,128)(2,1)} %bitcast.23) | data formatting | bytes 688128 | tf_op jit(solution)/shard_map/optimization_barrier | solution.py:447
  26.3 2.2 %collective-permute-start.7 = (bf16[448,384]{1,0:T(8,128)(2,1)}, bf16[448,384]{1,0:T(8,128)(2,1)}, u32[]{:S(2)}, u32[]{:S(2)}) collective-permute-start(bf16[448,384]{1,0:T(8,128)(2,1)} %copy.15), channel_id=1, source_target_pairs={{0,12},{4,0},{8,4},{12,8},{1,13},{5,1},{9,5},{13,9},{2,14},{6,2},{... | collective-permute-start | bytes 1032200 | tf_op jit(solution)/shard_map/ppermute | solution.py:192
  29.1 1.5 collective-permute-start.4
  31.1 2.3 %pad_maximum_fusion.2.refs_0_.refs_1_ = bf16[320,1792]{1,0:T(8,128)(2,1)} fusion(bf16[160,1792]{1,0:T(8,128)(2,1)} %collective-permute-done.20, bf16[160,1792]{1,0:T(8,128)(2,1)} %get-tuple-element.88), kind=kLoop, calls=%fused_computation.20 | loop fusion | flops 2293760 | bytes 2293760 | tf_op jit(solution)/shard_map/concatenate | solution.py:498
  33.5 2.9 %collective-permute-done.7.refs_2_.refs_5_ = bf16[448,384]{1,0:T(8,128)(2,1)} collective-permute-done((bf16[448,384]{1,0:T(8,128)(2,1)}, bf16[448,384]{1,0:T(8,128)(2,1)}, u32[]{:S(2)}, u32[]{:S(2)}) %collective-permute-start.7) | collective-permute-done | bytes 344096 | tf_op jit(solution)/shard_map/ppermute | solution.py:192
  36.3 1.9 %copy.16 = bf16[448,384]{1,0:T(8,128)(2,1)} copy(bf16[448,384]{0,1:T(8,128)(2,1)} %bitcast.24) | data formatting | bytes 688128 | tf_op jit(solution)/shard_map/optimization_barrier | solution.py:447
  38.2 2.6 %collective-permute-start.12 = (bf16[448,384]{1,0:T(8,128)(2,1)}, bf16[448,384]{1,0:T(8,128)(2,1)}, u32[]{:S(2)}, u32[]{:S(2)}) collective-permute-start(bf16[448,384]{1,0:T(8,128)(2,1)} %copy.16), channel_id=1, source_target_pairs={{0,8},{4,12},{8,0},{12,4},{1,9},{5,13},{9,1},{13,5},{2,10},{6,14},... | collective-permute-start | bytes 1032200 | tf_op jit(solution)/shard_map/ppermute | solution.py:192
  40.8 1.3 copy-done.1
  43.8 1.6 collective-permute-start.8
  46.6 1.5 project.8
  48.7 3.4 %project.9 = (f32[160,384]{1,0:T(8,128)S(1)}, f32[160,384]{1,0:T(8,128)}) custom-call(s32[4]{0:T(128)S(1)} %copy-done.17, bf16[320,1792]{1,0:T(8,128)(2,1)S(1)} %pad_maximum_fusion.1.refs_0_.refs_1_, bf16[448,384]{1,0:T(8,128)(2,1)S(1)} %collective-permute-done.2.refs_2_.refs_1_, bf16[448,384]{1,0:T(8,128)(2,1)} %collective-permute-done.3.refs_3_.refs_2_, ...), custom_call_target="tpu_custom_call" | custom-call | flops 440401920 | bytes 2523136 | tf_op jit(solution)/shard_map/project/pallas_call | solution.py:300
  53.3 2.3 %collective-permute-done.12.refs_2_.refs_9_ = bf16[448,384]{1,0:T(8,128)(2,1)} collective-permute-done((bf16[448,384]{1,0:T(8,128)(2,1)}, bf16[448,384]{1,0:T(8,128)(2,1)}, u32[]{:S(2)}, u32[]{:S(2)}) %collective-permute-start.12) | collective-permute-done | bytes 344096 | tf_op jit(solution)/shard_map/ppermute | solution.py:192
  55.6 2.5 %collective-permute-start.13 = (bf16[448,384]{1,0:T(8,128)(2,1)}, bf16[448,384]{1,0:T(8,128)(2,1)}, u32[]{:S(2)}, u32[]{:S(2)}) collective-permute-start(bf16[448,384]{1,0:T(8,128)(2,1)} %collective-permute-done.12.refs_2_.refs_9_), channel_id=1, source_target_pairs={{0,2},{1,17},{2,0},{3,19},{16,18},{17,1},{18,16},{19,3},{4,6},{5,2... | collective-permute-start | bytes 1032200 | tf_op jit(solution)/shard_map/ppermute | solution.py:471
  58.1 1.7 constant_dynamic-slice_fusion
  59.8 1.8 copy.22
  62.2 2.0 %collective-permute-start.10 = (bf16[448,384]{1,0:T(8,128)(2,1)S(1)}, bf16[448,384]{1,0:T(8,128)(2,1)}, u32[]{:S(2)}, u32[]{:S(2)}) collective-permute-start(bf16[448,384]{1,0:T(8,128)(2,1)S(1)} %collective-permute-done.8.refs_3_.refs_6_), channel_id=1, source_target_pairs={{0,16},{1,3},{2,18},{3,1},{16,0},{17,19},{18,2},{19,17},{4,20},{5,... | collective-permute-start | bytes 1032200 | tf_op jit(solution)/shard_map/ppermute | solution.py:473
  64.3 5.4 %collective-permute-done.22.refs_2_ = bf16[896,128]{1,0:T(8,128)(2,1)} collective-permute-done((bf16[896,128]{1,0:T(8,128)(2,1)}, bf16[896,128]{1,0:T(8,128)(2,1)}, u32[]{:S(2)}, u32[]{:S(2)}) %collective-permute-start.22) | collective-permute-done | bytes 229408 | tf_op jit(solution)/shard_map/ppermute | solution.py:192
  71.2 2.0 %collective-permute-start.15 = (bf16[448,384]{1,0:T(8,128)(2,1)}, bf16[448,384]{1,0:T(8,128)(2,1)}, u32[]{:S(2)}, u32[]{:S(2)}) collective-permute-start(bf16[448,384]{1,0:T(8,128)(2,1)} %collective-permute-done.13.refs_3_.refs_10_), channel_id=1, source_target_pairs={{0,16},{1,3},{2,18},{3,1},{16,0},{17,19},{18,2},{19,17},{4,20},{5,... | collective-permute-start | bytes 1032200 | tf_op jit(solution)/shard_map/ppermute | solution.py:473
  73.2 1.5 add_convert_fusion.3
  74.7 1.9 %finish.4 = (f32[160,384]{1,0:T(8,128)}, bf16[160,128]{1,0:T(8,128)(2,1)}, bf16[160,256]{1,0:T(8,128)(2,1)}) custom-call(f32[160,384]{1,0:T(8,128)} %copy-done.11, f32[160,384]{1,0:T(8,128)} %collective-permute-done.1.come_ref, f32[2,128]{1,0:T(2,128)} %gain_ref.9), custom_call_target="tpu_custom_call" | custom-call | flops 1228800 | bytes 983040 | tf_op jit(solution)/shard_map/finish/pallas_call | solution.py:335
  76.6 1.9 %finish.5 = (f32[160,384]{1,0:T(8,128)}, bf16[160,128]{1,0:T(8,128)(2,1)}, bf16[160,256]{1,0:T(8,128)(2,1)}) custom-call(f32[160,384]{1,0:T(8,128)} %copy-done.12, f32[160,384]{1,0:T(8,128)} %collective-permute-done.6.come_ref, f32[2,128]{1,0:T(2,128)} %gain_ref.9), custom_call_target="tpu_custom_call" | custom-call | flops 1228800 | bytes 983040 | tf_op jit(solution)/shard_map/finish/pallas_call | solution.py:335
  78.5 1.7 collective-permute-start.26
  80.3 1.3 copy-done.6
  81.6 2.6 %project.10 = (f32[160,384]{1,0:T(8,128)S(1)}, f32[160,384]{1,0:T(8,128)S(1)}) custom-call(s32[4]{0:T(128)S(1)} %copy-done.17, bf16[320,1792]{1,0:T(8,128)(2,1)S(1)} %copy-done.6, bf16[448,384]{1,0:T(8,128)(2,1)} %collective-permute-done.7.refs_2_.refs_5_, bf16[448,384]{1,0:T(8,128)(2,1)S(1)} %collective-permute-done.8.refs_3_.refs_6_, ...), custom_call_target="tpu_custom_call" | custom-call | flops 440401920 | bytes 2523136 | tf_op jit(solution)/shard_map/project/pallas_call | solution.py:300
  85.0 2.7 %project.13 = (f32[160,128]{1,0:T(8,128)S(1)}, f32[160,128]{1,0:T(8,128)}) custom-call(s32[2]{0:T(128)S(1)} %pad_add_fusion.1.refs_0_, bf16[320,1792]{1,0:T(8,128)(2,1)S(1)} %copy-done.2, bf16[896,128]{1,0:T(8,128)(2,1)} %collective-permute-done.22.refs_2_, bf16[896,128]{1,0:T(8,128)(2,1)} %collective-permute-done.23.refs_3_), custom_call_target="tpu_custom_call" | custom-call | flops 146800640 | bytes 1605632 | tf_op jit(solution)/shard_map/project/pallas_call | solution.py:300
  90.8 2.2 %collective-permute-start.30 = (bf16[896,128]{1,0:T(8,128)(2,1)}, bf16[896,128]{1,0:T(8,128)(2,1)}, u32[]{:S(2)}, u32[]{:S(2)}) collective-permute-start(bf16[896,128]{1,0:T(8,128)(2,1)} %bitcast.9), channel_id=1, source_target_pairs={{0,8},{4,12},{8,0},{12,4},{1,9},{5,13},{9,1},{13,5},{2,10},{6,14},... | collective-permute-start | bytes 688136 | tf_op jit(solution)/shard_map/ppermute | solution.py:192
  93.0 1.8 finish.6
  95.7 1.3 copy-done.7
  97.0 2.6 %project.11 = (f32[160,384]{1,0:T(8,128)S(1)}, f32[160,384]{1,0:T(8,128)S(1)}) custom-call(s32[4]{0:T(128)S(1)} %copy-done.17, bf16[320,1792]{1,0:T(8,128)(2,1)S(1)} %copy-done.7, bf16[448,384]{1,0:T(8,128)(2,1)} %collective-permute-done.12.refs_2_.refs_9_, bf16[448,384]{1,0:T(8,128)(2,1)} %collective-permute-done.13.refs_3_.refs_10_, ...), custom_call_target="tpu_custom_call" | custom-call | flops 440401920 | bytes 2523136 | tf_op jit(solution)/shard_map/project/pallas_call | solution.py:300
  99.7 1.5 add_convert_fusion.2
  101.2 2.2 %collective-permute-start.18 = (bf16[160,128]{1,0:T(8,128)(2,1)}, bf16[160,128]{1,0:T(8,128)(2,1)}, u32[]{:S(2)}, u32[]{:S(2)}) collective-permute-start(bf16[160,128]{1,0:T(8,128)(2,1)} %get-tuple-element.59), channel_id=1, source_target_pairs={{0,4},{4,8},{8,12},{12,0},{1,5},{5,9},{9,13},{13,1},{2,6},{6,10},{... | collective-permute-start | bytes 122888 | tf_op jit(solution)/shard_map/ppermute | solution.py:192
  103.4 2.6 %project.14 = (f32[160,128]{1,0:T(8,128)S(1)}, f32[160,128]{1,0:T(8,128)}) custom-call(s32[2]{0:T(128)S(1)} %pad_add_fusion.1.refs_0_, bf16[320,1792]{1,0:T(8,128)(2,1)S(1)} %copy-done.3, bf16[896,128]{1,0:T(8,128)(2,1)} %collective-permute-done.26.refs_2_, bf16[896,128]{1,0:T(8,128)(2,1)S(1)} %collective-permute-done.27.refs_3_), custom_call_target="tpu_custom_call" | custom-call | flops 146800640 | bytes 1605632 | tf_op jit(solution)/shard_map/project/pallas_call | solution.py:300
  108.0 1.9 finish.7
  109.9 3.1 %collective-permute-start.36 = (bf16[160,256]{1,0:T(8,128)(2,1)}, bf16[160,256]{1,0:T(8,128)(2,1)S(1)}, u32[]{:S(2)}, u32[]{:S(2)}) collective-permute-start(bf16[160,256]{1,0:T(8,128)(2,1)} %get-tuple-element.75), channel_id=1, source_target_pairs={{0,8},{4,12},{8,0},{12,4},{1,9},{5,13},{9,1},{13,5},{2,10},{6,14},... | collective-permute-start | bytes 245768 | tf_op jit(solution)/shard_map/ppermute | solution.py:192
  113.9 1.2 copy-done.4
  115.2 2.1 %project.15 = (f32[160,128]{1,0:T(8,128)S(1)}, f32[160,128]{1,0:T(8,128)S(1)}) custom-call(s32[2]{0:T(128)S(1)} %pad_add_fusion.1.refs_0_, bf16[320,1792]{1,0:T(8,128)(2,1)S(1)} %copy-done.4, bf16[896,128]{1,0:T(8,128)(2,1)} %collective-permute-done.30.refs_2_, bf16[896,128]{1,0:T(8,128)(2,1)} %collective-permute-done.31.refs_3_), custom_call_target="tpu_custom_call" | custom-call | flops 146800640 | bytes 1605632 | tf_op jit(solution)/shard_map/project/pallas_call | solution.py:300
  117.3 1.3 collective-permute-start.19
  119.3 1.5 collective-permute-start.38
  121.4 1.6 collective-permute-start.29
  124.4 4.9 %collective-permute-done.38 = bf16[640,256]{1,0:T(8,128)(2,1)S(1)} collective-permute-done((bf16[640,256]{1,0:T(8,128)(2,1)}, bf16[640,256]{1,0:T(8,128)(2,1)S(1)}, u32[]{:S(2)}, u32[]{:S(2)}) %collective-permute-start.38) | collective-permute-done | bytes 327712 | tf_op jit(solution)/shard_map/ppermute | solution.py:527
  129.4 1.5 collective-permute-done.39
  131.1 9.1 %attention.1 = (f32[640,128]{1,0:T(8,128)S(1)}, f32[2560,128]{1,0:T(8,128)S(1)}, f32[2560,128]{1,0:T(8,128)S(1)}) custom-call(bf16[640,128]{1,0:T(8,128)(2,1)S(1)} %pad_maximum_fusion.3.q_ref, bf16[640,128]{1,0:T(8,128)(2,1)S(1)} %pad_maximum_fusion.4.g_ref, bf16[2560,128]{1,0:T(8,128)(2,1)S(1)} %get-tuple-element.87.k_ref, ...), custom_call_target="tpu_custom_call" | custom-call | flops 2097152000 | bytes 5242880 | tf_op jit(solution)/shard_map/attention/pallas_call | solution.py:252
  140.6 2.9 %collective-permute-done.43 = f32[2,640,256]{2,1,0:T(8,128)S(1)} collective-permute-done((f32[2,640,256]{2,1,0:T(8,128)S(1)}, f32[2,640,256]{2,1,0:T(8,128)S(1)}, u32[]{:S(2)}, u32[]{:S(2)}) %collective-permute-start.43) | collective-permute-done | bytes 1310752 | tf_op jit(solution)/shard_map/ppermute | solution.py:535
  143.7 1.6 collective-permute-start.44
  146.6 6.9 %collective-permute-done.44 = bf16[640,256]{1,0:T(8,128)(2,1)S(1)} collective-permute-done((bf16[640,256]{1,0:T(8,128)(2,1)S(1)}, bf16[640,256]{1,0:T(8,128)(2,1)S(1)}, u32[]{:S(2)}, u32[]{:S(2)}) %collective-permute-start.44) | collective-permute-done | bytes 327712 | tf_op jit(solution)/shard_map/ppermute | solution.py:536
  154.3 1.7 collective-permute-start.47
  158.0 2.9 %collective-permute-start.41 = (bf16[160,128]{1,0:T(8,128)(2,1)S(1)}, bf16[160,128]{1,0:T(8,128)(2,1)S(1)}, u32[]{:S(2)}, u32[]{:S(2)}) collective-permute-start(bf16[160,128]{1,0:T(8,128)(2,1)S(1)} %get-tuple-element.97), channel_id=1, source_target_pairs={{0,12},{4,0},{8,4},{12,8},{1,13},{5,1},{9,5},{13,9},{2,14},{6,2},{... | collective-permute-start | bytes 122888 | tf_op jit(solution)/shard_map/ppermute | solution.py:192
  160.9 3.1 %collective-permute-done.41.refs_6_ = bf16[160,128]{1,0:T(8,128)(2,1)S(1)} collective-permute-done((bf16[160,128]{1,0:T(8,128)(2,1)S(1)}, bf16[160,128]{1,0:T(8,128)(2,1)S(1)}, u32[]{:S(2)}, u32[]{:S(2)}) %collective-permute-start.41) | collective-permute-done | bytes 40992 | tf_op jit(solution)/shard_map/ppermute | solution.py:192
  163.9 2.7 %collective-permute-done.40.refs_5_ = bf16[160,128]{1,0:T(8,128)(2,1)S(1)} collective-permute-done((bf16[160,128]{1,0:T(8,128)(2,1)S(1)}, bf16[160,128]{1,0:T(8,128)(2,1)S(1)}, u32[]{:S(2)}, u32[]{:S(2)}) %collective-permute-start.40) | collective-permute-done | bytes 40992 | tf_op jit(solution)/shard_map/ppermute | solution.py:192
  167.3 3.0 %unfinish.1.mine = bf16[160,1536]{1,0:T(8,128)(2,1)} custom-call(f32[2,128]{1,0:T(2,128)} %gain_ref.9, f32[160,384]{1,0:T(8,128)} %get-tuple-element.45.refs_0_, f32[160,384]{1,0:T(8,128)} %get-tuple-element.48.refs_1_, f32[160,384]{1,0:T(8,128)} %get-tuple-element.52.refs_2_, f32[160,384]{1,0:T(8,128)} %get-tuple-element.56.refs_3_, ...), custom_call_target="tpu_custom_call" | custom-call | flops 4915200 | bytes 1966080 | tf_op jit(solution)/shard_map/unfinish/pallas_call | solution.py:374
  170.3 2.1 %collective-permute-done.48.theirs = bf16[160,1536]{1,0:T(8,128)(2,1)S(1)} collective-permute-done((bf16[160,1536]{1,0:T(8,128)(2,1)}, bf16[160,1536]{1,0:T(8,128)(2,1)S(1)}, u32[]{:S(2)}, u32[]{:S(2)}) %collective-permute-start.48) | collective-permute-done | bytes 491552 | tf_op jit(solution)/shard_map/ppermute | solution.py:542
  172.3 1.3 copy-done.9
  174.7 5.0 %back_project.1 = (f32[160,1792]{1,0:T(8,128)S(1)}, bf16[160,1792]{1,0:T(8,128)(2,1)S(1)}) custom-call(s32[4]{0:T(128)S(1)} %copy-done.17, bf16[160,1536]{1,0:T(8,128)(2,1)S(1)} %copy-done.10, bf16[160,1536]{1,0:T(8,128)(2,1)S(1)} %collective-permute-done.48.theirs, bf16[1792,384]{1,0:T(8,128)(2,1)S(1)} %copy-done.9, ...), custom_call_target="tpu_custom_call" | custom-call | flops 1761607680 | bytes 5505024 | tf_op jit(solution)/shard_map/back_project/pallas_call | solution.py:425
  179.9 1.8 collective-permute-done.49
  184.2 2.1 %convert_add_fusion = f32[160,3584]{1,0:T(8,128)} fusion(bf16[160,3584]{1,0:T(8,128)(2,1)S(1)} %copy-done.20, bf16[160,3584]{1,0:T(8,128)(2,1)S(1)} %copy-done.18, f32[160,1792]{1,0:T(8,128)S(1)} %get-tuple-element.85, f32[160,1792]{1,0:T(8,128)S(1)} %get-tuple-element.84, f32[160]{0:T(256)S(1)} %broadcast_multiply_fusion, f32[3584]{0:T(1024)S(1)} %copy-done.24, ...), kind=kLoop, calls=%fused_computation.5 | loop fusion | flops 5160960 | bytes 6896896 | tf_op jit(solution)/shard_map/add | solution.py:548
  (177 shorter events, 33.9 us)
Async XLA Ops:
  2.0 9.9 %copy-start.19 = (bf16[448,3,128]{0,2,1:T(8,128)(2,1)}, bf16[448,3,128]{0,2,1:T(8,128)(2,1)S(1)}, u32[]{:S(2)}) copy-start(bf16[448,3,128]{0,2,1:T(8,128)(2,1)S(1)} %copy.13) | copy-start | bytes 1032196
  2.9 13.7 %collective-permute-start.2 = (bf16[448,384]{1,0:T(8,128)(2,1)}, bf16[448,384]{1,0:T(8,128)(2,1)S(1)}, u32[]{:S(2)}, u32[]{:S(2)}) collective-permute-start(bf16[448,384]{1,0:T(8,128)(2,1)} %copy.14), channel_id=1, source_target_pairs={{0,4},{4,8},{8,12},{12,0},{1,5},{5,9},{9,13},{13,1},{2,6},{6,10},{... | collective-permute-start | bytes 1032200 | tf_op jit(solution)/shard_map/ppermute | solution.py:192
  11.9 19.2 %collective-permute-start.20 = (bf16[160,1792]{1,0:T(8,128)(2,1)}, bf16[160,1792]{1,0:T(8,128)(2,1)}, u32[]{:S(2)}, u32[]{:S(2)}) collective-permute-start(bf16[160,1792]{1,0:T(8,128)(2,1)} %get-tuple-element.89), channel_id=1, source_target_pairs={{0,1},{1,0},{2,3},{3,2},{4,5},{5,4},{6,7},{7,6},{8,9},{9,8},{10,11... | collective-permute-start | bytes 1720328 | tf_op jit(solution)/shard_map/ppermute | solution.py:498
  13.0 30.8 %collective-permute-start = (bf16[160,1792]{1,0:T(8,128)(2,1)}, bf16[160,1792]{1,0:T(8,128)(2,1)}, u32[]{:S(2)}, u32[]{:S(2)}) collective-permute-start(bf16[160,1792]{1,0:T(8,128)(2,1)} %get-tuple-element.91), channel_id=1, source_target_pairs={{0,1},{1,0},{2,3},{3,2},{4,5},{5,4},{6,7},{7,6},{8,9},{9,8},{10,11... | collective-permute-start | bytes 1720328 | tf_op jit(solution)/shard_map/ppermute | solution.py:498
  16.6 14.0 %collective-permute-start.3 = (bf16[448,384]{1,0:T(8,128)(2,1)S(1)}, bf16[448,384]{1,0:T(8,128)(2,1)}, u32[]{:S(2)}, u32[]{:S(2)}) collective-permute-start(bf16[448,384]{1,0:T(8,128)(2,1)S(1)} %collective-permute-done.2.refs_2_.refs_1_), channel_id=1, source_target_pairs={{0,2},{1,17},{2,0},{3,19},{16,18},{17,1},{18,16},{19,3},{4,6},{5,2... | collective-permute-start | bytes 1032200 | tf_op jit(solution)/shard_map/ppermute | solution.py:471
  26.3 10.0 %collective-permute-start.7 = (bf16[448,384]{1,0:T(8,128)(2,1)}, bf16[448,384]{1,0:T(8,128)(2,1)}, u32[]{:S(2)}, u32[]{:S(2)}) collective-permute-start(bf16[448,384]{1,0:T(8,128)(2,1)} %copy.15), channel_id=1, source_target_pairs={{0,12},{4,0},{8,4},{12,8},{1,13},{5,1},{9,5},{13,9},{2,14},{6,2},{... | collective-permute-start | bytes 1032200 | tf_op jit(solution)/shard_map/ppermute | solution.py:192
  29.1 19.6 %collective-permute-start.4 = (bf16[448,384]{1,0:T(8,128)(2,1)S(1)}, bf16[448,384]{1,0:T(8,128)(2,1)}, u32[]{:S(2)}, u32[]{:S(2)}) collective-permute-start(bf16[448,384]{1,0:T(8,128)(2,1)S(1)} %collective-permute-done.2.refs_2_.refs_1_), channel_id=1, source_target_pairs={{0,16},{1,3},{2,18},{3,1},{16,0},{17,19},{18,2},{19,17},{4,20},{5,... | collective-permute-start | bytes 1032200 | tf_op jit(solution)/shard_map/ppermute | solution.py:472
  30.6 18.1 %collective-permute-start.5 = (bf16[448,384]{1,0:T(8,128)(2,1)}, bf16[448,384]{1,0:T(8,128)(2,1)}, u32[]{:S(2)}, u32[]{:S(2)}) collective-permute-start(bf16[448,384]{1,0:T(8,128)(2,1)} %collective-permute-done.3.refs_3_.refs_2_), channel_id=1, source_target_pairs={{0,16},{1,3},{2,18},{3,1},{16,0},{17,19},{18,2},{19,17},{4,20},{5,... | collective-permute-start | bytes 1032200 | tf_op jit(solution)/shard_map/ppermute | solution.py:473
  38.2 17.4 %collective-permute-start.12 = (bf16[448,384]{1,0:T(8,128)(2,1)}, bf16[448,384]{1,0:T(8,128)(2,1)}, u32[]{:S(2)}, u32[]{:S(2)}) collective-permute-start(bf16[448,384]{1,0:T(8,128)(2,1)} %copy.16), channel_id=1, source_target_pairs={{0,8},{4,12},{8,0},{12,4},{1,9},{5,13},{9,1},{13,5},{2,10},{6,14},... | collective-permute-start | bytes 1032200 | tf_op jit(solution)/shard_map/ppermute | solution.py:192
  43.8 17.7 %collective-permute-start.21 = (f32[160,128]{1,0:T(8,128)}, f32[160,128]{1,0:T(8,128)}, u32[]{:S(2)}, u32[]{:S(2)}) collective-permute-start(f32[160,128]{1,0:T(8,128)} %get-tuple-element.62), channel_id=1, source_target_pairs={{0,1},{1,0},{2,3},{3,2},{4,5},{5,4},{6,7},{7,6},{8,9},{9,8},{10,11... | collective-permute-start | bytes 245768 | tf_op jit(solution)/shard_map/ppermute | solution.py:521
  43.8 18.4 %collective-permute-start.8 = (bf16[448,384]{1,0:T(8,128)(2,1)}, bf16[448,384]{1,0:T(8,128)(2,1)S(1)}, u32[]{:S(2)}, u32[]{:S(2)}) collective-permute-start(bf16[448,384]{1,0:T(8,128)(2,1)} %collective-permute-done.7.refs_2_.refs_5_), channel_id=1, source_target_pairs={{0,2},{1,17},{2,0},{3,19},{16,18},{17,1},{18,16},{19,3},{4,6},{5,2... | collective-permute-start | bytes 1032200 | tf_op jit(solution)/shard_map/ppermute | solution.py:471
  46.5 5.6 %copy-start.5 = (bf16[320,1792]{1,0:T(8,128)(2,1)}, bf16[320,1792]{1,0:T(8,128)(2,1)S(1)}, u32[]{:S(2)}) copy-start(bf16[320,1792]{1,0:T(8,128)(2,1)S(1)} %pad_maximum_fusion.1.refs_0_.refs_1_) | copy-start | bytes 3440644
  48.7 24.5 %copy-start.16 = (f32[160,128]{1,0:T(8,128)S(1)}, f32[160,128]{1,0:T(8,128)}, u32[]{:S(2)}) copy-start(f32[160,128]{1,0:T(8,128)} %copy-done.15) | copy-start | bytes 245764
  48.7 13.5 %collective-permute-start.1 = (f32[160,384]{1,0:T(8,128)}, f32[160,384]{1,0:T(8,128)}, u32[]{:S(2)}, u32[]{:S(2)}) collective-permute-start(f32[160,384]{1,0:T(8,128)} %get-tuple-element.44), channel_id=1, source_target_pairs={{0,1},{1,0},{2,3},{3,2},{4,5},{5,4},{6,7},{7,6},{8,9},{9,8},{10,11... | collective-permute-start | bytes 737288 | tf_op jit(solution)/shard_map/ppermute | solution.py:512
  52.8 17.6 %collective-permute-start.6 = (f32[160,384]{1,0:T(8,128)}, f32[160,384]{1,0:T(8,128)}, u32[]{:S(2)}, u32[]{:S(2)}) collective-permute-start(f32[160,384]{1,0:T(8,128)} %get-tuple-element.47), channel_id=1, source_target_pairs={{0,1},{1,0},{2,3},{3,2},{4,5},{5,4},{6,7},{7,6},{8,9},{9,8},{10,11... | collective-permute-start | bytes 737288 | tf_op jit(solution)/shard_map/ppermute | solution.py:512
  55.6 15.5 %collective-permute-start.13 = (bf16[448,384]{1,0:T(8,128)(2,1)}, bf16[448,384]{1,0:T(8,128)(2,1)}, u32[]{:S(2)}, u32[]{:S(2)}) collective-permute-start(bf16[448,384]{1,0:T(8,128)(2,1)} %collective-permute-done.12.refs_2_.refs_9_), channel_id=1, source_target_pairs={{0,2},{1,17},{2,0},{3,19},{16,18},{17,1},{18,16},{19,3},{4,6},{5,2... | collective-permute-start | bytes 1032200 | tf_op jit(solution)/shard_map/ppermute | solution.py:471
  61.6 8.1 %collective-permute-start.22 = (bf16[896,128]{1,0:T(8,128)(2,1)}, bf16[896,128]{1,0:T(8,128)(2,1)}, u32[]{:S(2)}, u32[]{:S(2)}) collective-permute-start(bf16[896,128]{1,0:T(8,128)(2,1)} %bitcast.9), channel_id=1, source_target_pairs={{0,4},{4,8},{8,12},{12,0},{1,5},{5,9},{9,13},{13,1},{2,6},{6,10},{... | collective-permute-start | bytes 688136 | tf_op jit(solution)/shard_map/ppermute | solution.py:192
  62.2 16.2 %collective-permute-start.9 = (bf16[448,384]{1,0:T(8,128)(2,1)}, bf16[448,384]{1,0:T(8,128)(2,1)}, u32[]{:S(2)}, u32[]{:S(2)}) collective-permute-start(bf16[448,384]{1,0:T(8,128)(2,1)} %collective-permute-done.7.refs_2_.refs_5_), channel_id=1, source_target_pairs={{0,16},{1,3},{2,18},{3,1},{16,0},{17,19},{18,2},{19,17},{4,20},{5,... | collective-permute-start | bytes 1032200 | tf_op jit(solution)/shard_map/ppermute | solution.py:472
  62.2 18.0 %collective-permute-start.10 = (bf16[448,384]{1,0:T(8,128)(2,1)S(1)}, bf16[448,384]{1,0:T(8,128)(2,1)}, u32[]{:S(2)}, u32[]{:S(2)}) collective-permute-start(bf16[448,384]{1,0:T(8,128)(2,1)S(1)} %collective-permute-done.8.refs_3_.refs_6_), channel_id=1, source_target_pairs={{0,16},{1,3},{2,18},{3,1},{16,0},{17,19},{18,2},{19,17},{4,20},{5,... | collective-permute-start | bytes 1032200 | tf_op jit(solution)/shard_map/ppermute | solution.py:473
  69.7 25.1 %collective-permute-start.14 = (bf16[448,384]{1,0:T(8,128)(2,1)}, bf16[448,384]{1,0:T(8,128)(2,1)}, u32[]{:S(2)}, u32[]{:S(2)}) collective-permute-start(bf16[448,384]{1,0:T(8,128)(2,1)} %collective-permute-done.12.refs_2_.refs_9_), channel_id=1, source_target_pairs={{0,16},{1,3},{2,18},{3,1},{16,0},{17,19},{18,2},{19,17},{4,20},{5,... | collective-permute-start | bytes 1032200 | tf_op jit(solution)/shard_map/ppermute | solution.py:472
  70.4 13.8 %collective-permute-start.23 = (bf16[896,128]{1,0:T(8,128)(2,1)}, bf16[896,128]{1,0:T(8,128)(2,1)}, u32[]{:S(2)}, u32[]{:S(2)}) collective-permute-start(bf16[896,128]{1,0:T(8,128)(2,1)} %collective-permute-done.22.refs_2_), channel_id=1, source_target_pairs={{0,2},{1,17},{2,0},{3,19},{16,18},{17,1},{18,16},{19,3},{4,6},{5,2... | collective-permute-start | bytes 688136 | tf_op jit(solution)/shard_map/ppermute | solution.py:485
  71.2 24.1 %collective-permute-start.15 = (bf16[448,384]{1,0:T(8,128)(2,1)}, bf16[448,384]{1,0:T(8,128)(2,1)}, u32[]{:S(2)}, u32[]{:S(2)}) collective-permute-start(bf16[448,384]{1,0:T(8,128)(2,1)} %collective-permute-done.13.refs_3_.refs_10_), channel_id=1, source_target_pairs={{0,16},{1,3},{2,18},{3,1},{16,0},{17,19},{18,2},{19,17},{4,20},{5,... | collective-permute-start | bytes 1032200 | tf_op jit(solution)/shard_map/ppermute | solution.py:473
  76.6 7.7 %copy-start.29 = (bf16[160,256]{1,0:T(8,128)(2,1)S(1)}, bf16[160,256]{1,0:T(8,128)(2,1)}, u32[]{:S(2)}) copy-start(bf16[160,256]{1,0:T(8,128)(2,1)} %get-tuple-element.72) | copy-start | bytes 245764
  78.5 10.4 %collective-permute-start.26 = (bf16[896,128]{1,0:T(8,128)(2,1)}, bf16[896,128]{1,0:T(8,128)(2,1)}, u32[]{:S(2)}, u32[]{:S(2)}) collective-permute-start(bf16[896,128]{1,0:T(8,128)(2,1)} %bitcast.9), channel_id=1, source_target_pairs={{0,12},{4,0},{8,4},{12,8},{1,13},{5,1},{9,5},{13,9},{2,14},{6,2},{... | collective-permute-start | bytes 688136 | tf_op jit(solution)/shard_map/ppermute | solution.py:192
  80.2 4.7 %copy-start.2 = (bf16[320,1792]{1,0:T(8,128)(2,1)S(1)}, bf16[320,1792]{1,0:T(8,128)(2,1)}, u32[]{:S(2)}) copy-start(bf16[320,1792]{1,0:T(8,128)(2,1)} %pad_maximum_fusion.2.refs_0_.refs_1_) | copy-start | bytes 3440644
  80.2 7.5 %collective-permute-start.34 = (bf16[160,256]{1,0:T(8,128)(2,1)}, bf16[160,256]{1,0:T(8,128)(2,1)S(1)}, u32[]{:S(2)}, u32[]{:S(2)}) collective-permute-start(bf16[160,256]{1,0:T(8,128)(2,1)} %get-tuple-element.73), channel_id=1, source_target_pairs={{0,12},{4,0},{8,4},{12,8},{1,13},{5,1},{9,5},{13,9},{2,14},{6,2},{... | collective-permute-start | bytes 245768 | tf_op jit(solution)/shard_map/ppermute | solution.py:192
  84.2 5.8 %collective-permute-start.11 = (f32[160,384]{1,0:T(8,128)S(1)}, f32[160,384]{1,0:T(8,128)S(1)}, u32[]{:S(2)}, u32[]{:S(2)}) collective-permute-start(f32[160,384]{1,0:T(8,128)S(1)} %get-tuple-element.51), channel_id=1, source_target_pairs={{0,1},{1,0},{2,3},{3,2},{4,5},{5,4},{6,7},{7,6},{8,9},{9,8},{10,11... | collective-permute-start | bytes 737288 | tf_op jit(solution)/shard_map/ppermute | solution.py:512
  87.7 11.9 %collective-permute-start.24 = (f32[160,128]{1,0:T(8,128)}, f32[160,128]{1,0:T(8,128)}, u32[]{:S(2)}, u32[]{:S(2)}) collective-permute-start(f32[160,128]{1,0:T(8,128)} %get-tuple-element.65), channel_id=1, source_target_pairs={{0,1},{1,0},{2,3},{3,2},{4,5},{5,4},{6,7},{7,6},{8,9},{9,8},{10,11... | collective-permute-start | bytes 245768 | tf_op jit(solution)/shard_map/ppermute | solution.py:521
  88.9 4.1 %copy-start.35 = (bf16[640,256]{1,0:T(8,128)(2,1)}, bf16[640,256]{1,0:T(8,128)(2,1)S(1)}, u32[]{:S(2)}) copy-start(bf16[640,256]{1,0:T(8,128)(2,1)S(1)} %get-tuple-element.104) | copy-start | bytes 983044
  88.9 32.0 %collective-permute-start.17 = (bf16[160,128]{1,0:T(8,128)(2,1)}, bf16[160,128]{1,0:T(8,128)(2,1)}, u32[]{:S(2)}, u32[]{:S(2)}) collective-permute-start(bf16[160,128]{1,0:T(8,128)(2,1)} %get-tuple-element.58), channel_id=1, source_target_pairs={{0,12},{4,0},{8,4},{12,8},{1,13},{5,1},{9,5},{13,9},{2,14},{6,2},{... | collective-permute-start | bytes 122888 | tf_op jit(solution)/shard_map/ppermute | solution.py:192
  90.8 16.2 %collective-permute-start.30 = (bf16[896,128]{1,0:T(8,128)(2,1)}, bf16[896,128]{1,0:T(8,128)(2,1)}, u32[]{:S(2)}, u32[]{:S(2)}) collective-permute-start(bf16[896,128]{1,0:T(8,128)(2,1)} %bitcast.9), channel_id=1, source_target_pairs={{0,8},{4,12},{8,0},{12,4},{1,9},{5,13},{9,1},{13,5},{2,10},{6,14},... | collective-permute-start | bytes 688136 | tf_op jit(solution)/shard_map/ppermute | solution.py:192
  94.8 6.4 %collective-permute-start.27 = (bf16[896,128]{1,0:T(8,128)(2,1)}, bf16[896,128]{1,0:T(8,128)(2,1)S(1)}, u32[]{:S(2)}, u32[]{:S(2)}) collective-permute-start(bf16[896,128]{1,0:T(8,128)(2,1)} %collective-permute-done.26.refs_2_), channel_id=1, source_target_pairs={{0,2},{1,17},{2,0},{3,19},{16,18},{17,1},{18,16},{19,3},{4,6},{5,2... | collective-permute-start | bytes 688136 | tf_op jit(solution)/shard_map/ppermute | solution.py:485
  95.3 8.1 %copy-start.3 = (bf16[320,1792]{1,0:T(8,128)(2,1)S(1)}, bf16[320,1792]{1,0:T(8,128)(2,1)}, u32[]{:S(2)}) copy-start(bf16[320,1792]{1,0:T(8,128)(2,1)} %pad_maximum_fusion.2.refs_0_.refs_1_) | copy-start | bytes 3440644
  95.3 10.7 %collective-permute-start.35 = (bf16[160,256]{1,0:T(8,128)(2,1)}, bf16[160,256]{1,0:T(8,128)(2,1)S(1)}, u32[]{:S(2)}, u32[]{:S(2)}) collective-permute-start(bf16[160,256]{1,0:T(8,128)(2,1)} %get-tuple-element.74), channel_id=1, source_target_pairs={{0,4},{4,8},{8,12},{12,0},{1,5},{5,9},{9,13},{13,1},{2,6},{6,10},{... | collective-permute-start | bytes 245768 | tf_op jit(solution)/shard_map/ppermute | solution.py:192
  99.6 6.4 %copy-start.13 = (f32[160,384]{1,0:T(8,128)}, f32[160,384]{1,0:T(8,128)S(1)}, u32[]{:S(2)}) copy-start(f32[160,384]{1,0:T(8,128)S(1)} %get-tuple-element.54.own_ref) | copy-start | bytes 737284
  99.6 7.7 %collective-permute-start.16 = (f32[160,384]{1,0:T(8,128)S(1)}, f32[160,384]{1,0:T(8,128)S(1)}, u32[]{:S(2)}, u32[]{:S(2)}) collective-permute-start(f32[160,384]{1,0:T(8,128)S(1)} %get-tuple-element.55), channel_id=1, source_target_pairs={{0,1},{1,0},{2,3},{3,2},{4,5},{5,4},{6,7},{7,6},{8,9},{9,8},{10,11... | collective-permute-start | bytes 737288 | tf_op jit(solution)/shard_map/ppermute | solution.py:512
  101.2 20.2 %collective-permute-start.18 = (bf16[160,128]{1,0:T(8,128)(2,1)}, bf16[160,128]{1,0:T(8,128)(2,1)}, u32[]{:S(2)}, u32[]{:S(2)}) collective-permute-start(bf16[160,128]{1,0:T(8,128)(2,1)} %get-tuple-element.59), channel_id=1, source_target_pairs={{0,4},{4,8},{8,12},{12,0},{1,5},{5,9},{9,13},{13,1},{2,6},{6,10},{... | collective-permute-start | bytes 122888 | tf_op jit(solution)/shard_map/ppermute | solution.py:192
  106.0 7.0 %collective-permute-start.28 = (f32[160,128]{1,0:T(8,128)}, f32[160,128]{1,0:T(8,128)}, u32[]{:S(2)}, u32[]{:S(2)}) collective-permute-start(f32[160,128]{1,0:T(8,128)} %get-tuple-element.68), channel_id=1, source_target_pairs={{0,1},{1,0},{2,3},{3,2},{4,5},{5,4},{6,7},{7,6},{8,9},{9,8},{10,11... | collective-permute-start | bytes 245768 | tf_op jit(solution)/shard_map/ppermute | solution.py:521
  107.0 6.9 %collective-permute-start.31 = (bf16[896,128]{1,0:T(8,128)(2,1)}, bf16[896,128]{1,0:T(8,128)(2,1)}, u32[]{:S(2)}, u32[]{:S(2)}) collective-permute-start(bf16[896,128]{1,0:T(8,128)(2,1)} %collective-permute-done.30.refs_2_), channel_id=1, source_target_pairs={{0,2},{1,17},{2,0},{3,19},{16,18},{17,1},{18,16},{19,3},{4,6},{5,2... | collective-permute-start | bytes 688136 | tf_op jit(solution)/shard_map/ppermute | solution.py:485
  109.8 7.5 %copy-start.38 = (bf16[160,128]{1,0:T(8,128)(2,1)S(1)}, bf16[160,128]{1,0:T(8,128)(2,1)}, u32[]{:S(2)}) copy-start(bf16[160,128]{1,0:T(8,128)(2,1)} %get-tuple-element.60) | copy-start | bytes 122884
  109.8 11.0 %copy-start.31 = (bf16[160,128]{1,0:T(8,128)(2,1)S(1)}, bf16[160,128]{1,0:T(8,128)(2,1)}, u32[]{:S(2)}) copy-start(bf16[160,128]{1,0:T(8,128)(2,1)} %add_convert_fusion.2) | copy-start | bytes 122884
  109.8 13.8 %copy-start.30 = (bf16[160,128]{1,0:T(8,128)(2,1)S(1)}, bf16[160,128]{1,0:T(8,128)(2,1)}, u32[]{:S(2)}) copy-start(bf16[160,128]{1,0:T(8,128)(2,1)} %get-tuple-element.57) | copy-start | bytes 122884
  109.8 19.5 %copy-start.27 = (bf16[160,128]{1,0:T(8,128)(2,1)S(1)}, bf16[160,128]{1,0:T(8,128)(2,1)}, u32[]{:S(2)}) copy-start(bf16[160,128]{1,0:T(8,128)(2,1)} %add_convert_fusion.3) | copy-start | bytes 122884
  109.9 8.8 %collective-permute-start.36 = (bf16[160,256]{1,0:T(8,128)(2,1)}, bf16[160,256]{1,0:T(8,128)(2,1)S(1)}, u32[]{:S(2)}, u32[]{:S(2)}) collective-permute-start(bf16[160,256]{1,0:T(8,128)(2,1)} %get-tuple-element.75), channel_id=1, source_target_pairs={{0,8},{4,12},{8,0},{12,4},{1,9},{5,13},{9,1},{13,5},{2,10},{6,14},... | collective-permute-start | bytes 245768 | tf_op jit(solution)/shard_map/ppermute | solution.py:192
  115.2 3.5 %copy-start.22 = (bf16[2560,256]{1,0:T(8,128)(2,1)S(1)}, bf16[2560,256]{1,0:T(8,128)(2,1)}, u32[]{:S(2)}) copy-start(bf16[2560,256]{1,0:T(8,128)(2,1)} %get-tuple-element.103) | copy-start | bytes 3932164
  117.3 3.6 %collective-permute-start.32 = (f32[160,128]{1,0:T(8,128)S(1)}, f32[160,128]{1,0:T(8,128)S(1)}, u32[]{:S(2)}, u32[]{:S(2)}) collective-permute-start(f32[160,128]{1,0:T(8,128)S(1)} %get-tuple-element.71), channel_id=1, source_target_pairs={{0,1},{1,0},{2,3},{3,2},{4,5},{5,4},{6,7},{7,6},{8,9},{9,8},{10,11... | collective-permute-start | bytes 245768 | tf_op jit(solution)/shard_map/ppermute | solution.py:521
  117.3 5.6 %collective-permute-start.19 = (bf16[160,128]{1,0:T(8,128)(2,1)S(1)}, bf16[160,128]{1,0:T(8,128)(2,1)S(1)}, u32[]{:S(2)}, u32[]{:S(2)}) collective-permute-start(bf16[160,128]{1,0:T(8,128)(2,1)S(1)} %copy-done.38), channel_id=1, source_target_pairs={{0,8},{4,12},{8,0},{12,4},{1,9},{5,13},{9,1},{13,5},{2,10},{6,14},... | collective-permute-start | bytes 122888 | tf_op jit(solution)/shard_map/ppermute | solution.py:192
  119.3 10.0 %collective-permute-start.38 = (bf16[640,256]{1,0:T(8,128)(2,1)}, bf16[640,256]{1,0:T(8,128)(2,1)S(1)}, u32[]{:S(2)}, u32[]{:S(2)}) collective-permute-start(bf16[640,256]{1,0:T(8,128)(2,1)} %get-tuple-element.100), channel_id=1, source_target_pairs={{0,2},{2,0},{1,3},{3,1},{4,6},{6,4},{5,7},{7,5},{8,10},{10,8},{9,1... | collective-permute-start | bytes 983048 | tf_op jit(solution)/shard_map/ppermute | solution.py:527
  120.8 8.5 %collective-permute-start.37 = (bf16[640,256]{1,0:T(8,128)(2,1)}, bf16[640,256]{1,0:T(8,128)(2,1)S(1)}, u32[]{:S(2)}, u32[]{:S(2)}) collective-permute-start(bf16[640,256]{1,0:T(8,128)(2,1)} %get-tuple-element.100), channel_id=1, source_target_pairs={{0,1},{1,0},{2,3},{3,2},{4,5},{5,4},{6,7},{7,6},{8,9},{9,8},{10,11... | collective-permute-start | bytes 983048 | tf_op jit(solution)/shard_map/ppermute | solution.py:529
  120.9 8.4 %collective-permute-start.25 = (bf16[160,128]{1,0:T(8,128)(2,1)S(1)}, bf16[160,128]{1,0:T(8,128)(2,1)S(1)}, u32[]{:S(2)}, u32[]{:S(2)}) collective-permute-start(bf16[160,128]{1,0:T(8,128)(2,1)S(1)} %copy-done.31), channel_id=1, source_target_pairs={{0,12},{4,0},{8,4},{12,8},{1,13},{5,1},{9,5},{13,9},{2,14},{6,2},{... | collective-permute-start | bytes 122888 | tf_op jit(solution)/shard_map/ppermute | solution.py:192
  121.4 7.9 %collective-permute-start.29 = (bf16[160,128]{1,0:T(8,128)(2,1)S(1)}, bf16[160,128]{1,0:T(8,128)(2,1)S(1)}, u32[]{:S(2)}, u32[]{:S(2)}) collective-permute-start(bf16[160,128]{1,0:T(8,128)(2,1)S(1)} %add_convert_fusion.1), channel_id=1, source_target_pairs={{0,4},{4,8},{8,12},{12,0},{1,5},{5,9},{9,13},{13,1},{2,6},{6,10},{... | collective-permute-start | bytes 122888 | tf_op jit(solution)/shard_map/ppermute | solution.py:192
  123.0 6.3 %collective-permute-start.33 = (bf16[160,128]{1,0:T(8,128)(2,1)S(1)}, bf16[160,128]{1,0:T(8,128)(2,1)S(1)}, u32[]{:S(2)}, u32[]{:S(2)}) collective-permute-start(bf16[160,128]{1,0:T(8,128)(2,1)S(1)} %add_convert_fusion), channel_id=1, source_target_pairs={{0,8},{4,12},{8,0},{12,4},{1,9},{5,13},{9,1},{13,5},{2,10},{6,14},... | collective-permute-start | bytes 122888 | tf_op jit(solution)/shard_map/ppermute | solution.py:192
  129.3 1.6 collective-permute-start.39
  140.4 3.1 %collective-permute-start.43 = (f32[2,640,256]{2,1,0:T(8,128)S(1)}, f32[2,640,256]{2,1,0:T(8,128)S(1)}, u32[]{:S(2)}, u32[]{:S(2)}) collective-permute-start(f32[2,640,256]{2,1,0:T(8,128)S(1)} %slice.70), channel_id=1, source_target_pairs={{0,1},{1,0},{2,3},{3,2},{4,5},{5,4},{6,7},{7,6},{8,9},{9,8},{10,11... | collective-permute-start | bytes 3932168 | tf_op jit(solution)/shard_map/ppermute | solution.py:535
  143.7 9.8 %collective-permute-start.44 = (bf16[640,256]{1,0:T(8,128)(2,1)S(1)}, bf16[640,256]{1,0:T(8,128)(2,1)S(1)}, u32[]{:S(2)}, u32[]{:S(2)}) collective-permute-start(bf16[640,256]{1,0:T(8,128)(2,1)S(1)} %fusion.12), channel_id=1, source_target_pairs={{0,2},{2,0},{1,3},{3,1},{4,6},{6,4},{5,7},{7,5},{8,10},{10,8},{9,1... | collective-permute-start | bytes 983048 | tf_op jit(solution)/shard_map/ppermute | solution.py:536
  146.0 14.9 %collective-permute-start.42 = (bf16[160,128]{1,0:T(8,128)(2,1)S(1)}, bf16[160,128]{1,0:T(8,128)(2,1)S(1)}, u32[]{:S(2)}, u32[]{:S(2)}) collective-permute-start(bf16[160,128]{1,0:T(8,128)(2,1)S(1)} %get-tuple-element.96), channel_id=1, source_target_pairs={{0,8},{4,12},{8,0},{12,4},{1,9},{5,13},{9,1},{13,5},{2,10},{6,14},... | collective-permute-start | bytes 122888 | tf_op jit(solution)/shard_map/ppermute | solution.py:192
  154.3 12.4 %collective-permute-start.47 = (bf16[160,256]{1,0:T(8,128)(2,1)S(1)}, bf16[160,256]{1,0:T(8,128)(2,1)S(1)}, u32[]{:S(2)}, u32[]{:S(2)}) collective-permute-start(bf16[160,256]{1,0:T(8,128)(2,1)S(1)} %get-tuple-element.92), channel_id=1, source_target_pairs={{0,8},{4,12},{8,0},{12,4},{1,9},{5,13},{9,1},{13,5},{2,10},{6,14},... | collective-permute-start | bytes 245768 | tf_op jit(solution)/shard_map/ppermute | solution.py:192
  156.0 10.7 %collective-permute-start.46 = (bf16[160,256]{1,0:T(8,128)(2,1)S(1)}, bf16[160,256]{1,0:T(8,128)(2,1)}, u32[]{:S(2)}, u32[]{:S(2)}) collective-permute-start(bf16[160,256]{1,0:T(8,128)(2,1)S(1)} %get-tuple-element.93), channel_id=1, source_target_pairs={{0,12},{4,0},{8,4},{12,8},{1,13},{5,1},{9,5},{13,9},{2,14},{6,2},{... | collective-permute-start | bytes 245768 | tf_op jit(solution)/shard_map/ppermute | solution.py:192
  157.0 9.6 %collective-permute-start.45 = (bf16[160,256]{1,0:T(8,128)(2,1)S(1)}, bf16[160,256]{1,0:T(8,128)(2,1)}, u32[]{:S(2)}, u32[]{:S(2)}) collective-permute-start(bf16[160,256]{1,0:T(8,128)(2,1)S(1)} %get-tuple-element.94), channel_id=1, source_target_pairs={{0,4},{4,8},{8,12},{12,0},{1,5},{5,9},{9,13},{13,1},{2,6},{6,10},{... | collective-permute-start | bytes 245768 | tf_op jit(solution)/shard_map/ppermute | solution.py:192
  158.0 5.9 %collective-permute-start.41 = (bf16[160,128]{1,0:T(8,128)(2,1)S(1)}, bf16[160,128]{1,0:T(8,128)(2,1)S(1)}, u32[]{:S(2)}, u32[]{:S(2)}) collective-permute-start(bf16[160,128]{1,0:T(8,128)(2,1)S(1)} %get-tuple-element.97), channel_id=1, source_target_pairs={{0,12},{4,0},{8,4},{12,8},{1,13},{5,1},{9,5},{13,9},{2,14},{6,2},{... | collective-permute-start | bytes 122888 | tf_op jit(solution)/shard_map/ppermute | solution.py:192
  160.9 5.8 %copy-start.32 = (bf16[160,128]{1,0:T(8,128)(2,1)}, bf16[160,128]{1,0:T(8,128)(2,1)S(1)}, u32[]{:S(2)}) copy-start(bf16[160,128]{1,0:T(8,128)(2,1)S(1)} %collective-permute-done.42.refs_7_) | copy-start | bytes 122884
  160.9 5.8 %collective-permute-start.40 = (bf16[160,128]{1,0:T(8,128)(2,1)S(1)}, bf16[160,128]{1,0:T(8,128)(2,1)S(1)}, u32[]{:S(2)}, u32[]{:S(2)}) collective-permute-start(bf16[160,128]{1,0:T(8,128)(2,1)S(1)} %get-tuple-element.98), channel_id=1, source_target_pairs={{0,4},{4,8},{8,12},{12,0},{1,5},{5,9},{9,13},{13,1},{2,6},{6,10},{... | collective-permute-start | bytes 122888 | tf_op jit(solution)/shard_map/ppermute | solution.py:192
  170.3 2.1 %collective-permute-start.48 = (bf16[160,1536]{1,0:T(8,128)(2,1)}, bf16[160,1536]{1,0:T(8,128)(2,1)S(1)}, u32[]{:S(2)}, u32[]{:S(2)}) collective-permute-start(bf16[160,1536]{1,0:T(8,128)(2,1)} %unfinish.1.mine), channel_id=1, source_target_pairs={{0,1},{1,0},{2,3},{3,2},{4,5},{5,4},{6,7},{7,6},{8,9},{9,8},{10,11... | collective-permute-start | bytes 1474568 | tf_op jit(solution)/shard_map/ppermute | solution.py:542
  179.7 2.0 %collective-permute-start.49 = (bf16[160,1792]{1,0:T(8,128)(2,1)S(1)}, bf16[160,1792]{1,0:T(8,128)(2,1)S(1)}, u32[]{:S(2)}, u32[]{:S(2)}) collective-permute-start(bf16[160,1792]{1,0:T(8,128)(2,1)S(1)} %get-tuple-element.80), channel_id=1, source_target_pairs={{0,1},{1,0},{2,3},{3,2},{4,5},{5,4},{6,7},{7,6},{8,9},{9,8},{10,11... | collective-permute-start | bytes 1720328 | tf_op jit(solution)/shard_map/ppermute | solution.py:544
  (25 other events, 39.0 us)

commit v3 on v0

--- a/solution.py
+++ b/solution.py
@@ -1,8 +1,11 @@
 import math
+from functools import partial
 
 import jax
 import jax.numpy as jnp
 from jax import lax
+from jax.experimental import pallas as pl
+from jax.experimental.pallas import tpu as pltpu
 from jax.sharding import PartitionSpec as P
 
 
@@ -18,7 +21,7 @@
     )
 
 
-def body(tokens, cotangent, modulation, w_qkv, w_out, qk_gain):
+def token_gather_body(tokens, cotangent, modulation, w_qkv, w_out, qk_gain):
     head_dim = qk_gain.shape[1]
     width = w_out.shape[0]
     nheads = width // head_dim
@@ -170,6 +173,466 @@
     return final_output
 
 
+CORE_SWAP = [(0, 1), (1, 0), (2, 3), (3, 2)]
+CHIP_SWAP = [(0, 2), (2, 0), (1, 3), (3, 1)]
+PLANE = ("group", "seq")
+
+
+def plane_swap(first):
+    pairs = []
+    for group in range(2):
+        for seq in range(4):
+            along_chip = (seq % 2 == 0) == first
+            to = group * 4 + (seq ^ 2) if along_chip else (1 - group) * 4 + seq
+            pairs.append((group * 4 + seq, to))
+    return pairs
+
+
+def around(value, step, count):
+    return lax.ppermute(value, "tensor", [(i, (i + step) % count) for i in range(count)])
+
+
+def place():
+    seq = lax.axis_index("seq")
+    core, chip, group = seq & 1, seq >> 1, lax.axis_index("group")
+    return core, chip, group, 2 * group + chip
+
+
+def arrivals():
+    core, chip, group, mine = place()
+    across = 2 * group + (1 - chip)
+    over = 2 * (1 - group) + chip
+    return mine, jnp.where(core == 0, across, over), jnp.where(core == 0, over, across), 3 - mine
+
+
+def call(kernel, name, out, operands, megabytes, flops=0, touched=0, roots=0, far=(), scratch=()):
+    vmem = pl.BlockSpec(memory_space=pltpu.VMEM)
+    anywhere = pl.BlockSpec(memory_space=pl.ANY)
+    out = tuple(jax.ShapeDtypeStruct(shape, dtype) for shape, dtype in out)
+    return pl.pallas_call(
+        kernel,
+        out_shape=out,
+        in_specs=[anywhere if i in far else vmem for i in range(len(operands))],
+        out_specs=(vmem,) * len(out),
+        scratch_shapes=list(scratch),
+        compiler_params=pltpu.CompilerParams(vmem_limit_bytes=megabytes and megabytes * 1024 * 1024),
+        cost_estimate=pl.CostEstimate(flops=0, bytes_accessed=0, transcendentals=0),
+        name=name,
+    )(*operands)
+
+
+BF16, F32 = jnp.bfloat16, jnp.float32
+NT = (((1,), (1,)), ((), ()))
+TN = (((0,), (0,)), ((), ()))
+
+
+def pack_kernel(w_in, w_out, early, late, quarter, sems):
+    core, _, _, mine = place()
+    part, dim = early.shape[1:]
+    half, tile = 4 * part, dim // 4
+    rows = pl.ds(pl.multiple_of(core * half + mine * part, tile), part)
+    targets = (early.at[0], early.at[1], late.at[0])
+    copies = [pltpu.make_async_copy(w_in.at[j, rows, :], to, sems.at[j]) for j, to in enumerate(targets)]
+    lanes = pl.ds(pl.multiple_of(core * half, dim), half)
+    heads = pl.ds(pl.multiple_of(mine * tile, tile), tile)
+    copies.append(pltpu.make_async_copy(w_out.at[heads, lanes], quarter, sems.at[3]))
+    for copy in copies:
+        copy.start()
+    for copy in copies:
+        copy.wait()
+    for i in range(part // tile):
+        late[1, i * tile : (i + 1) * tile, :] = quarter[:, i * dim : (i + 1) * dim]
+
+
+def pack(w_in, w_out):
+    _, width, dim = w_in.shape
+    part = width // 8
+    return call(
+        pack_kernel,
+        "pack",
+        [((2, part, dim), BF16)] * 2,
+        (w_in, w_out),
+        None,
+        touched=16 * part * dim,
+        far=(0, 1),
+        scratch=[pltpu.VMEM((dim // 4, 4 * part), BF16), pltpu.SemaphoreType.DMA((4,))],
+    )
+
+
+def front_kernel(x_ref, c_ref, mod_ref, keep_ref, send_ref, inv_ref):
+    half = keep_ref.shape[1] // 2
+    core = place()[0]
+    x = x_ref[...].astype(F32)
+    inv = lax.rsqrt(jnp.mean(x * x, axis=-1, keepdims=True) + 1e-06)
+    inv_ref[...] = inv
+    for i in range(2):
+        at = pl.ds(i * half, half)
+        xhat = x_ref[:, at].astype(F32) * inv
+        normed = (xhat * (1.0 + mod_ref[1:2, at]) + mod_ref[0:1, at]).astype(BF16)
+        scaled = (c_ref[:, at].astype(F32) * mod_ref[2:3, at]).astype(BF16)
+
+        @pl.when(core == i)
+        def _():
+            keep_ref[:, :half] = normed
+            keep_ref[:, half:] = scaled
+
+        @pl.when(core != i)
+        def _():
+            send_ref[:, :half] = normed
+            send_ref[:, half:] = scaled
+
+
+def front(tokens, cotangent, modulation):
+    size = tokens.size
+    return call(
+        front_kernel,
+        "front",
+        [(tokens.shape, BF16), (tokens.shape, BF16), ((tokens.shape[0], 1), F32)],
+        (tokens, cotangent, modulation),
+        12,
+        flops=20 * size,
+        touched=8 * size,
+    )
+
+
+def project_kernel(first, keep_ref, come_ref, *refs):
+    rows, half = keep_ref.shape[0], keep_ref.shape[1] // 2
+    if first:
+        w_in, w_out, own_ref, away_ref, whole, whole_out, sems = refs
+        dim = w_in.shape[2]
+        at = pl.ds(pl.multiple_of(place()[0] * half, dim), half)
+        copies = [
+            pltpu.make_async_copy(w_in.at[j, at, :], whole.at[:, j * dim : (j + 1) * dim], sems.at[j])
+            for j in range(3)
+        ]
+        copies.append(pltpu.make_async_copy(w_out.at[:, at], whole_out, sems.at[3]))
+        for copy in copies:
+            copy.start()
+        for copy in copies:
+            copy.wait()
+    else:
+        *blocks, own_ref, away_ref, whole, whole_out = refs
+        dim = whole_out.shape[0]
+        tile = dim // 4
+        for early, late, at in zip(blocks[:4], blocks[4:], arrivals()):
+            part = early.shape[1]
+            to = pl.ds(pl.multiple_of(at * part, tile), part)
+            for j, block in enumerate((early[0], early[1], late[0])):
+                whole[to, j * dim : (j + 1) * dim] = block
+            to = pl.ds(pl.multiple_of(at * tile, tile), tile)
+            for t in range(part // tile):
+                whole_out[to, t * dim : (t + 1) * dim] = late[1, t * tile : (t + 1) * tile, :]
+    x = jnp.concatenate([keep_ref[...], come_ref[...]], axis=0)
+    qkv = jnp.dot(x[:, :half], whole[...], preferred_element_type=F32)
+    grad = lax.dot_general(x[:, half:], whole_out[...], NT, preferred_element_type=F32)
+    own_ref[:, : 3 * dim] = qkv[:rows]
+    own_ref[:, 3 * dim :] = grad[:rows]
+    away_ref[:, : 3 * dim] = qkv[rows:]
+    away_ref[:, 3 * dim :] = grad[rows:]
+
+
+def project(keep, come, blocks, weights=()):
+    rows, half = keep.shape[0], keep.shape[1] // 2
+    first = len(weights) == 2
+    dim = weights[0].shape[2] if first else blocks[0][0].shape[2]
+    sums = ((rows, 4 * dim), F32)
+    return call(
+        partial(project_kernel, first),
+        "project",
+        [sums, sums, ((half, 3 * dim), BF16)],
+        (keep, come, *weights, *[block for eight in blocks for block in eight]),
+        12,
+        flops=16 * rows * half * dim,
+        touched=8 * half * (dim + rows),
+        far=(2, 3) if first else (),
+        scratch=[pltpu.VMEM((dim, half), BF16)] + [pltpu.SemaphoreType.DMA((4,))] * first,
+    )
+
+
+def unit(raw):
+    back = lax.rsqrt(jnp.mean(raw * raw, axis=-1, keepdims=True) + 1e-06)
+    return raw * back, back
+
+
+def finish_kernel(slots, own_ref, come_ref, gain_ref, raw_ref, *refs):
+    dim = gain_ref.shape[1]
+    for i in range(slots):
+        at = 4 * dim * i
+        raw = own_ref[:, at : at + 4 * dim] + come_ref[:, at : at + 4 * dim]
+        raw_ref[:, 2 * dim * i : 2 * dim * (i + 1)] = raw[:, : 2 * dim]
+        qh, _ = unit(raw[:, :dim])
+        kh, _ = unit(raw[:, dim : 2 * dim])
+        kv_ref, qg_ref = refs[i], refs[slots + i]
+        qg_ref[:, :dim] = (qh * gain_ref[0:1, :]).astype(BF16)
+        qg_ref[:, dim:] = raw[:, 3 * dim :].astype(BF16)
+        kv_ref[:, :dim] = (kh * gain_ref[1:2, :]).astype(BF16)
+        kv_ref[:, dim:] = raw[:, 2 * dim : 3 * dim].astype(BF16)
+
+
+def finish(own, come, gains):
+    rows, dim = own.shape[0], gains.shape[1]
+    slots = own.shape[1] // (4 * dim)
+    raw, *refs = call(
+        partial(finish_kernel, slots),
+        "finish",
+        [((rows, 2 * dim * slots), F32)] + [((rows, 2 * dim), BF16)] * (2 * slots),
+        (own, come, gains),
+        6,
+        flops=20 * own.size,
+        touched=16 * own.size,
+        roots=2 * rows * slots,
+    )
+    return raw, refs[:slots], refs[slots:]
+
+
+def attention_kernel(scale, block, slots, *refs):
+    qgs, kvs = refs[:slots], refs[slots:-9]
+    dq_ref, stay_ref, send_ref, q_ref, g_ref, k_ref, v_ref, prob_ref, dprob_ref = refs[-9:]
+    total, dim = k_ref.shape
+    rows = q_ref.shape[0]
+    steps = total // block
+    for i, qg in enumerate(qgs):
+        at = pl.ds(i * qg.shape[0], qg.shape[0])
+        q_ref[at, :] = qg[:, :dim]
+        g_ref[at, :] = qg[:, dim:]
+    at = 0
+    for kv in kvs:
+        k_ref[pl.ds(at, kv.shape[0]), :] = kv[:, :dim]
+        v_ref[pl.ds(at, kv.shape[0]), :] = kv[:, dim:]
+        at += kv.shape[0]
+
+    def scores(i, top):
+        here = pl.ds(pl.multiple_of(i * block, block), block)
+        s = lax.dot_general(k_ref[here, :], q_ref[...], NT, preferred_element_type=F32) * scale
+        prob_ref[here, :] = s
+        dprob_ref[here, :] = lax.dot_general(
+            v_ref[here, :], g_ref[...], NT, preferred_element_type=F32
+        )
+        return jnp.maximum(top, jnp.max(s, axis=0, keepdims=True))
+
+    top = lax.fori_loop(0, steps, scores, jnp.full((1, rows), -jnp.inf, F32))
+
+    def weigh(i, carry):
+        norm, cross = carry
+        here = pl.ds(pl.multiple_of(i * block, block), block)
+        e = jnp.exp(prob_ref[here, :] - top)
+        prob_ref[here, :] = e
+        return (
+            norm + jnp.sum(e, axis=0, keepdims=True),
+            cross + jnp.sum(e * dprob_ref[here, :], axis=0, keepdims=True),
+        )
+
+    none = jnp.zeros((1, rows), F32)
+    norm, cross = lax.fori_loop(0, steps, weigh, (none, none))
+    inverse = 1.0 / norm
+    delta = cross * inverse
+    dq = jnp.zeros((dim, rows), F32)
+    quarter = total // 4
+    for turn in range(4):
+        out_ref = (stay_ref, send_ref)[turn % 2]
+
+        def back(i, dq):
+            here = pl.ds(pl.multiple_of(turn * quarter + i * block, block), block)
+            to = pl.ds(pl.multiple_of(i * block, block), block)
+            p = prob_ref[here, :] * inverse
+            ds = (p * (dprob_ref[here, :] - delta)).astype(BF16)
+            out_ref[turn // 2, to, :dim] = jnp.dot(ds, q_ref[...], preferred_element_type=F32) * scale
+            out_ref[turn // 2, to, dim:] = jnp.dot(
+                p.astype(BF16), g_ref[...], preferred_element_type=F32
+            )
+            return dq + lax.dot_general(k_ref[here, :], ds, TN, preferred_element_type=F32)
+
+        dq = lax.fori_loop(0, quarter // block, back, dq)
+    dq_ref[...] = (dq.T * scale).astype(BF16)
+
+
+def attention(qgs, kvs):
+    dim = qgs[0].shape[1] // 2
+    rows = sum(qg.shape[0] for qg in qgs)
+    total = 4 * rows
+    work = rows * total * dim
+    block = rows // 2
+    terms = ((2, rows, 2 * dim), F32)
+    return call(
+        partial(attention_kernel, 1.0 / math.sqrt(dim), block, len(qgs)),
+        "attention",
+        [((rows, dim), BF16), terms, terms],
+        (*qgs, *kvs),
+        24,
+        flops=10 * work,
+        touched=16 * total * dim,
+        roots=rows * total,
+        scratch=[pltpu.VMEM((rows, dim), BF16)] * 2
+        + [pltpu.VMEM((total, dim), BF16)] * 2
+        + [pltpu.VMEM((total, rows), F32)] * 2,
+    )
+
+
+def unfinish_kernel(slots, gain_ref, *refs):
+    raws, dqs, dkvs = refs[:slots], refs[slots : 2 * slots], refs[2 * slots : 3 * slots]
+    out_ref = refs[-1]
+    dim = gain_ref.shape[1]
+
+    def unit_back(raw, gain, upstream):
+        hat, scale_back = unit(raw)
+        up = upstream.astype(F32) * gain
+        return scale_back * (up - hat * jnp.mean(up * hat, axis=-1, keepdims=True))
+
+    for i, (raw, dq, dkv) in enumerate(zip(raws, dqs, dkvs)):
+        at = 3 * dim * i
+        dq = unit_back(raw[:, :dim], gain_ref[0:1, :], dq[...])
+        dk = unit_back(raw[:, dim:], gain_ref[1:2, :], dkv[:, :dim])
+        out_ref[:, at : at + dim] = dq.astype(BF16)
+        out_ref[:, at + dim : at + 2 * dim] = dk.astype(BF16)
+        out_ref[:, at + 2 * dim : at + 3 * dim] = dkv[:, dim:]
+
+
+def unfinish(gains, raws, dqs, dkvs):
+    slots, (rows, dim) = len(dqs), dqs[0].shape
+    return call(
+        partial(unfinish_kernel, slots),
+        "unfinish",
+        [((rows, 3 * dim * slots), BF16)],
+        (gains, *raws, *dqs, *dkvs),
+        6,
+        flops=60 * slots * rows * dim,
+        touched=24 * slots * rows * dim,
+        roots=2 * rows * slots,
+    )[0]
+
+
+def back_project_kernel(mine, theirs, *refs):
+    weights, (own_ref, away_ref) = refs[:-2], refs[-2:]
+    rows, half = own_ref.shape
+    width = mine.shape[1] // len(weights)
+    grads = jnp.concatenate([mine[...], theirs[...]], axis=0)
+    step = half // 7 if half % 7 == 0 else half
+    for to in range(0, half, step):
+        total = None
+        for i, whole in enumerate(weights):
+            part = lax.dot_general(
+                grads[:, width * i : width * (i + 1)],
+                whole[to : to + step, :],
+                NT,
+                preferred_element_type=F32,
+            )
+            total = part if total is None else total + part
+        own_ref[:, to : to + step] = total[:rows]
+        away_ref[:, to : to + step] = total[rows:].astype(BF16)
+
+
+def back_project(mine, theirs, weights):
+    (rows, columns), half = mine.shape, weights[0].shape[0]
+    return call(
+        back_project_kernel,
+        "back_project",
+        [((rows, half), F32), ((rows, half), BF16)],
+        (mine, theirs, *weights),
+        16,
+        flops=4 * rows * half * columns,
+        touched=2 * half * columns,
+    )
+
+
+def close_kernel(own_ref, away_ref, x_ref, c_ref, mod_ref, inv_ref, out_ref):
+    half = own_ref.shape[1]
+    core = place()[0]
+    inv = inv_ref[...]
+    total = 0.0
+    for i in range(2):
+        at = pl.ds(i * half, half)
+        grad = jnp.where(core == i, own_ref[...], away_ref[...].astype(F32))
+        dhat = grad * (1.0 + mod_ref[1:2, at])
+        out_ref[:, at] = dhat
+        total += jnp.sum(dhat * x_ref[:, at].astype(F32), axis=-1, keepdims=True)
+    cross = total * (inv * inv * (0.5 / half))
+    for i in range(2):
+        at = pl.ds(i * half, half)
+        dhat = out_ref[:, at] - x_ref[:, at].astype(F32) * cross
+        out_ref[:, at] = c_ref[:, at].astype(F32) + inv * dhat
+
+
+def close(own, away, tokens, cotangent, modulation, inv):
+    size = tokens.size
+    return call(
+        close_kernel,
+        "close",
+        [(tokens.shape, F32)],
+        (own, away, tokens, cotangent, modulation, inv),
+        12,
+        flops=10 * size,
+        touched=12 * size,
+    )[0]
+
+
+def after(value, *earlier):
+    return lax.optimization_barrier((value, *earlier))[0]
+
+
+def weight_gather_body(count, tokens, cotangent, modulation, w_qkv, w_out, qk_gain):
+    rows, dim = tokens.shape[0], qk_gain.shape[1]
+
+    def swap(value, pairs):
+        return lax.ppermute(value, "seq", pairs)
+
+    w_in = jnp.transpose(w_qkv, (1, 0, 2))
+    packed = pack(w_in, w_out)
+    keep, send, inv = front(after(tokens, packed[0]), cotangent, modulation)
+    come = swap(send, CORE_SWAP)
+    came, ones, twos, fars, moved = list(packed), [], [], [], ()
+    raws, wholes, kvs, qgs, pieces, chips = [], [], [], [], [], []
+
+    def exchange(kv, *earlier):
+        kv_chip = swap(after(kv, *earlier), CHIP_SWAP)
+        chips.append(kv_chip)
+        pieces.append([kv, swap(kv, CORE_SWAP), kv_chip])
+
+    def slot(step, blocks, weights, earlier):
+        own, away, whole = project(after(keep, *earlier), come, blocks, weights)
+        raw, (kv,), (qg,) = finish(own, swap(away, CORE_SWAP), qk_gain)
+        wholes.append(whole)
+        raws.append(raw)
+        kvs.append(around(kv, -step, count) if step else kv)
+        qgs.append(around(qg, -step, count) if step else qg)
+
+    slot(0, [], (w_in, w_out), ())
+    for step in range(1, count):
+        eight = [None] * 8
+        for i in range(2):
+            if step < count - 1:
+                came[i] = around(after(came[i], *moved), 1, count)
+            else:
+                came[i] = around(after(packed[i], *moved), -1, count)
+            moved = (came[i],)
+            pace = [keep, *ones[-1:], *twos[-1:], *fars[:-1][-1:]]
+            if i == 0 and step > 2:
+                pace += [raws[step - 2]]
+            own = after(came[i], *pace)
+            ones.append(lax.ppermute(own, PLANE, plane_swap(True)))
+            twos.append(lax.ppermute(own, PLANE, plane_swap(False)))
+            fars.append(lax.ppermute(ones[-1], PLANE, plane_swap(False)))
+            eight[4 * i : 4 * i + 4] = own, ones[-1], twos[-1], fars[-1]
+        slot(step, [eight], (), (*kvs[1:], *qgs[1:]))
+        if step == 1:
+            exchange(jnp.concatenate(kvs, axis=0))
+        elif step > 1:
+            exchange(kvs[-1], *chips)
+    pieces[-1][2] = after(pieces[-1][2], qgs[-1])
+    pieces = [[*four, swap(four[2], CORE_SWAP)] for four in pieces]
+    slots = range(count)
+    dq, stay, send = attention(qgs, [p[i] for i in range(4) for p in pieces])
+    dq = dq.reshape(count, rows, dim)
+    dqs = [around(dq[i], i, count) if i else dq[i] for i in slots]
+    summed = stay + swap(send, CORE_SWAP)
+    came, *dqs = lax.optimization_barrier((swap(summed[1].astype(BF16), CHIP_SWAP), *dqs))
+    dkv = (summed[0] + came.astype(F32)).astype(BF16).reshape(count, rows, 2 * dim)
+    dkvs = [around(dkv[i], i, count) if i else dkv[i] for i in slots]
+
+    dqkv = unfinish(qk_gain, raws, dqs, dkvs)
+    own, away = back_project(dqkv, swap(dqkv, CORE_SWAP), wholes)
+    return close(own, swap(away, CORE_SWAP), tokens, cotangent, modulation, inv)
+
+
 def solution(mesh):
     placed = (
         P(("group", "seq", "tensor"), None),
@@ -179,6 +642,15 @@
         P("tensor", None),
         P(),
     )
+    sizes = dict(mesh.shape)
+
+    def body(*args):
+        weight_elements = args[3].size + args[4].size
+        token_elements = 2 * 3 * args[0].size
+        if sizes["group"] == 2 and sizes["seq"] == 4 and weight_elements < token_elements:
+            return weight_gather_body(sizes["tensor"], *args)
+        return token_gather_body(*args)
+
     return jax.shard_map(
         body,
         mesh=mesh,

time: 353 us -> 143 us (0.41)
  waiting for transfers between devices: 236 us -> 71.3 us
  matrix products: 52.3 us -> 0 us
  starting transfers between devices: 0.31 us -> 47.7 us
  Pallas kernels: 0 us -> 23.5 us
  local copies, waits for them, and re-layouts: 19.7 us -> 0.12 us
  blocking collectives: 16.4 us -> 0 us
  between operations: 13.5 us -> 0.32 us
  other arithmetic: 12.5 us -> 0.24 us
    all_gather x2 -> x0, waiting for transfers between devices: 128 us -> none  [the longest x1 82.9 us: body(): lax.all_gather(layer_normed, 'tensor', axis=0, tiled=True)]
    reduce_scatter x1 -> x0, waiting for transfers between devices: 83.3 us -> none  [body(): lax.psum_scatter(lax.dot_general(dqkv, flat_in, (((1,), (1,)), ((), ())),...]
    ppermute x0 -> x54, waiting for transfers between devices: none -> 71.3 us  [the longest x18 39 us: around(): lax.ppermute(value, 'tensor', [(i, (i + step) % count) for i in range(cou...]
    dot_general x38 -> x0, matrix products: 52.3 us -> none  [the longest x5 11.8 us: output_step(): jnp.einsum('hqk,khd->hqd', weights_b, pair[1], preferred_element_type=jnp...]
    ppermute x0 -> x54, starting transfers between devices: none -> 47.7 us  [the longest x18 20.7 us: around(): lax.ppermute(value, 'tensor', [(i, (i + step) % count) for i in range(cou...]
    unnamed x5 -> x0, waiting for transfers between devices: 24.8 us -> none
    pallas_call x0 -> x14, Pallas kernels: none -> 23.5 us  [call(): pl.pallas_call(kernel, out_shape=out, in_specs=[anywhere if i in far else...]
    all_gather x2 -> x0, blocking collectives: 16.4 us -> none  [the longest x1 8.35 us: body(): lax.all_gather(keys_b, 'seq', axis=0, tiled=True)]
  transfers between devices with their start and end apart: 4 -> 54, of which waited for: 4 -> 28; matrix products, arithmetic and copies ran while one was open for 9% -> 0% of each run, Pallas kernels for 0% -> 3%
where the time goes in v3:
time: 143 us
  waiting for transfers between devices  71.3 us (50%)
  starting transfers between devices  47.7 us (33%)
  Pallas kernels  23.5 us (16%)
    ppermute x18, waiting for transfers between devices, around(): lax.ppermute(value, 'tensor', [(i, (i + step) % count) for i in range(cou...  39 us
    pallas_call x14, Pallas kernels, call(): pl.pallas_call(kernel, out_shape=out, in_specs=[anywhere if i in far else...  23.5 us
    ppermute x18, starting transfers between devices, around(): lax.ppermute(value, 'tensor', [(i, (i + step) % count) for i in range(cou...  20.7 us
    ppermute x18, waiting for transfers between devices, swap(): return lax.ppermute(value, 'seq', pairs)  20.4 us
    ppermute x6, starting transfers between devices, weight_gather_body(): twos.append(lax.ppermute(own, PLANE, plane_swap(False)))  8.1 us
    ppermute x6, starting transfers between devices, weight_gather_body(): fars.append(lax.ppermute(ones[-1], PLANE, plane_swap(False)))  7.03 us
    ppermute x18, starting transfers between devices, swap(): return lax.ppermute(value, 'seq', pairs)  6 us
    ppermute x6, starting transfers between devices, weight_gather_body(): ones.append(lax.ppermute(own, PLANE, plane_swap(True)))  5.82 us
  transfers between devices with their start and end apart: 54, of which 28 were waited for; matrix products, arithmetic and copies ran while one was open for 0% of the time, Pallas kernels for 3%

profile of v3, /device:TPU:0, one launch (start us, length us, event | category | flops | bytes accessed | tf_op | source)
XLA Modules:
  0.0 143.2 jit_solution(1215724119743624600)
XLA Ops:
  0.0 2.0 %pack.1 = (bf16[2,448,128]{2,1,0:T(8,128)(2,1)}, bf16[2,448,128]{2,1,0:T(8,128)(2,1)}) custom-call(bf16[3,3584,128]{2,1,0:T(8,128)(2,1)} %bitcast.9, bf16[128,3584]{1,0:T(8,128)(2,1)} %refs_1_.1), custom_call_target="tpu_custom_call" | custom-call | tf_op jit(solution)/shard_map/pack/pallas_call | solution.py:212
  2.1 1.3 front.1
  3.4 0.5 collective-permute-start
  3.9 2.6 %collective-permute-start.2 = (bf16[2,448,128]{2,1,0:T(8,128)(2,1)S(1)}, bf16[2,448,128]{2,1,0:T(8,128)(2,1)S(1)}, u32[]{:S(2)}, u32[]{:S(2)}) collective-permute-start(bf16[2,448,128]{2,1,0:T(8,128)(2,1)S(1)} %copy-done.7), channel_id=1, source_target_pairs={{0,4},{4,8},{8,12},{12,0},{1,5},{5,9},{9,13},{13,1},{2,6},{6,10},{... | collective-permute-start | bytes 688136 | tf_op jit(solution)/shard_map/ppermute | solution.py:192
  6.5 8.2 %collective-permute-done.2.refs_0_ = bf16[2,448,128]{2,1,0:T(8,128)(2,1)S(1)} collective-permute-done((bf16[2,448,128]{2,1,0:T(8,128)(2,1)S(1)}, bf16[2,448,128]{2,1,0:T(8,128)(2,1)S(1)}, u32[]{:S(2)}, u32[]{:S(2)}) %collective-permute-start.2) | collective-permute-done | bytes 229408 | tf_op jit(solution)/shard_map/ppermute | solution.py:192
  14.8 1.6 %collective-permute-start.4 = (bf16[2,448,128]{2,1,0:T(8,128)(2,1)S(1)}, bf16[2,448,128]{2,1,0:T(8,128)(2,1)S(1)}, u32[]{:S(2)}, u32[]{:S(2)}) collective-permute-start(bf16[2,448,128]{2,1,0:T(8,128)(2,1)S(1)} %collective-permute-done.2.refs_0_), channel_id=1, source_target_pairs={{0,16},{1,3},{2,18},{3,1},{16,0},{17,19},{18,2},{19,17},{4,20},{5,... | collective-permute-start | bytes 688136 | tf_op jit(solution)/shard_map/ppermute | solution.py:612
  16.4 1.5 %collective-permute-start.3 = (bf16[2,448,128]{2,1,0:T(8,128)(2,1)S(1)}, bf16[2,448,128]{2,1,0:T(8,128)(2,1)S(1)}, u32[]{:S(2)}, u32[]{:S(2)}) collective-permute-start(bf16[2,448,128]{2,1,0:T(8,128)(2,1)S(1)} %collective-permute-done.2.refs_0_), channel_id=1, source_target_pairs={{0,2},{1,17},{2,0},{3,19},{16,18},{17,1},{18,16},{19,3},{4,6},{5,2... | collective-permute-start | bytes 688136 | tf_op jit(solution)/shard_map/ppermute | solution.py:611
  17.9 6.1 %collective-permute-done.6.refs_4_ = bf16[2,448,128]{2,1,0:T(8,128)(2,1)S(1)} collective-permute-done((bf16[2,448,128]{2,1,0:T(8,128)(2,1)S(1)}, bf16[2,448,128]{2,1,0:T(8,128)(2,1)S(1)}, u32[]{:S(2)}, u32[]{:S(2)}) %collective-permute-start.6) | collective-permute-done | bytes 229408 | tf_op jit(solution)/shard_map/ppermute | solution.py:192
  23.9 1.4 collective-permute-start.7
  25.3 1.5 %collective-permute-start.8 = (bf16[2,448,128]{2,1,0:T(8,128)(2,1)S(1)}, bf16[2,448,128]{2,1,0:T(8,128)(2,1)S(1)}, u32[]{:S(2)}, u32[]{:S(2)}) collective-permute-start(bf16[2,448,128]{2,1,0:T(8,128)(2,1)S(1)} %collective-permute-done.6.refs_4_), channel_id=1, source_target_pairs={{0,16},{1,3},{2,18},{3,1},{16,0},{17,19},{18,2},{19,17},{4,20},{5,... | collective-permute-start | bytes 688136 | tf_op jit(solution)/shard_map/ppermute | solution.py:612
  26.8 0.5 collective-permute-start.5
  27.3 5.1 %collective-permute-done.7.refs_5_ = bf16[2,448,128]{2,1,0:T(8,128)(2,1)S(1)} collective-permute-done((bf16[2,448,128]{2,1,0:T(8,128)(2,1)S(1)}, bf16[2,448,128]{2,1,0:T(8,128)(2,1)S(1)}, u32[]{:S(2)}, u32[]{:S(2)}) %collective-permute-start.7) | collective-permute-done | bytes 229408 | tf_op jit(solution)/shard_map/ppermute | solution.py:611
  32.4 1.4 collective-permute-start.9
  33.9 1.4 collective-permute-start.15
  35.3 0.9 collective-permute-start.14
  36.2 3.2 %collective-permute-done.9.refs_7_ = bf16[2,448,128]{2,1,0:T(8,128)(2,1)S(1)} collective-permute-done((bf16[2,448,128]{2,1,0:T(8,128)(2,1)S(1)}, bf16[2,448,128]{2,1,0:T(8,128)(2,1)S(1)}, u32[]{:S(2)}, u32[]{:S(2)}) %collective-permute-start.9) | collective-permute-done | bytes 229408 | tf_op jit(solution)/shard_map/ppermute | solution.py:613
  39.4 1.2 project.5
  40.7 1.0 collective-permute-done.17.refs_4_
  41.7 1.0 collective-permute-start.24
  42.7 0.6 collective-permute-done.15.refs_2_
  43.4 1.3 collective-permute-start.18
  44.7 1.6 %collective-permute-start.19 = (bf16[2,448,128]{2,1,0:T(8,128)(2,1)S(1)}, bf16[2,448,128]{2,1,0:T(8,128)(2,1)S(1)}, u32[]{:S(2)}, u32[]{:S(2)}) collective-permute-start(bf16[2,448,128]{2,1,0:T(8,128)(2,1)S(1)} %collective-permute-done.17.refs_4_), channel_id=1, source_target_pairs={{0,16},{1,3},{2,18},{3,1},{16,0},{17,19},{18,2},{19,17},{4,20},{5,... | collective-permute-start | bytes 688136 | tf_op jit(solution)/shard_map/ppermute | solution.py:612
  46.7 2.0 %collective-permute-done.24.refs_0_ = bf16[2,448,128]{2,1,0:T(8,128)(2,1)S(1)} collective-permute-done((bf16[2,448,128]{2,1,0:T(8,128)(2,1)S(1)}, bf16[2,448,128]{2,1,0:T(8,128)(2,1)S(1)}, u32[]{:S(2)}, u32[]{:S(2)}) %collective-permute-start.24) | collective-permute-done | bytes 229408 | tf_op jit(solution)/shard_map/ppermute | solution.py:192
  48.7 3.6 %collective-permute-start.28 = (bf16[2,448,128]{2,1,0:T(8,128)(2,1)S(1)}, bf16[2,448,128]{2,1,0:T(8,128)(2,1)S(1)}, u32[]{:S(2)}, u32[]{:S(2)}) collective-permute-start(bf16[2,448,128]{2,1,0:T(8,128)(2,1)S(1)} %copy-done.6), channel_id=1, source_target_pairs={{0,12},{4,0},{8,4},{12,8},{1,13},{5,1},{9,5},{13,9},{2,14},{6,2},{... | collective-permute-start | bytes 688136 | tf_op jit(solution)/shard_map/ppermute | solution.py:192
  52.3 2.5 %collective-permute-start.20 = (bf16[2,448,128]{2,1,0:T(8,128)(2,1)S(1)}, bf16[2,448,128]{2,1,0:T(8,128)(2,1)S(1)}, u32[]{:S(2)}, u32[]{:S(2)}) collective-permute-start(bf16[2,448,128]{2,1,0:T(8,128)(2,1)S(1)} %collective-permute-done.18.refs_5_), channel_id=1, source_target_pairs={{0,16},{1,3},{2,18},{3,1},{16,0},{17,19},{18,2},{19,17},{4,20},{5,... | collective-permute-start | bytes 688136 | tf_op jit(solution)/shard_map/ppermute | solution.py:613
  55.5 2.7 %collective-permute-start.11 = (bf16[160,256]{1,0:T(8,128)(2,1)S(1)}, bf16[160,256]{1,0:T(8,128)(2,1)S(1)}, u32[]{:S(2)}, u32[]{:S(2)}) collective-permute-start(bf16[160,256]{1,0:T(8,128)(2,1)S(1)} %get-tuple-element.75), channel_id=1, source_target_pairs={{0,12},{4,0},{8,4},{12,8},{1,13},{5,1},{9,5},{13,9},{2,14},{6,2},{... | collective-permute-start | bytes 245768 | tf_op jit(solution)/shard_map/ppermute | solution.py:192
  58.2 2.8 %collective-permute-start.12 = (bf16[160,256]{1,0:T(8,128)(2,1)S(1)}, bf16[160,256]{1,0:T(8,128)(2,1)S(1)}, u32[]{:S(2)}, u32[]{:S(2)}) collective-permute-start(bf16[160,256]{1,0:T(8,128)(2,1)S(1)} %get-tuple-element.76), channel_id=1, source_target_pairs={{0,12},{4,0},{8,4},{12,8},{1,13},{5,1},{9,5},{13,9},{2,14},{6,2},{... | collective-permute-start | bytes 245768 | tf_op jit(solution)/shard_map/ppermute | solution.py:192
  61.0 2.7 %collective-permute-done.26.refs_2_ = bf16[2,448,128]{2,1,0:T(8,128)(2,1)S(1)} collective-permute-done((bf16[2,448,128]{2,1,0:T(8,128)(2,1)S(1)}, bf16[2,448,128]{2,1,0:T(8,128)(2,1)S(1)}, u32[]{:S(2)}, u32[]{:S(2)}) %collective-permute-start.26) | collective-permute-done | bytes 229408 | tf_op jit(solution)/shard_map/ppermute | solution.py:612
  64.1 1.2 project.6
  65.4 1.4 project.4
  66.8 0.5 collective-permute-start.1
  67.3 1.8 %collective-permute-start.30 = (bf16[2,448,128]{2,1,0:T(8,128)(2,1)S(1)}, bf16[2,448,128]{2,1,0:T(8,128)(2,1)S(1)}, u32[]{:S(2)}, u32[]{:S(2)}) collective-permute-start(bf16[2,448,128]{2,1,0:T(8,128)(2,1)S(1)} %collective-permute-done.28.refs_4_), channel_id=1, source_target_pairs={{0,16},{1,3},{2,18},{3,1},{16,0},{17,19},{18,2},{19,17},{4,20},{5,... | collective-permute-start | bytes 688136 | tf_op jit(solution)/shard_map/ppermute | solution.py:612
  69.7 2.0 %collective-permute-start.31 = (bf16[2,448,128]{2,1,0:T(8,128)(2,1)S(1)}, bf16[2,448,128]{2,1,0:T(8,128)(2,1)S(1)}, u32[]{:S(2)}, u32[]{:S(2)}) collective-permute-start(bf16[2,448,128]{2,1,0:T(8,128)(2,1)S(1)} %collective-permute-done.29.refs_5_), channel_id=1, source_target_pairs={{0,16},{1,3},{2,18},{3,1},{16,0},{17,19},{18,2},{19,17},{4,20},{5,... | collective-permute-start | bytes 688136 | tf_op jit(solution)/shard_map/ppermute | solution.py:613
  71.9 0.4 collective-permute-start.22
  72.3 2.5 %collective-permute-start.23 = (bf16[160,256]{1,0:T(8,128)(2,1)S(1)}, bf16[160,256]{1,0:T(8,128)(2,1)S(1)}, u32[]{:S(2)}, u32[]{:S(2)}) collective-permute-start(bf16[160,256]{1,0:T(8,128)(2,1)S(1)} %get-tuple-element.86), channel_id=1, source_target_pairs={{0,8},{4,12},{8,0},{12,4},{1,9},{5,13},{9,1},{13,5},{2,10},{6,14},... | collective-permute-start | bytes 245768 | tf_op jit(solution)/shard_map/ppermute | solution.py:192
  75.0 4.1 %collective-permute-done.22.refs_5_ = bf16[160,256]{1,0:T(8,128)(2,1)S(1)} collective-permute-done((bf16[160,256]{1,0:T(8,128)(2,1)S(1)}, bf16[160,256]{1,0:T(8,128)(2,1)S(1)}, u32[]{:S(2)}, u32[]{:S(2)}) %collective-permute-start.22) | collective-permute-done | bytes 81952 | tf_op jit(solution)/shard_map/ppermute | solution.py:192
  79.1 0.9 collective-permute-done.23.refs_2_
  79.9 1.3 project.7
  81.3 1.5 %collective-permute-start.38 = (bf16[320,256]{1,0:T(8,128)(2,1)S(1)}, bf16[320,256]{1,0:T(8,128)(2,1)S(1)}, u32[]{:S(2)}, u32[]{:S(2)}) collective-permute-start(bf16[320,256]{1,0:T(8,128)(2,1)S(1)} %constant_dynamic-update-slice_fusion.refs_4_), channel_id=1, source_target_pairs={{0,2},{2,0},{1,3},{3,1},{4,6},{6,4},{5,7},{7,5},{8,10},{10,8},{9,1... | collective-permute-start | bytes 491528 | tf_op jit(solution)/shard_map/ppermute | solution.py:576
  82.8 5.2 %collective-permute-done.38.refs_10_ = bf16[320,256]{1,0:T(8,128)(2,1)S(1)} collective-permute-done((bf16[320,256]{1,0:T(8,128)(2,1)S(1)}, bf16[320,256]{1,0:T(8,128)(2,1)S(1)}, u32[]{:S(2)}, u32[]{:S(2)}) %collective-permute-start.38) | collective-permute-done | bytes 163872 | tf_op jit(solution)/shard_map/ppermute | solution.py:576
  88.0 1.4 collective-permute-start.39
  89.5 0.4 collective-permute-start.34
  90.4 2.0 %collective-permute-done.39.refs_11_ = bf16[160,256]{1,0:T(8,128)(2,1)S(1)} collective-permute-done((bf16[160,256]{1,0:T(8,128)(2,1)S(1)}, bf16[160,256]{1,0:T(8,128)(2,1)S(1)}, u32[]{:S(2)}, u32[]{:S(2)}) %collective-permute-start.39) | collective-permute-done | bytes 81952 | tf_op jit(solution)/shard_map/ppermute | solution.py:576
  92.4 4.2 %collective-permute-done.34.refs_6_ = bf16[160,256]{1,0:T(8,128)(2,1)S(1)} collective-permute-done((bf16[160,256]{1,0:T(8,128)(2,1)S(1)}, bf16[160,256]{1,0:T(8,128)(2,1)S(1)}, u32[]{:S(2)}, u32[]{:S(2)}) %collective-permute-start.34) | collective-permute-done | bytes 81952 | tf_op jit(solution)/shard_map/ppermute | solution.py:192
  96.7 0.5 collective-permute-start.36
  97.5 3.6 %collective-permute-done.40.refs_12_ = bf16[160,256]{1,0:T(8,128)(2,1)S(1)} collective-permute-done((bf16[160,256]{1,0:T(8,128)(2,1)S(1)}, bf16[160,256]{1,0:T(8,128)(2,1)S(1)}, u32[]{:S(2)}, u32[]{:S(2)}) %collective-permute-start.40) | collective-permute-done | bytes 81952 | tf_op jit(solution)/shard_map/ppermute | solution.py:576
  101.1 0.5 collective-permute-start.43
  101.6 0.8 collective-permute-done.37.refs_9_
  102.5 8.8 %attention.1 = (bf16[640,128]{1,0:T(8,128)(2,1)S(1)}, f32[2,640,256]{2,1,0:T(8,128)S(1)}, f32[2,640,256]{2,1,0:T(8,128)S(1)}) custom-call(bf16[160,256]{1,0:T(8,128)(2,1)S(1)} %get-tuple-element.95.refs_0_, bf16[160,256]{1,0:T(8,128)(2,1)S(1)} %collective-permute-done.12.refs_1_, bf16[160,256]{1,0:T(8,128)(2,1)S(1)} %collective-permute-done.23.refs_2_, ...), custom_call_target="tpu_custom_call" | custom-call | tf_op jit(solution)/shard_map/attention/pallas_call | solution.py:212
  111.8 2.7 %collective-permute-done.44 = f32[2,640,256]{2,1,0:T(8,128)S(1)} collective-permute-done((f32[2,640,256]{2,1,0:T(8,128)S(1)}, f32[2,640,256]{2,1,0:T(8,128)S(1)}, u32[]{:S(2)}, u32[]{:S(2)}) %collective-permute-start.44) | collective-permute-done | bytes 1310752 | tf_op jit(solution)/shard_map/ppermute | solution.py:576
  114.8 1.0 collective-permute-start.48
  115.8 0.7 collective-permute-start.47
  116.9 2.0 %collective-permute-done.48.refs_7_ = bf16[160,128]{1,0:T(8,128)(2,1)S(1)} collective-permute-done((bf16[160,128]{1,0:T(8,128)(2,1)S(1)}, bf16[160,128]{1,0:T(8,128)(2,1)S(1)}, u32[]{:S(2)}, u32[]{:S(2)}) %collective-permute-start.48) | collective-permute-done | bytes 40992 | tf_op jit(solution)/shard_map/ppermute | solution.py:192
  118.8 2.8 %collective-permute-done.47.refs_6_ = bf16[160,128]{1,0:T(8,128)(2,1)S(1)} collective-permute-done((bf16[160,128]{1,0:T(8,128)(2,1)S(1)}, bf16[160,128]{1,0:T(8,128)(2,1)S(1)}, u32[]{:S(2)}, u32[]{:S(2)}) %collective-permute-start.47) | collective-permute-done | bytes 40992 | tf_op jit(solution)/shard_map/ppermute | solution.py:192
  121.6 0.7 collective-permute-done.46.refs_5_
  122.3 2.4 %collective-permute-done.45 = bf16[640,256]{1,0:T(8,128)(2,1)S(1)} collective-permute-done((bf16[640,256]{1,0:T(8,128)(2,1)S(1)}, bf16[640,256]{1,0:T(8,128)(2,1)S(1)}, u32[]{:S(2)}, u32[]{:S(2)}) %collective-permute-start.45) | collective-permute-done | bytes 327712 | tf_op jit(solution)/shard_map/ppermute | solution.py:576
  125.0 1.9 %collective-permute-start.49 = (bf16[160,256]{1,0:T(8,128)(2,1)S(1)}, bf16[160,256]{1,0:T(8,128)(2,1)S(1)}, u32[]{:S(2)}, u32[]{:S(2)}) collective-permute-start(bf16[160,256]{1,0:T(8,128)(2,1)S(1)} %get-tuple-element.119), channel_id=1, source_target_pairs={{0,4},{4,8},{8,12},{12,0},{1,5},{5,9},{9,13},{13,1},{2,6},{6,10},{... | collective-permute-start | bytes 245768 | tf_op jit(solution)/shard_map/ppermute | solution.py:192
  126.9 2.9 %collective-permute-done.51.refs_11_ = bf16[160,256]{1,0:T(8,128)(2,1)S(1)} collective-permute-done((bf16[160,256]{1,0:T(8,128)(2,1)S(1)}, bf16[160,256]{1,0:T(8,128)(2,1)S(1)}, u32[]{:S(2)}, u32[]{:S(2)}) %collective-permute-start.51) | collective-permute-done | bytes 81952 | tf_op jit(solution)/shard_map/ppermute | solution.py:192
  129.8 3.7 %collective-permute-done.50.refs_10_ = bf16[160,256]{1,0:T(8,128)(2,1)S(1)} collective-permute-done((bf16[160,256]{1,0:T(8,128)(2,1)S(1)}, bf16[160,256]{1,0:T(8,128)(2,1)S(1)}, u32[]{:S(2)}, u32[]{:S(2)}) %collective-permute-start.50) | collective-permute-done | bytes 81952 | tf_op jit(solution)/shard_map/ppermute | solution.py:192
  133.5 0.7 unfinish.1.mine
  134.3 1.9 %collective-permute-done.52.theirs = bf16[160,1536]{1,0:T(8,128)(2,1)S(1)} collective-permute-done((bf16[160,1536]{1,0:T(8,128)(2,1)S(1)}, bf16[160,1536]{1,0:T(8,128)(2,1)S(1)}, u32[]{:S(2)}, u32[]{:S(2)}) %collective-permute-start.52) | collective-permute-done | bytes 491552 | tf_op jit(solution)/shard_map/ppermute | solution.py:576
  136.2 2.5 %back_project.1 = (f32[160,1792]{1,0:T(8,128)S(1)}, bf16[160,1792]{1,0:T(8,128)(2,1)S(1)}) custom-call(bf16[160,1536]{1,0:T(8,128)(2,1)S(1)} %unfinish.1.mine, bf16[160,1536]{1,0:T(8,128)(2,1)S(1)} %collective-permute-done.52.theirs, bf16[1792,384]{1,0:T(8,128)(2,1)S(1)} %get-tuple-element.110.refs_0_, bf16[1792,384]{1,0:T(8,128)(2,1)S(1)} %get-tuple-element.111.refs_1_, ...), custom_call_target="tpu_custom_call" | custom-call | tf_op jit(solution)/shard_map/back_project/pallas_call | solution.py:212
  138.9 1.8 %collective-permute-done.53.away_ref = bf16[160,1792]{1,0:T(8,128)(2,1)S(1)} collective-permute-done((bf16[160,1792]{1,0:T(8,128)(2,1)S(1)}, bf16[160,1792]{1,0:T(8,128)(2,1)S(1)}, u32[]{:S(2)}, u32[]{:S(2)}) %collective-permute-start.53) | collective-permute-done | bytes 573472 | tf_op jit(solution)/shard_map/ppermute | solution.py:576
  140.8 2.4 %close.1 = f32[160,3584]{1,0:T(8,128)} custom-call(f32[160,1792]{1,0:T(8,128)S(1)} %get-tuple-element.114.own_ref, bf16[160,1792]{1,0:T(8,128)(2,1)S(1)} %collective-permute-done.53.away_ref, bf16[160,3584]{1,0:T(8,128)(2,1)S(1)} %copy-done.1, bf16[160,3584]{1,0:T(8,128)(2,1)S(1)} %copy-done.2, f32[3,3584]{1,0:T(4,128)S(1)} %copy-done.4, ...), custom_call_target="tpu_custom_call" | custom-call | tf_op jit(solution)/shard_map/close/pallas_call | solution.py:212
  (81 shorter events, 5.5 us)
Async XLA Ops:
  0.0 2.0 %copy-start.1 = (bf16[160,3584]{1,0:T(8,128)(2,1)S(1)}, bf16[160,3584]{1,0:T(8,128)(2,1)}, u32[]{:S(2)}) copy-start(bf16[160,3584]{1,0:T(8,128)(2,1)} %x_ref.2) | copy-start | bytes 3440644
  0.0 2.1 %copy-start.2 = (bf16[160,3584]{1,0:T(8,128)(2,1)S(1)}, bf16[160,3584]{1,0:T(8,128)(2,1)}, u32[]{:S(2)}) copy-start(bf16[160,3584]{1,0:T(8,128)(2,1)} %c_ref.3) | copy-start | bytes 3440644
  0.0 2.1 %copy-start.4 = (f32[3,3584]{1,0:T(4,128)S(1)}, f32[3,3584]{1,0:T(4,128)}, u32[]{:S(2)}) copy-start(f32[3,3584]{1,0:T(4,128)} %mod_ref.3) | copy-start | bytes 129028
  2.0 1.9 %copy-start.7 = (bf16[2,448,128]{2,1,0:T(8,128)(2,1)S(1)}, bf16[2,448,128]{2,1,0:T(8,128)(2,1)}, u32[]{:S(2)}) copy-start(bf16[2,448,128]{2,1,0:T(8,128)(2,1)} %get-tuple-element.88) | copy-start | bytes 688132
  2.0 12.7 %copy-start.6 = (bf16[2,448,128]{2,1,0:T(8,128)(2,1)S(1)}, bf16[2,448,128]{2,1,0:T(8,128)(2,1)}, u32[]{:S(2)}) copy-start(bf16[2,448,128]{2,1,0:T(8,128)(2,1)} %get-tuple-element.90) | copy-start | bytes 688132
  3.4 36.0 %collective-permute-start = (bf16[160,3584]{1,0:T(8,128)(2,1)S(1)}, bf16[160,3584]{1,0:T(8,128)(2,1)S(1)}, u32[]{:S(2)}, u32[]{:S(2)}) collective-permute-start(bf16[160,3584]{1,0:T(8,128)(2,1)S(1)} %get-tuple-element.64), channel_id=1, source_target_pairs={{0,1},{1,0},{2,3},{3,2},{4,5},{5,4},{6,7},{7,6},{8,9},{9,8},{10,11... | collective-permute-start | bytes 3440648 | tf_op jit(solution)/shard_map/ppermute | solution.py:576
  3.9 10.9 %collective-permute-start.2 = (bf16[2,448,128]{2,1,0:T(8,128)(2,1)S(1)}, bf16[2,448,128]{2,1,0:T(8,128)(2,1)S(1)}, u32[]{:S(2)}, u32[]{:S(2)}) collective-permute-start(bf16[2,448,128]{2,1,0:T(8,128)(2,1)S(1)} %copy-done.7), channel_id=1, source_target_pairs={{0,4},{4,8},{8,12},{12,0},{1,5},{5,9},{9,13},{13,1},{2,6},{6,10},{... | collective-permute-start | bytes 688136 | tf_op jit(solution)/shard_map/ppermute | solution.py:192
  14.8 9.2 %collective-permute-start.6 = (bf16[2,448,128]{2,1,0:T(8,128)(2,1)S(1)}, bf16[2,448,128]{2,1,0:T(8,128)(2,1)S(1)}, u32[]{:S(2)}, u32[]{:S(2)}) collective-permute-start(bf16[2,448,128]{2,1,0:T(8,128)(2,1)S(1)} %copy-done.6), channel_id=1, source_target_pairs={{0,4},{4,8},{8,12},{12,0},{1,5},{5,9},{9,13},{13,1},{2,6},{6,10},{... | collective-permute-start | bytes 688136 | tf_op jit(solution)/shard_map/ppermute | solution.py:192
  14.8 40.0 %copy-start.5 = (f32[2,128]{1,0:T(2,128)S(1)}, f32[2,128]{1,0:T(2,128)}, u32[]{:S(2)}) copy-start(f32[2,128]{1,0:T(2,128)} %gain_ref.9) | copy-start | bytes 3076
  14.8 9.2 %collective-permute-start.4 = (bf16[2,448,128]{2,1,0:T(8,128)(2,1)S(1)}, bf16[2,448,128]{2,1,0:T(8,128)(2,1)S(1)}, u32[]{:S(2)}, u32[]{:S(2)}) collective-permute-start(bf16[2,448,128]{2,1,0:T(8,128)(2,1)S(1)} %collective-permute-done.2.refs_0_), channel_id=1, source_target_pairs={{0,16},{1,3},{2,18},{3,1},{16,0},{17,19},{18,2},{19,17},{4,20},{5,... | collective-permute-start | bytes 688136 | tf_op jit(solution)/shard_map/ppermute | solution.py:612
  16.4 7.6 %collective-permute-start.3 = (bf16[2,448,128]{2,1,0:T(8,128)(2,1)S(1)}, bf16[2,448,128]{2,1,0:T(8,128)(2,1)S(1)}, u32[]{:S(2)}, u32[]{:S(2)}) collective-permute-start(bf16[2,448,128]{2,1,0:T(8,128)(2,1)S(1)} %collective-permute-done.2.refs_0_), channel_id=1, source_target_pairs={{0,2},{1,17},{2,0},{3,19},{16,18},{17,1},{18,16},{19,3},{4,6},{5,2... | collective-permute-start | bytes 688136 | tf_op jit(solution)/shard_map/ppermute | solution.py:611
  23.9 8.5 %collective-permute-start.7 = (bf16[2,448,128]{2,1,0:T(8,128)(2,1)S(1)}, bf16[2,448,128]{2,1,0:T(8,128)(2,1)S(1)}, u32[]{:S(2)}, u32[]{:S(2)}) collective-permute-start(bf16[2,448,128]{2,1,0:T(8,128)(2,1)S(1)} %collective-permute-done.6.refs_4_), channel_id=1, source_target_pairs={{0,2},{1,17},{2,0},{3,19},{16,18},{17,1},{18,16},{19,3},{4,6},{5,2... | collective-permute-start | bytes 688136 | tf_op jit(solution)/shard_map/ppermute | solution.py:611
  25.3 8.6 %collective-permute-start.13 = (bf16[2,448,128]{2,1,0:T(8,128)(2,1)S(1)}, bf16[2,448,128]{2,1,0:T(8,128)(2,1)S(1)}, u32[]{:S(2)}, u32[]{:S(2)}) collective-permute-start(bf16[2,448,128]{2,1,0:T(8,128)(2,1)S(1)} %collective-permute-done.2.refs_0_), channel_id=1, source_target_pairs={{0,4},{4,8},{8,12},{12,0},{1,5},{5,9},{9,13},{13,1},{2,6},{6,10},{... | collective-permute-start | bytes 688136 | tf_op jit(solution)/shard_map/ppermute | solution.py:192
  25.3 8.6 %collective-permute-start.8 = (bf16[2,448,128]{2,1,0:T(8,128)(2,1)S(1)}, bf16[2,448,128]{2,1,0:T(8,128)(2,1)S(1)}, u32[]{:S(2)}, u32[]{:S(2)}) collective-permute-start(bf16[2,448,128]{2,1,0:T(8,128)(2,1)S(1)} %collective-permute-done.6.refs_4_), channel_id=1, source_target_pairs={{0,16},{1,3},{2,18},{3,1},{16,0},{17,19},{18,2},{19,17},{4,20},{5,... | collective-permute-start | bytes 688136 | tf_op jit(solution)/shard_map/ppermute | solution.py:612
  26.8 7.1 %collective-permute-start.5 = (bf16[2,448,128]{2,1,0:T(8,128)(2,1)S(1)}, bf16[2,448,128]{2,1,0:T(8,128)(2,1)S(1)}, u32[]{:S(2)}, u32[]{:S(2)}) collective-permute-start(bf16[2,448,128]{2,1,0:T(8,128)(2,1)S(1)} %collective-permute-done.3.refs_1_), channel_id=1, source_target_pairs={{0,16},{1,3},{2,18},{3,1},{16,0},{17,19},{18,2},{19,17},{4,20},{5,... | collective-permute-start | bytes 688136 | tf_op jit(solution)/shard_map/ppermute | solution.py:613
  32.4 6.9 %collective-permute-start.9 = (bf16[2,448,128]{2,1,0:T(8,128)(2,1)S(1)}, bf16[2,448,128]{2,1,0:T(8,128)(2,1)S(1)}, u32[]{:S(2)}, u32[]{:S(2)}) collective-permute-start(bf16[2,448,128]{2,1,0:T(8,128)(2,1)S(1)} %collective-permute-done.7.refs_5_), channel_id=1, source_target_pairs={{0,16},{1,3},{2,18},{3,1},{16,0},{17,19},{18,2},{19,17},{4,20},{5,... | collective-permute-start | bytes 688136 | tf_op jit(solution)/shard_map/ppermute | solution.py:613
  33.9 7.8 %collective-permute-start.17 = (bf16[2,448,128]{2,1,0:T(8,128)(2,1)S(1)}, bf16[2,448,128]{2,1,0:T(8,128)(2,1)S(1)}, u32[]{:S(2)}, u32[]{:S(2)}) collective-permute-start(bf16[2,448,128]{2,1,0:T(8,128)(2,1)S(1)} %collective-permute-done.6.refs_4_), channel_id=1, source_target_pairs={{0,4},{4,8},{8,12},{12,0},{1,5},{5,9},{9,13},{13,1},{2,6},{6,10},{... | collective-permute-start | bytes 688136 | tf_op jit(solution)/shard_map/ppermute | solution.py:192
  33.9 9.4 %collective-permute-start.15 = (bf16[2,448,128]{2,1,0:T(8,128)(2,1)S(1)}, bf16[2,448,128]{2,1,0:T(8,128)(2,1)S(1)}, u32[]{:S(2)}, u32[]{:S(2)}) collective-permute-start(bf16[2,448,128]{2,1,0:T(8,128)(2,1)S(1)} %collective-permute-done.13.refs_0_), channel_id=1, source_target_pairs={{0,16},{1,3},{2,18},{3,1},{16,0},{17,19},{18,2},{19,17},{4,20},{5,... | collective-permute-start | bytes 688136 | tf_op jit(solution)/shard_map/ppermute | solution.py:612
  35.3 8.0 %collective-permute-start.14 = (bf16[2,448,128]{2,1,0:T(8,128)(2,1)S(1)}, bf16[2,448,128]{2,1,0:T(8,128)(2,1)S(1)}, u32[]{:S(2)}, u32[]{:S(2)}) collective-permute-start(bf16[2,448,128]{2,1,0:T(8,128)(2,1)S(1)} %collective-permute-done.13.refs_0_), channel_id=1, source_target_pairs={{0,2},{1,17},{2,0},{3,19},{16,18},{17,1},{18,16},{19,3},{4,6},{5,2... | collective-permute-start | bytes 688136 | tf_op jit(solution)/shard_map/ppermute | solution.py:611
  40.6 14.1 %collective-permute-start.10 = (f32[160,512]{1,0:T(8,128)S(1)}, f32[160,512]{1,0:T(8,128)S(1)}, u32[]{:S(2)}, u32[]{:S(2)}) collective-permute-start(f32[160,512]{1,0:T(8,128)S(1)} %get-tuple-element.73), channel_id=1, source_target_pairs={{0,1},{1,0},{2,3},{3,2},{4,5},{5,4},{6,7},{7,6},{8,9},{9,8},{10,11... | collective-permute-start | bytes 983048 | tf_op jit(solution)/shard_map/ppermute | solution.py:576
  41.7 7.0 %collective-permute-start.24 = (bf16[2,448,128]{2,1,0:T(8,128)(2,1)S(1)}, bf16[2,448,128]{2,1,0:T(8,128)(2,1)S(1)}, u32[]{:S(2)}, u32[]{:S(2)}) collective-permute-start(bf16[2,448,128]{2,1,0:T(8,128)(2,1)S(1)} %copy-done.7), channel_id=1, source_target_pairs={{0,12},{4,0},{8,4},{12,8},{1,13},{5,1},{9,5},{13,9},{2,14},{6,2},{... | collective-permute-start | bytes 688136 | tf_op jit(solution)/shard_map/ppermute | solution.py:192
  43.4 8.9 %collective-permute-start.18 = (bf16[2,448,128]{2,1,0:T(8,128)(2,1)S(1)}, bf16[2,448,128]{2,1,0:T(8,128)(2,1)S(1)}, u32[]{:S(2)}, u32[]{:S(2)}) collective-permute-start(bf16[2,448,128]{2,1,0:T(8,128)(2,1)S(1)} %collective-permute-done.17.refs_4_), channel_id=1, source_target_pairs={{0,2},{1,17},{2,0},{3,19},{16,18},{17,1},{18,16},{19,3},{4,6},{5,2... | collective-permute-start | bytes 688136 | tf_op jit(solution)/shard_map/ppermute | solution.py:611
  44.7 10.2 %collective-permute-start.19 = (bf16[2,448,128]{2,1,0:T(8,128)(2,1)S(1)}, bf16[2,448,128]{2,1,0:T(8,128)(2,1)S(1)}, u32[]{:S(2)}, u32[]{:S(2)}) collective-permute-start(bf16[2,448,128]{2,1,0:T(8,128)(2,1)S(1)} %collective-permute-done.17.refs_4_), channel_id=1, source_target_pairs={{0,16},{1,3},{2,18},{3,1},{16,0},{17,19},{18,2},{19,17},{4,20},{5,... | collective-permute-start | bytes 688136 | tf_op jit(solution)/shard_map/ppermute | solution.py:612
  46.3 8.6 %collective-permute-start.16 = (bf16[2,448,128]{2,1,0:T(8,128)(2,1)S(1)}, bf16[2,448,128]{2,1,0:T(8,128)(2,1)S(1)}, u32[]{:S(2)}, u32[]{:S(2)}) collective-permute-start(bf16[2,448,128]{2,1,0:T(8,128)(2,1)S(1)} %collective-permute-done.14.refs_1_), channel_id=1, source_target_pairs={{0,16},{1,3},{2,18},{3,1},{16,0},{17,19},{18,2},{19,17},{4,20},{5,... | collective-permute-start | bytes 688136 | tf_op jit(solution)/shard_map/ppermute | solution.py:613
  48.7 9.5 %collective-permute-start.28 = (bf16[2,448,128]{2,1,0:T(8,128)(2,1)S(1)}, bf16[2,448,128]{2,1,0:T(8,128)(2,1)S(1)}, u32[]{:S(2)}, u32[]{:S(2)}) collective-permute-start(bf16[2,448,128]{2,1,0:T(8,128)(2,1)S(1)} %copy-done.6), channel_id=1, source_target_pairs={{0,12},{4,0},{8,4},{12,8},{1,13},{5,1},{9,5},{13,9},{2,14},{6,2},{... | collective-permute-start | bytes 688136 | tf_op jit(solution)/shard_map/ppermute | solution.py:192
  52.3 8.7 %collective-permute-start.20 = (bf16[2,448,128]{2,1,0:T(8,128)(2,1)S(1)}, bf16[2,448,128]{2,1,0:T(8,128)(2,1)S(1)}, u32[]{:S(2)}, u32[]{:S(2)}) collective-permute-start(bf16[2,448,128]{2,1,0:T(8,128)(2,1)S(1)} %collective-permute-done.18.refs_5_), channel_id=1, source_target_pairs={{0,16},{1,3},{2,18},{3,1},{16,0},{17,19},{18,2},{19,17},{4,20},{5,... | collective-permute-start | bytes 688136 | tf_op jit(solution)/shard_map/ppermute | solution.py:613
  54.9 8.7 %collective-permute-start.26 = (bf16[2,448,128]{2,1,0:T(8,128)(2,1)S(1)}, bf16[2,448,128]{2,1,0:T(8,128)(2,1)S(1)}, u32[]{:S(2)}, u32[]{:S(2)}) collective-permute-start(bf16[2,448,128]{2,1,0:T(8,128)(2,1)S(1)} %collective-permute-done.24.refs_0_), channel_id=1, source_target_pairs={{0,16},{1,3},{2,18},{3,1},{16,0},{17,19},{18,2},{19,17},{4,20},{5,... | collective-permute-start | bytes 688136 | tf_op jit(solution)/shard_map/ppermute | solution.py:612
  55.1 8.5 %collective-permute-start.25 = (bf16[2,448,128]{2,1,0:T(8,128)(2,1)S(1)}, bf16[2,448,128]{2,1,0:T(8,128)(2,1)S(1)}, u32[]{:S(2)}, u32[]{:S(2)}) collective-permute-start(bf16[2,448,128]{2,1,0:T(8,128)(2,1)S(1)} %collective-permute-done.24.refs_0_), channel_id=1, source_target_pairs={{0,2},{1,17},{2,0},{3,19},{16,18},{17,1},{18,16},{19,3},{4,6},{5,2... | collective-permute-start | bytes 688136 | tf_op jit(solution)/shard_map/ppermute | solution.py:611
  55.5 8.5 %collective-permute-start.11 = (bf16[160,256]{1,0:T(8,128)(2,1)S(1)}, bf16[160,256]{1,0:T(8,128)(2,1)S(1)}, u32[]{:S(2)}, u32[]{:S(2)}) collective-permute-start(bf16[160,256]{1,0:T(8,128)(2,1)S(1)} %get-tuple-element.75), channel_id=1, source_target_pairs={{0,12},{4,0},{8,4},{12,8},{1,13},{5,1},{9,5},{13,9},{2,14},{6,2},{... | collective-permute-start | bytes 245768 | tf_op jit(solution)/shard_map/ppermute | solution.py:192
  58.2 7.2 %copy-start = (bf16[3584,3,128]{2,0,1:T(8,128)(2,1)S(1)}, bf16[3584,3,128]{2,0,1:T(8,128)(2,1)}, u32[]{:S(2)}) copy-start(bf16[3584,3,128]{2,0,1:T(8,128)(2,1)} %param.9) | copy-start | bytes 8257540
  58.2 7.2 %copy-start.3 = (bf16[128,3584]{1,0:T(8,128)(2,1)S(1)}, bf16[128,3584]{1,0:T(8,128)(2,1)}, u32[]{:S(2)}) copy-start(bf16[128,3584]{1,0:T(8,128)(2,1)} %refs_1_.1) | copy-start | bytes 2752516
  58.2 5.9 %collective-permute-start.12 = (bf16[160,256]{1,0:T(8,128)(2,1)S(1)}, bf16[160,256]{1,0:T(8,128)(2,1)S(1)}, u32[]{:S(2)}, u32[]{:S(2)}) collective-permute-start(bf16[160,256]{1,0:T(8,128)(2,1)S(1)} %get-tuple-element.76), channel_id=1, source_target_pairs={{0,12},{4,0},{8,4},{12,8},{1,13},{5,1},{9,5},{13,9},{2,14},{6,2},{... | collective-permute-start | bytes 245768 | tf_op jit(solution)/shard_map/ppermute | solution.py:192
  63.7 6.0 %collective-permute-start.29 = (bf16[2,448,128]{2,1,0:T(8,128)(2,1)S(1)}, bf16[2,448,128]{2,1,0:T(8,128)(2,1)S(1)}, u32[]{:S(2)}, u32[]{:S(2)}) collective-permute-start(bf16[2,448,128]{2,1,0:T(8,128)(2,1)S(1)} %collective-permute-done.28.refs_4_), channel_id=1, source_target_pairs={{0,2},{1,17},{2,0},{3,19},{16,18},{17,1},{18,16},{19,3},{4,6},{5,2... | collective-permute-start | bytes 688136 | tf_op jit(solution)/shard_map/ppermute | solution.py:611
  65.3 6.4 %collective-permute-start.21 = (f32[160,512]{1,0:T(8,128)S(1)}, f32[160,512]{1,0:T(8,128)S(1)}, u32[]{:S(2)}, u32[]{:S(2)}) collective-permute-start(f32[160,512]{1,0:T(8,128)S(1)} %get-tuple-element.83), channel_id=1, source_target_pairs={{0,1},{1,0},{2,3},{3,2},{4,5},{5,4},{6,7},{7,6},{8,9},{9,8},{10,11... | collective-permute-start | bytes 983048 | tf_op jit(solution)/shard_map/ppermute | solution.py:576
  66.8 5.5 %collective-permute-start.1 = (f32[160,512]{1,0:T(8,128)S(1)}, f32[160,512]{1,0:T(8,128)S(1)}, u32[]{:S(2)}, u32[]{:S(2)}) collective-permute-start(f32[160,512]{1,0:T(8,128)S(1)} %get-tuple-element.66), channel_id=1, source_target_pairs={{0,1},{1,0},{2,3},{3,2},{4,5},{5,4},{6,7},{7,6},{8,9},{9,8},{10,11... | collective-permute-start | bytes 983048 | tf_op jit(solution)/shard_map/ppermute | solution.py:576
  67.3 12.6 %collective-permute-start.30 = (bf16[2,448,128]{2,1,0:T(8,128)(2,1)S(1)}, bf16[2,448,128]{2,1,0:T(8,128)(2,1)S(1)}, u32[]{:S(2)}, u32[]{:S(2)}) collective-permute-start(bf16[2,448,128]{2,1,0:T(8,128)(2,1)S(1)} %collective-permute-done.28.refs_4_), channel_id=1, source_target_pairs={{0,16},{1,3},{2,18},{3,1},{16,0},{17,19},{18,2},{19,17},{4,20},{5,... | collective-permute-start | bytes 688136 | tf_op jit(solution)/shard_map/ppermute | solution.py:612
  69.1 10.8 %collective-permute-start.27 = (bf16[2,448,128]{2,1,0:T(8,128)(2,1)S(1)}, bf16[2,448,128]{2,1,0:T(8,128)(2,1)S(1)}, u32[]{:S(2)}, u32[]{:S(2)}) collective-permute-start(bf16[2,448,128]{2,1,0:T(8,128)(2,1)S(1)} %collective-permute-done.25.refs_1_), channel_id=1, source_target_pairs={{0,16},{1,3},{2,18},{3,1},{16,0},{17,19},{18,2},{19,17},{4,20},{5,... | collective-permute-start | bytes 688136 | tf_op jit(solution)/shard_map/ppermute | solution.py:613
  69.7 10.3 %collective-permute-start.31 = (bf16[2,448,128]{2,1,0:T(8,128)(2,1)S(1)}, bf16[2,448,128]{2,1,0:T(8,128)(2,1)S(1)}, u32[]{:S(2)}, u32[]{:S(2)}) collective-permute-start(bf16[2,448,128]{2,1,0:T(8,128)(2,1)S(1)} %collective-permute-done.29.refs_5_), channel_id=1, source_target_pairs={{0,16},{1,3},{2,18},{3,1},{16,0},{17,19},{18,2},{19,17},{4,20},{5,... | collective-permute-start | bytes 688136 | tf_op jit(solution)/shard_map/ppermute | solution.py:613
  71.9 7.2 %collective-permute-start.22 = (bf16[160,256]{1,0:T(8,128)(2,1)S(1)}, bf16[160,256]{1,0:T(8,128)(2,1)S(1)}, u32[]{:S(2)}, u32[]{:S(2)}) collective-permute-start(bf16[160,256]{1,0:T(8,128)(2,1)S(1)} %get-tuple-element.85), channel_id=1, source_target_pairs={{0,8},{4,12},{8,0},{12,4},{1,9},{5,13},{9,1},{13,5},{2,10},{6,14},... | collective-permute-start | bytes 245768 | tf_op jit(solution)/shard_map/ppermute | solution.py:192
  72.3 7.6 %collective-permute-start.23 = (bf16[160,256]{1,0:T(8,128)(2,1)S(1)}, bf16[160,256]{1,0:T(8,128)(2,1)S(1)}, u32[]{:S(2)}, u32[]{:S(2)}) collective-permute-start(bf16[160,256]{1,0:T(8,128)(2,1)S(1)} %get-tuple-element.86), channel_id=1, source_target_pairs={{0,8},{4,12},{8,0},{12,4},{1,9},{5,13},{9,1},{13,5},{2,10},{6,14},... | collective-permute-start | bytes 245768 | tf_op jit(solution)/shard_map/ppermute | solution.py:192
  81.2 8.2 %collective-permute-start.32 = (f32[160,512]{1,0:T(8,128)S(1)}, f32[160,512]{1,0:T(8,128)S(1)}, u32[]{:S(2)}, u32[]{:S(2)}) collective-permute-start(f32[160,512]{1,0:T(8,128)S(1)} %get-tuple-element.93), channel_id=1, source_target_pairs={{0,1},{1,0},{2,3},{3,2},{4,5},{5,4},{6,7},{7,6},{8,9},{9,8},{10,11... | collective-permute-start | bytes 983048 | tf_op jit(solution)/shard_map/ppermute | solution.py:576
  81.3 6.7 %collective-permute-start.38 = (bf16[320,256]{1,0:T(8,128)(2,1)S(1)}, bf16[320,256]{1,0:T(8,128)(2,1)S(1)}, u32[]{:S(2)}, u32[]{:S(2)}) collective-permute-start(bf16[320,256]{1,0:T(8,128)(2,1)S(1)} %constant_dynamic-update-slice_fusion.refs_4_), channel_id=1, source_target_pairs={{0,2},{2,0},{1,3},{3,1},{4,6},{6,4},{5,7},{7,5},{8,10},{10,8},{9,1... | collective-permute-start | bytes 491528 | tf_op jit(solution)/shard_map/ppermute | solution.py:576
  88.0 4.4 %collective-permute-start.39 = (bf16[160,256]{1,0:T(8,128)(2,1)S(1)}, bf16[160,256]{1,0:T(8,128)(2,1)S(1)}, u32[]{:S(2)}, u32[]{:S(2)}) collective-permute-start(bf16[160,256]{1,0:T(8,128)(2,1)S(1)} %collective-permute-done.22.refs_5_), channel_id=1, source_target_pairs={{0,2},{2,0},{1,3},{3,1},{4,6},{6,4},{5,7},{7,5},{8,10},{10,8},{9,1... | collective-permute-start | bytes 245768 | tf_op jit(solution)/shard_map/ppermute | solution.py:576
  89.5 7.1 %collective-permute-start.34 = (bf16[160,256]{1,0:T(8,128)(2,1)S(1)}, bf16[160,256]{1,0:T(8,128)(2,1)S(1)}, u32[]{:S(2)}, u32[]{:S(2)}) collective-permute-start(bf16[160,256]{1,0:T(8,128)(2,1)S(1)} %get-tuple-element.98), channel_id=1, source_target_pairs={{0,4},{4,8},{8,12},{12,0},{1,5},{5,9},{9,13},{13,1},{2,6},{6,10},{... | collective-permute-start | bytes 245768 | tf_op jit(solution)/shard_map/ppermute | solution.py:192
  90.0 11.1 %collective-permute-start.35 = (bf16[320,256]{1,0:T(8,128)(2,1)S(1)}, bf16[320,256]{1,0:T(8,128)(2,1)S(1)}, u32[]{:S(2)}, u32[]{:S(2)}) collective-permute-start(bf16[320,256]{1,0:T(8,128)(2,1)S(1)} %constant_dynamic-update-slice_fusion.refs_4_), channel_id=1, source_target_pairs={{0,1},{1,0},{2,3},{3,2},{4,5},{5,4},{6,7},{7,6},{8,9},{9,8},{10,11... | collective-permute-start | bytes 491528 | tf_op jit(solution)/shard_map/ppermute | solution.py:576
  90.0 7.5 %collective-permute-start.33 = (bf16[160,256]{1,0:T(8,128)(2,1)S(1)}, bf16[160,256]{1,0:T(8,128)(2,1)S(1)}, u32[]{:S(2)}, u32[]{:S(2)}) collective-permute-start(bf16[160,256]{1,0:T(8,128)(2,1)S(1)} %get-tuple-element.96), channel_id=1, source_target_pairs={{0,4},{4,8},{8,12},{12,0},{1,5},{5,9},{9,13},{13,1},{2,6},{6,10},{... | collective-permute-start | bytes 245768 | tf_op jit(solution)/shard_map/ppermute | solution.py:192
  96.6 4.4 %collective-permute-start.40 = (bf16[160,256]{1,0:T(8,128)(2,1)S(1)}, bf16[160,256]{1,0:T(8,128)(2,1)S(1)}, u32[]{:S(2)}, u32[]{:S(2)}) collective-permute-start(bf16[160,256]{1,0:T(8,128)(2,1)S(1)} %collective-permute-done.34.refs_6_), channel_id=1, source_target_pairs={{0,2},{2,0},{1,3},{3,1},{4,6},{6,4},{5,7},{7,5},{8,10},{10,8},{9,1... | collective-permute-start | bytes 245768 | tf_op jit(solution)/shard_map/ppermute | solution.py:576
  96.7 5.0 %collective-permute-start.41 = (bf16[320,256]{1,0:T(8,128)(2,1)S(1)}, bf16[320,256]{1,0:T(8,128)(2,1)S(1)}, u32[]{:S(2)}, u32[]{:S(2)}) collective-permute-start(bf16[320,256]{1,0:T(8,128)(2,1)S(1)} %collective-permute-done.38.refs_10_), channel_id=1, source_target_pairs={{0,1},{1,0},{2,3},{3,2},{4,5},{5,4},{6,7},{7,6},{8,9},{9,8},{10,11... | collective-permute-start | bytes 491528 | tf_op jit(solution)/shard_map/ppermute | solution.py:576
  96.7 5.0 %collective-permute-start.36 = (bf16[160,256]{1,0:T(8,128)(2,1)S(1)}, bf16[160,256]{1,0:T(8,128)(2,1)S(1)}, u32[]{:S(2)}, u32[]{:S(2)}) collective-permute-start(bf16[160,256]{1,0:T(8,128)(2,1)S(1)} %collective-permute-done.22.refs_5_), channel_id=1, source_target_pairs={{0,1},{1,0},{2,3},{3,2},{4,5},{5,4},{6,7},{7,6},{8,9},{9,8},{10,11... | collective-permute-start | bytes 245768 | tf_op jit(solution)/shard_map/ppermute | solution.py:576
  97.5 4.1 %collective-permute-start.42 = (bf16[160,256]{1,0:T(8,128)(2,1)S(1)}, bf16[160,256]{1,0:T(8,128)(2,1)S(1)}, u32[]{:S(2)}, u32[]{:S(2)}) collective-permute-start(bf16[160,256]{1,0:T(8,128)(2,1)S(1)} %collective-permute-done.39.refs_11_), channel_id=1, source_target_pairs={{0,1},{1,0},{2,3},{3,2},{4,5},{5,4},{6,7},{7,6},{8,9},{9,8},{10,11... | collective-permute-start | bytes 245768 | tf_op jit(solution)/shard_map/ppermute | solution.py:576
  101.1 1.3 collective-permute-start.37
  101.1 1.4 collective-permute-start.43
  111.4 3.1 %collective-permute-start.44 = (f32[2,640,256]{2,1,0:T(8,128)S(1)}, f32[2,640,256]{2,1,0:T(8,128)S(1)}, u32[]{:S(2)}, u32[]{:S(2)}) collective-permute-start(f32[2,640,256]{2,1,0:T(8,128)S(1)} %get-tuple-element.103), channel_id=1, source_target_pairs={{0,1},{1,0},{2,3},{3,2},{4,5},{5,4},{6,7},{7,6},{8,9},{9,8},{10,11... | collective-permute-start | bytes 3932168 | tf_op jit(solution)/shard_map/ppermute | solution.py:576
  114.7 10.0 %collective-permute-start.45 = (bf16[640,256]{1,0:T(8,128)(2,1)S(1)}, bf16[640,256]{1,0:T(8,128)(2,1)S(1)}, u32[]{:S(2)}, u32[]{:S(2)}) collective-permute-start(bf16[640,256]{1,0:T(8,128)(2,1)S(1)} %fusion.2), channel_id=1, source_target_pairs={{0,2},{2,0},{1,3},{3,1},{4,6},{6,4},{5,7},{7,5},{8,10},{10,8},{9,1... | collective-permute-start | bytes 983048 | tf_op jit(solution)/shard_map/ppermute | solution.py:576
  114.8 4.1 %collective-permute-start.48 = (bf16[160,128]{1,0:T(8,128)(2,1)S(1)}, bf16[160,128]{1,0:T(8,128)(2,1)S(1)}, u32[]{:S(2)}, u32[]{:S(2)}) collective-permute-start(bf16[160,128]{1,0:T(8,128)(2,1)S(1)} %get-tuple-element.121), channel_id=1, source_target_pairs={{0,12},{4,0},{8,4},{12,8},{1,13},{5,1},{9,5},{13,9},{2,14},{6,2},{... | collective-permute-start | bytes 122888 | tf_op jit(solution)/shard_map/ppermute | solution.py:192
  115.8 5.8 %collective-permute-start.47 = (bf16[160,128]{1,0:T(8,128)(2,1)S(1)}, bf16[160,128]{1,0:T(8,128)(2,1)S(1)}, u32[]{:S(2)}, u32[]{:S(2)}) collective-permute-start(bf16[160,128]{1,0:T(8,128)(2,1)S(1)} %get-tuple-element.122), channel_id=1, source_target_pairs={{0,8},{4,12},{8,0},{12,4},{1,9},{5,13},{9,1},{13,5},{2,10},{6,14},... | collective-permute-start | bytes 122888 | tf_op jit(solution)/shard_map/ppermute | solution.py:192
  116.5 5.8 %collective-permute-start.46 = (bf16[160,128]{1,0:T(8,128)(2,1)S(1)}, bf16[160,128]{1,0:T(8,128)(2,1)S(1)}, u32[]{:S(2)}, u32[]{:S(2)}) collective-permute-start(bf16[160,128]{1,0:T(8,128)(2,1)S(1)} %get-tuple-element.123), channel_id=1, source_target_pairs={{0,4},{4,8},{8,12},{12,0},{1,5},{5,9},{9,13},{13,1},{2,6},{6,10},{... | collective-permute-start | bytes 122888 | tf_op jit(solution)/shard_map/ppermute | solution.py:192
  124.8 5.0 %collective-permute-start.51 = (bf16[160,256]{1,0:T(8,128)(2,1)S(1)}, bf16[160,256]{1,0:T(8,128)(2,1)S(1)}, u32[]{:S(2)}, u32[]{:S(2)}) collective-permute-start(bf16[160,256]{1,0:T(8,128)(2,1)S(1)} %get-tuple-element.117), channel_id=1, source_target_pairs={{0,12},{4,0},{8,4},{12,8},{1,13},{5,1},{9,5},{13,9},{2,14},{6,2},{... | collective-permute-start | bytes 245768 | tf_op jit(solution)/shard_map/ppermute | solution.py:192
  124.9 8.6 %collective-permute-start.50 = (bf16[160,256]{1,0:T(8,128)(2,1)S(1)}, bf16[160,256]{1,0:T(8,128)(2,1)S(1)}, u32[]{:S(2)}, u32[]{:S(2)}) collective-permute-start(bf16[160,256]{1,0:T(8,128)(2,1)S(1)} %get-tuple-element.118), channel_id=1, source_target_pairs={{0,8},{4,12},{8,0},{12,4},{1,9},{5,13},{9,1},{13,5},{2,10},{6,14},... | collective-permute-start | bytes 245768 | tf_op jit(solution)/shard_map/ppermute | solution.py:192
  125.0 8.5 %collective-permute-start.49 = (bf16[160,256]{1,0:T(8,128)(2,1)S(1)}, bf16[160,256]{1,0:T(8,128)(2,1)S(1)}, u32[]{:S(2)}, u32[]{:S(2)}) collective-permute-start(bf16[160,256]{1,0:T(8,128)(2,1)S(1)} %get-tuple-element.119), channel_id=1, source_target_pairs={{0,4},{4,8},{8,12},{12,0},{1,5},{5,9},{9,13},{13,1},{2,6},{6,10},{... | collective-permute-start | bytes 245768 | tf_op jit(solution)/shard_map/ppermute | solution.py:192
  134.3 1.9 %collective-permute-start.52 = (bf16[160,1536]{1,0:T(8,128)(2,1)S(1)}, bf16[160,1536]{1,0:T(8,128)(2,1)S(1)}, u32[]{:S(2)}, u32[]{:S(2)}) collective-permute-start(bf16[160,1536]{1,0:T(8,128)(2,1)S(1)} %unfinish.1.mine), channel_id=1, source_target_pairs={{0,1},{1,0},{2,3},{3,2},{4,5},{5,4},{6,7},{7,6},{8,9},{9,8},{10,11... | collective-permute-start | bytes 1474568 | tf_op jit(solution)/shard_map/ppermute | solution.py:576
  138.7 2.0 %collective-permute-start.53 = (bf16[160,1792]{1,0:T(8,128)(2,1)S(1)}, bf16[160,1792]{1,0:T(8,128)(2,1)S(1)}, u32[]{:S(2)}, u32[]{:S(2)}) collective-permute-start(bf16[160,1792]{1,0:T(8,128)(2,1)S(1)} %get-tuple-element.115), channel_id=1, source_target_pairs={{0,1},{1,0},{2,3},{3,2},{4,5},{5,4},{6,7},{7,6},{8,9},{9,8},{10,11... | collective-permute-start | bytes 1720328 | tf_op jit(solution)/shard_map/ppermute | solution.py:576

commit v4 on v3

--- a/solution.py
+++ b/solution.py
@@ -205,14 +205,14 @@
     return mine, jnp.where(core == 0, across, over), jnp.where(core == 0, over, across), 3 - mine
 
 
-def call(kernel, name, out, operands, megabytes, flops=0, touched=0, roots=0, far=(), scratch=()):
+def call(kernel, name, out, operands, megabytes, far=(), scratch=()):
     vmem = pl.BlockSpec(memory_space=pltpu.VMEM)
-    anywhere = pl.BlockSpec(memory_space=pl.ANY)
+    hbm = pl.BlockSpec(memory_space=pltpu.HBM)
     out = tuple(jax.ShapeDtypeStruct(shape, dtype) for shape, dtype in out)
     return pl.pallas_call(
         kernel,
         out_shape=out,
-        in_specs=[anywhere if i in far else vmem for i in range(len(operands))],
+        in_specs=[hbm if i in far else vmem for i in range(len(operands))],
         out_specs=(vmem,) * len(out),
         scratch_shapes=list(scratch),
         compiler_params=pltpu.CompilerParams(vmem_limit_bytes=megabytes and megabytes * 1024 * 1024),
@@ -226,22 +226,21 @@
 TN = (((0,), (0,)), ((), ()))
 
 
-def pack_kernel(w_in, w_out, early, late, quarter, sems):
+def pack_kernel(w_in, w_out, packed, quarter, sems):
     core, _, _, mine = place()
-    part, dim = early.shape[1:]
+    part, dim = packed.shape[1:]
     half, tile = 4 * part, dim // 4
     rows = pl.ds(pl.multiple_of(core * half + mine * part, tile), part)
-    targets = (early.at[0], early.at[1], late.at[0])
-    copies = [pltpu.make_async_copy(w_in.at[j, rows, :], to, sems.at[j]) for j, to in enumerate(targets)]
+    copies = [pltpu.make_async_copy(w_in.at[j, rows, :], packed.at[j], sems.at[j]) for j in range(3)]
     lanes = pl.ds(pl.multiple_of(core * half, dim), half)
     heads = pl.ds(pl.multiple_of(mine * tile, tile), tile)
     copies.append(pltpu.make_async_copy(w_out.at[heads, lanes], quarter, sems.at[3]))
     for copy in copies:
         copy.start()
-    for copy in copies:
+    for copy in reversed(copies):
         copy.wait()
     for i in range(part // tile):
-        late[1, i * tile : (i + 1) * tile, :] = quarter[:, i * dim : (i + 1) * dim]
+        packed[3, i * tile : (i + 1) * tile, :] = quarter[:, i * dim : (i + 1) * dim]
 
 
 def pack(w_in, w_out):
@@ -250,13 +249,12 @@
     return call(
         pack_kernel,
         "pack",
-        [((2, part, dim), BF16)] * 2,
+        [((4, part, dim), BF16)],
         (w_in, w_out),
-        None,
-        touched=16 * part * dim,
+        60,
         far=(0, 1),
         scratch=[pltpu.VMEM((dim // 4, 4 * part), BF16), pltpu.SemaphoreType.DMA((4,))],
-    )
+    )[0]
 
 
 def front_kernel(x_ref, c_ref, mod_ref, keep_ref, send_ref, inv_ref):
@@ -283,15 +281,12 @@
 
 
 def front(tokens, cotangent, modulation):
-    size = tokens.size
     return call(
         front_kernel,
         "front",
         [(tokens.shape, BF16), (tokens.shape, BF16), ((tokens.shape[0], 1), F32)],
         (tokens, cotangent, modulation),
         12,
-        flops=20 * size,
-        touched=8 * size,
     )
 
 
@@ -314,14 +309,14 @@
         *blocks, own_ref, away_ref, whole, whole_out = refs
         dim = whole_out.shape[0]
         tile = dim // 4
-        for early, late, at in zip(blocks[:4], blocks[4:], arrivals()):
-            part = early.shape[1]
+        for block, at in zip(blocks, arrivals()):
+            part = block.shape[1]
             to = pl.ds(pl.multiple_of(at * part, tile), part)
-            for j, block in enumerate((early[0], early[1], late[0])):
-                whole[to, j * dim : (j + 1) * dim] = block
+            for j in range(3):
+                whole[to, j * dim : (j + 1) * dim] = block[j]
             to = pl.ds(pl.multiple_of(at * tile, tile), tile)
             for t in range(part // tile):
-                whole_out[to, t * dim : (t + 1) * dim] = late[1, t * tile : (t + 1) * tile, :]
+                whole_out[to, t * dim : (t + 1) * dim] = block[3, t * tile : (t + 1) * tile, :]
     x = jnp.concatenate([keep_ref[...], come_ref[...]], axis=0)
     qkv = jnp.dot(x[:, :half], whole[...], preferred_element_type=F32)
     grad = lax.dot_general(x[:, half:], whole_out[...], NT, preferred_element_type=F32)
@@ -334,16 +329,14 @@
 def project(keep, come, blocks, weights=()):
     rows, half = keep.shape[0], keep.shape[1] // 2
     first = len(weights) == 2
-    dim = weights[0].shape[2] if first else blocks[0][0].shape[2]
+    dim = (*weights, *blocks)[0].shape[2]
     sums = ((rows, 4 * dim), F32)
     return call(
         partial(project_kernel, first),
         "project",
         [sums, sums, ((half, 3 * dim), BF16)],
-        (keep, come, *weights, *[block for eight in blocks for block in eight]),
+        (keep, come, *weights, *blocks),
         12,
-        flops=16 * rows * half * dim,
-        touched=8 * half * (dim + rows),
         far=(2, 3) if first else (),
         scratch=[pltpu.VMEM((dim, half), BF16)] + [pltpu.SemaphoreType.DMA((4,))] * first,
     )
@@ -354,35 +347,23 @@
     return raw * back, back
 
 
-def finish_kernel(slots, own_ref, come_ref, gain_ref, raw_ref, *refs):
+def finish_kernel(own_ref, come_ref, gain_ref, raw_ref, *refs):
     dim = gain_ref.shape[1]
-    for i in range(slots):
-        at = 4 * dim * i
-        raw = own_ref[:, at : at + 4 * dim] + come_ref[:, at : at + 4 * dim]
-        raw_ref[:, 2 * dim * i : 2 * dim * (i + 1)] = raw[:, : 2 * dim]
-        qh, _ = unit(raw[:, :dim])
-        kh, _ = unit(raw[:, dim : 2 * dim])
-        kv_ref, qg_ref = refs[i], refs[slots + i]
-        qg_ref[:, :dim] = (qh * gain_ref[0:1, :]).astype(BF16)
-        qg_ref[:, dim:] = raw[:, 3 * dim :].astype(BF16)
-        kv_ref[:, :dim] = (kh * gain_ref[1:2, :]).astype(BF16)
-        kv_ref[:, dim:] = raw[:, 2 * dim : 3 * dim].astype(BF16)
-
-
-def finish(own, come, gains):
+    raw = own_ref[...] + come_ref[...]
+    raw_ref[...] = raw[:, : 2 * dim]
+    qh, _ = unit(raw[:, :dim])
+    kh, _ = unit(raw[:, dim : 2 * dim])
+    kv_ref, qg_ref, at = refs[0], refs[-1], 2 * dim * (2 - len(refs))
+    kv_ref[:, :dim] = (kh * gain_ref[1:2, :]).astype(BF16)
+    kv_ref[:, dim : 2 * dim] = raw[:, 2 * dim : 3 * dim].astype(BF16)
+    qg_ref[:, at : at + dim] = (qh * gain_ref[0:1, :]).astype(BF16)
+    qg_ref[:, at + dim :] = raw[:, 3 * dim :].astype(BF16)
+
+
+def finish(own, come, gains, joined):
     rows, dim = own.shape[0], gains.shape[1]
-    slots = own.shape[1] // (4 * dim)
-    raw, *refs = call(
-        partial(finish_kernel, slots),
-        "finish",
-        [((rows, 2 * dim * slots), F32)] + [((rows, 2 * dim), BF16)] * (2 * slots),
-        (own, come, gains),
-        6,
-        flops=20 * own.size,
-        touched=16 * own.size,
-        roots=2 * rows * slots,
-    )
-    return raw, refs[:slots], refs[slots:]
+    ready = [((rows, 4 * dim), BF16)] if joined else [((rows, 2 * dim), BF16)] * 2
+    return call(finish_kernel, "finish", [((rows, 2 * dim), F32)] + ready, (own, come, gains), 6)
 
 
 def attention_kernel(scale, block, slots, *refs):
@@ -393,8 +374,8 @@
     steps = total // block
     for i, qg in enumerate(qgs):
         at = pl.ds(i * qg.shape[0], qg.shape[0])
-        q_ref[at, :] = qg[:, :dim]
-        g_ref[at, :] = qg[:, dim:]
+        q_ref[at, :] = qg[:, -2 * dim : -dim]
+        g_ref[at, :] = qg[:, -dim:]
     at = 0
     for kv in kvs:
         k_ref[pl.ds(at, kv.shape[0]), :] = kv[:, :dim]
@@ -436,32 +417,27 @@
             to = pl.ds(pl.multiple_of(i * block, block), block)
             p = prob_ref[here, :] * inverse
             ds = (p * (dprob_ref[here, :] - delta)).astype(BF16)
-            out_ref[turn // 2, to, :dim] = jnp.dot(ds, q_ref[...], preferred_element_type=F32) * scale
-            out_ref[turn // 2, to, dim:] = jnp.dot(
-                p.astype(BF16), g_ref[...], preferred_element_type=F32
-            )
+            dk = jnp.dot(ds, q_ref[...], preferred_element_type=F32) * scale
+            dv = jnp.dot(p.astype(BF16), g_ref[...], preferred_element_type=F32)
+            out_ref[turn // 2, to, :dim] = dk.astype(out_ref.dtype)
+            out_ref[turn // 2, to, dim:] = dv.astype(out_ref.dtype)
             return dq + lax.dot_general(k_ref[here, :], ds, TN, preferred_element_type=F32)
 
         dq = lax.fori_loop(0, quarter // block, back, dq)
     dq_ref[...] = (dq.T * scale).astype(BF16)
 
 
-def attention(qgs, kvs):
-    dim = qgs[0].shape[1] // 2
+def attention(qgs, pieces):
+    slots, dim = len(qgs), pieces[0][0].shape[1] // 2
     rows = sum(qg.shape[0] for qg in qgs)
     total = 4 * rows
-    work = rows * total * dim
-    block = rows // 2
-    terms = ((2, rows, 2 * dim), F32)
+    terms = (2, rows, 2 * dim)
     return call(
-        partial(attention_kernel, 1.0 / math.sqrt(dim), block, len(qgs)),
+        partial(attention_kernel, 1.0 / math.sqrt(dim), rows // 2, slots),
         "attention",
-        [((rows, dim), BF16), terms, terms],
-        (*qgs, *kvs),
+        [((rows, dim), BF16), (terms, F32), (terms, BF16)],
+        [*qgs, *[piece for some in pieces for piece in some]],
         24,
-        flops=10 * work,
-        touched=16 * total * dim,
-        roots=rows * total,
         scratch=[pltpu.VMEM((rows, dim), BF16)] * 2
         + [pltpu.VMEM((total, dim), BF16)] * 2
         + [pltpu.VMEM((total, rows), F32)] * 2,
@@ -495,17 +471,13 @@
         [((rows, 3 * dim * slots), BF16)],
         (gains, *raws, *dqs, *dkvs),
         6,
-        flops=60 * slots * rows * dim,
-        touched=24 * slots * rows * dim,
-        roots=2 * rows * slots,
     )[0]
 
 
-def back_project_kernel(mine, theirs, *refs):
-    weights, (own_ref, away_ref) = refs[:-2], refs[-2:]
-    rows, half = own_ref.shape
-    width = mine.shape[1] // len(weights)
-    grads = jnp.concatenate([mine[...], theirs[...]], axis=0)
+def back_project_kernel(grads, *refs):
+    weights, out_ref = refs[:-1], refs[-1]
+    half = out_ref.shape[1]
+    width = grads.shape[1] // len(weights)
     step = half // 7 if half % 7 == 0 else half
     for to in range(0, half, step):
         total = None
@@ -517,21 +489,12 @@
                 preferred_element_type=F32,
             )
             total = part if total is None else total + part
-        own_ref[:, to : to + step] = total[:rows]
-        away_ref[:, to : to + step] = total[rows:].astype(BF16)
-
-
-def back_project(mine, theirs, weights):
-    (rows, columns), half = mine.shape, weights[0].shape[0]
-    return call(
-        back_project_kernel,
-        "back_project",
-        [((rows, half), F32), ((rows, half), BF16)],
-        (mine, theirs, *weights),
-        16,
-        flops=4 * rows * half * columns,
-        touched=2 * half * columns,
-    )
+        out_ref[:, to : to + step] = total.astype(out_ref.dtype)
+
+
+def back_project(grads, weights, dtype):
+    shape = grads.shape[0], weights[0].shape[0]
+    return call(back_project_kernel, "back_project", [(shape, dtype)], (grads, *weights), 16)[0]
 
 
 def close_kernel(own_ref, away_ref, x_ref, c_ref, mod_ref, inv_ref, out_ref):
@@ -553,15 +516,12 @@
 
 
 def close(own, away, tokens, cotangent, modulation, inv):
-    size = tokens.size
     return call(
         close_kernel,
         "close",
         [(tokens.shape, F32)],
         (own, away, tokens, cotangent, modulation, inv),
         12,
-        flops=10 * size,
-        touched=12 * size,
     )[0]
 
 
@@ -577,60 +537,70 @@
 
     w_in = jnp.transpose(w_qkv, (1, 0, 2))
     packed = pack(w_in, w_out)
-    keep, send, inv = front(after(tokens, packed[0]), cotangent, modulation)
-    come = swap(send, CORE_SWAP)
-    came, ones, twos, fars, moved = list(packed), [], [], [], ()
-    raws, wholes, kvs, qgs, pieces, chips = [], [], [], [], [], []
-
-    def exchange(kv, *earlier):
-        kv_chip = swap(after(kv, *earlier), CHIP_SWAP)
-        chips.append(kv_chip)
-        pieces.append([kv, swap(kv, CORE_SWAP), kv_chip])
-
-    def slot(step, blocks, weights, earlier):
+    keep, send, inv = front(after(tokens, packed), cotangent, modulation)
+    came, swaps = packed, []
+    raws, wholes, heads = [], [], []
+
+    def in_plane(value, axes, pairs, *earlier):
+        swaps.append(lax.ppermute(after(value, *swaps[:-2][-1:], *earlier), axes, pairs))
+        return swaps[-1]
+
+    def slot(step, blocks, weights, *earlier):
         own, away, whole = project(after(keep, *earlier), come, blocks, weights)
-        raw, (kv,), (qg,) = finish(own, swap(away, CORE_SWAP), qk_gain)
+        raw, *head = finish(own, swap(away, CORE_SWAP), qk_gain, step < count - 1)
         wholes.append(whole)
         raws.append(raw)
-        kvs.append(around(kv, -step, count) if step else kv)
-        qgs.append(around(qg, -step, count) if step else qg)
-
-    slot(0, [], (w_in, w_out), ())
+        heads.append(head)
+
+    def across(value, step):
+        pairs = [(4 * t + s, (t + step) % count * 4 + (s ^ 2)) for t in range(count) for s in range(4)]
+        return lax.ppermute(value, ("tensor", "seq"), pairs)
+
+    def home(step, *earlier):
+        for i, part in enumerate(heads[step]):
+            heads[step][i] = around(after(part, *earlier), -step, count)
+            earlier = (heads[step][i],)
+        return earlier
+
     for step in range(1, count):
-        eight = [None] * 8
-        for i in range(2):
-            if step < count - 1:
-                came[i] = around(after(came[i], *moved), 1, count)
-            else:
-                came[i] = around(after(packed[i], *moved), -1, count)
-            moved = (came[i],)
-            pace = [keep, *ones[-1:], *twos[-1:], *fars[:-1][-1:]]
-            if i == 0 and step > 2:
-                pace += [raws[step - 2]]
-            own = after(came[i], *pace)
-            ones.append(lax.ppermute(own, PLANE, plane_swap(True)))
-            twos.append(lax.ppermute(own, PLANE, plane_swap(False)))
-            fars.append(lax.ppermute(ones[-1], PLANE, plane_swap(False)))
-            eight[4 * i : 4 * i + 4] = own, ones[-1], twos[-1], fars[-1]
-        slot(step, [eight], (), (*kvs[1:], *qgs[1:]))
+        last = step == count - 1
+        came = around(after(packed, came), -1, count) if last else around(came, 1, count)
         if step == 1:
-            exchange(jnp.concatenate(kvs, axis=0))
-        elif step > 1:
-            exchange(kvs[-1], *chips)
-    pieces[-1][2] = after(pieces[-1][2], qgs[-1])
+            come = swap(after(send, came), CORE_SWAP)
+        one = in_plane(came, PLANE, plane_swap(True), *([keep] if step == 1 else raws[: step - 1]))
+        sent = home(1, came) if last else ()
+        two = in_plane(came, PLANE, plane_swap(False), *sent)
+        far = in_plane(one, PLANE, plane_swap(False), *([two, raws[-1]] if last else ()))
+        if step == 1:
+            slot(0, [], (w_in, w_out))
+        if last:
+            for i in range(2, step):
+                sent = home(i, *sent)
+        slot(step, [came, one, two, far], (), *sent)
+    kv, qg = after(heads[-1][0], *sent), after(heads[-1][1], *sent)
+    turned = across(kv, 1 - count)
+    heads[-1] = [around(kv, 1 - count, count), around(qg, 1 - count, count)]
+
+    kv = jnp.concatenate([head[0][:, : 2 * dim] for head in heads[:-1]], axis=0)
+    pieces = [[kv, swap(kv, CORE_SWAP), in_plane(kv, "seq", CHIP_SWAP)]]
+    kv = heads[-1][0]
+    pieces.append([kv, swap(kv, CORE_SWAP), turned])
+    pieces[0][2] = after(pieces[0][2], *heads[-1], turned)
     pieces = [[*four, swap(four[2], CORE_SWAP)] for four in pieces]
+    pieces = [[four[i] for four in pieces] for i in range(4)]
+    qgs = [head[-1] for head in heads]
     slots = range(count)
-    dq, stay, send = attention(qgs, [p[i] for i in range(4) for p in pieces])
+    dq, stay, send = attention(qgs, pieces)
     dq = dq.reshape(count, rows, dim)
     dqs = [around(dq[i], i, count) if i else dq[i] for i in slots]
-    summed = stay + swap(send, CORE_SWAP)
+    summed = stay + swap(send, CORE_SWAP).astype(F32)
     came, *dqs = lax.optimization_barrier((swap(summed[1].astype(BF16), CHIP_SWAP), *dqs))
     dkv = (summed[0] + came.astype(F32)).astype(BF16).reshape(count, rows, 2 * dim)
     dkvs = [around(dkv[i], i, count) if i else dkv[i] for i in slots]
 
     dqkv = unfinish(qk_gain, raws, dqs, dkvs)
-    own, away = back_project(dqkv, swap(dqkv, CORE_SWAP), wholes)
-    return close(own, swap(away, CORE_SWAP), tokens, cotangent, modulation, inv)
+    away = swap(back_project(swap(dqkv, CORE_SWAP), wholes, BF16), CORE_SWAP)
+    return close(back_project(dqkv, wholes, F32), away, tokens, cotangent, modulation, inv)
 
 
 def solution(mesh):

time: 143 us -> 130 us (0.909)
  starting transfers between devices: 47.7 us -> 35.3 us
  waiting for transfers between devices: 71.3 us -> 68.1 us
    ppermute x18 -> x13, waiting for transfers between devices: 20.4 us -> 10.5 us  [swap(): return lax.ppermute(value, 'seq', pairs)]
    ppermute x18 -> x13, starting transfers between devices: 20.7 us -> 13.4 us  [around(): lax.ppermute(value, 'tensor', [(i, (i + step) % count) for i in range(cou...]
    ppermute x18 -> x11, waiting for transfers between devices: 11.9 us -> 19 us  [the longest x10 17.1 us: in_plane(): lax.ppermute(after(value, *swaps[:-2][-1:], *earlier), axes, pairs)]
    ppermute x18 -> x13, starting transfers between devices: 6 us -> 2.1 us  [swap(): return lax.ppermute(value, 'seq', pairs)]
    ppermute x18 -> x11, starting transfers between devices: 21 us -> 19.8 us  [the longest x10 15.9 us: in_plane(): lax.ppermute(after(value, *swaps[:-2][-1:], *earlier), axes, pairs)]
    pallas_call x14 -> x15, Pallas kernels: 23.5 us -> 24.4 us  [call(): pl.pallas_call(kernel, out_shape=out, in_specs=[hbm if i in far else vmem...]
    ppermute x18 -> x13, waiting for transfers between devices: 39 us -> 38.7 us  [around(): lax.ppermute(value, 'tensor', [(i, (i + step) % count) for i in range(cou...]
  transfers between devices with their start and end apart: 54 -> 37, of which waited for: 28 -> 25; matrix products, arithmetic and copies ran while one was open for 0% -> 0% of each run, Pallas kernels for 3% -> 6%
where the time goes in v4:
time: 130 us
  waiting for transfers between devices  68.1 us (52%)
  starting transfers between devices  35.3 us (27%)
  Pallas kernels  24.4 us (19%)
  local copies, waits for them, and re-layouts  1.38 us (1%)
    ppermute x13, waiting for transfers between devices, around(): lax.ppermute(value, 'tensor', [(i, (i + step) % count) for i in range(cou...  38.7 us
    pallas_call x15, Pallas kernels, call(): pl.pallas_call(kernel, out_shape=out, in_specs=[hbm if i in far else vmem...  24.4 us
    ppermute x10, waiting for transfers between devices, in_plane(): lax.ppermute(after(value, *swaps[:-2][-1:], *earlier), axes, pairs)  17.1 us
    ppermute x10, starting transfers between devices, in_plane(): lax.ppermute(after(value, *swaps[:-2][-1:], *earlier), axes, pairs)  15.9 us
    ppermute x13, starting transfers between devices, around(): lax.ppermute(value, 'tensor', [(i, (i + step) % count) for i in range(cou...  13.4 us
    ppermute x13, waiting for transfers between devices, swap(): return lax.ppermute(value, 'seq', pairs)  10.5 us
    ppermute x1, starting transfers between devices, across(): return lax.ppermute(value, ('tensor', 'seq'), pairs)  3.96 us
  transfers between devices with their start and end apart: 37, of which 25 were waited for; matrix products, arithmetic and copies ran while one was open for 0% of the time, Pallas kernels for 6%

profile of v4, /device:TPU:0, one launch (start us, length us, event | category | flops | bytes accessed | tf_op | source)
XLA Modules:
  0.0 129.8 jit_solution(1090572286756162722)
XLA Ops:
  0.0 2.0 %pack.1 = bf16[4,448,128]{2,1,0:T(8,128)(2,1)} custom-call(bf16[3,3584,128]{2,1,0:T(8,128)(2,1)} %bitcast.9, bf16[128,3584]{1,0:T(8,128)(2,1)} %refs_1_.1), custom_call_target="tpu_custom_call" | custom-call | tf_op jit(solution)/shard_map/pack/pallas_call | solution.py:212
  2.1 3.1 %collective-permute-start = (bf16[4,448,128]{2,1,0:T(8,128)(2,1)}, bf16[4,448,128]{2,1,0:T(8,128)(2,1)S(1)}, u32[]{:S(2)}, u32[]{:S(2)}) collective-permute-start(bf16[4,448,128]{2,1,0:T(8,128)(2,1)} %pack.1), channel_id=1, source_target_pairs={{0,4},{4,8},{8,12},{12,0},{1,5},{5,9},{9,13},{13,1},{2,6},{6,10},{... | collective-permute-start | bytes 1376264 | tf_op jit(solution)/shard_map/ppermute | solution.py:192
  5.2 1.3 copy-done.2
  6.4 1.3 front.1
  7.7 10.2 %collective-permute-done.refs_0_ = bf16[4,448,128]{2,1,0:T(8,128)(2,1)S(1)} collective-permute-done((bf16[4,448,128]{2,1,0:T(8,128)(2,1)}, bf16[4,448,128]{2,1,0:T(8,128)(2,1)S(1)}, u32[]{:S(2)}, u32[]{:S(2)}) %collective-permute-start) | collective-permute-done | bytes 458784 | tf_op jit(solution)/shard_map/ppermute | solution.py:192
  17.9 1.6 %collective-permute-start.3 = (bf16[4,448,128]{2,1,0:T(8,128)(2,1)S(1)}, bf16[4,448,128]{2,1,0:T(8,128)(2,1)S(1)}, u32[]{:S(2)}, u32[]{:S(2)}) collective-permute-start(bf16[4,448,128]{2,1,0:T(8,128)(2,1)S(1)} %collective-permute-done.refs_0_), channel_id=1, source_target_pairs={{0,2},{1,17},{2,0},{3,19},{16,18},{17,1},{18,16},{19,3},{4,6},{5,2... | collective-permute-start | bytes 1376264 | tf_op jit(solution)/shard_map/ppermute | solution.py:545
  19.5 1.2 collective-permute-done.1.come_ref
  20.7 1.4 %project.4 = (f32[160,512]{1,0:T(8,128)S(1)}, f32[160,512]{1,0:T(8,128)S(1)}, bf16[1792,384]{1,0:T(8,128)(2,1)S(1)}) custom-call(bf16[160,3584]{1,0:T(8,128)(2,1)S(1)} %get-tuple-element.76.keep_ref, bf16[160,3584]{1,0:T(8,128)(2,1)S(1)} %collective-permute-done.1.come_ref, bf16[3,3584,128]{2,1,0:T(8,128)(2,1)S(1)} %bitcast.10, bf16[128,3584]{1,0:T(8,128)(2,1)S(1)} %copy-done.4), custom_call_target="tpu_custom_call" | custom-call | tf_op jit(solution)/shard_map/project/pallas_call | solution.py:212
  22.1 0.2 collective-permute-start.2
  22.3 1.5 %collective-permute-start.4 = (bf16[4,448,128]{2,1,0:T(8,128)(2,1)S(1)}, bf16[4,448,128]{2,1,0:T(8,128)(2,1)S(1)}, u32[]{:S(2)}, u32[]{:S(2)}) collective-permute-start(bf16[4,448,128]{2,1,0:T(8,128)(2,1)S(1)} %collective-permute-done.refs_0_), channel_id=1, source_target_pairs={{0,16},{1,3},{2,18},{3,1},{16,0},{17,19},{18,2},{19,17},{4,20},{5,... | collective-permute-start | bytes 1376264 | tf_op jit(solution)/shard_map/ppermute | solution.py:545
  23.8 3.8 %collective-permute-done.3.refs_1_ = bf16[4,448,128]{2,1,0:T(8,128)(2,1)S(1)} collective-permute-done((bf16[4,448,128]{2,1,0:T(8,128)(2,1)S(1)}, bf16[4,448,128]{2,1,0:T(8,128)(2,1)S(1)}, u32[]{:S(2)}, u32[]{:S(2)}) %collective-permute-start.3) | collective-permute-done | bytes 458784 | tf_op jit(solution)/shard_map/ppermute | solution.py:545
  27.6 1.5 %collective-permute-start.5 = (bf16[4,448,128]{2,1,0:T(8,128)(2,1)S(1)}, bf16[4,448,128]{2,1,0:T(8,128)(2,1)S(1)}, u32[]{:S(2)}, u32[]{:S(2)}) collective-permute-start(bf16[4,448,128]{2,1,0:T(8,128)(2,1)S(1)} %collective-permute-done.3.refs_1_), channel_id=1, source_target_pairs={{0,16},{1,3},{2,18},{3,1},{16,0},{17,19},{18,2},{19,17},{4,20},{5,... | collective-permute-start | bytes 1376264 | tf_op jit(solution)/shard_map/ppermute | solution.py:545
  29.1 0.1 finish.4
  29.2 4.6 %collective-permute-done.7.refs_0_ = bf16[4,448,128]{2,1,0:T(8,128)(2,1)S(1)} collective-permute-done((bf16[4,448,128]{2,1,0:T(8,128)(2,1)S(1)}, bf16[4,448,128]{2,1,0:T(8,128)(2,1)S(1)}, u32[]{:S(2)}, u32[]{:S(2)}) %collective-permute-start.7) | collective-permute-done | bytes 458784 | tf_op jit(solution)/shard_map/ppermute | solution.py:192
  33.9 1.1 collective-permute-start.8
  35.0 1.4 %collective-permute-done.5.refs_3_ = bf16[4,448,128]{2,1,0:T(8,128)(2,1)S(1)} collective-permute-done((bf16[4,448,128]{2,1,0:T(8,128)(2,1)S(1)}, bf16[4,448,128]{2,1,0:T(8,128)(2,1)S(1)}, u32[]{:S(2)}, u32[]{:S(2)}) %collective-permute-start.5) | collective-permute-done | bytes 458784 | tf_op jit(solution)/shard_map/ppermute | solution.py:545
  36.5 1.2 project.5
  37.8 2.5 %collective-permute-start.9 = (bf16[4,448,128]{2,1,0:T(8,128)(2,1)S(1)}, bf16[4,448,128]{2,1,0:T(8,128)(2,1)S(1)}, u32[]{:S(2)}, u32[]{:S(2)}) collective-permute-start(bf16[4,448,128]{2,1,0:T(8,128)(2,1)S(1)} %collective-permute-done.7.refs_0_), channel_id=1, source_target_pairs={{0,16},{1,3},{2,18},{3,1},{16,0},{17,19},{18,2},{19,17},{4,20},{5,... | collective-permute-start | bytes 1376264 | tf_op jit(solution)/shard_map/ppermute | solution.py:545
  40.3 3.4 %collective-permute-done.8.refs_1_ = bf16[4,448,128]{2,1,0:T(8,128)(2,1)S(1)} collective-permute-done((bf16[4,448,128]{2,1,0:T(8,128)(2,1)S(1)}, bf16[4,448,128]{2,1,0:T(8,128)(2,1)S(1)}, u32[]{:S(2)}, u32[]{:S(2)}) %collective-permute-start.8) | collective-permute-done | bytes 458784 | tf_op jit(solution)/shard_map/ppermute | solution.py:545
  43.8 0.1 finish.5
  43.9 1.8 %collective-permute-done.12.refs_0_ = bf16[4,448,128]{2,1,0:T(8,128)(2,1)S(1)} collective-permute-done((bf16[4,448,128]{2,1,0:T(8,128)(2,1)S(1)}, bf16[4,448,128]{2,1,0:T(8,128)(2,1)S(1)}, u32[]{:S(2)}, u32[]{:S(2)}) %collective-permute-start.12) | collective-permute-done | bytes 458784 | tf_op jit(solution)/shard_map/ppermute | solution.py:192
  45.7 2.1 %collective-permute-start.13 = (bf16[160,512]{1,0:T(8,128)(2,1)S(1)}, bf16[160,512]{1,0:T(8,128)(2,1)S(1)}, u32[]{:S(2)}, u32[]{:S(2)}) collective-permute-start(bf16[160,512]{1,0:T(8,128)(2,1)S(1)} %get-tuple-element.74), channel_id=1, source_target_pairs={{0,12},{4,0},{8,4},{12,8},{1,13},{5,1},{9,5},{13,9},{2,14},{6,2},{... | collective-permute-start | bytes 491528 | tf_op jit(solution)/shard_map/ppermute | solution.py:192
  47.8 3.2 %collective-permute-done.13.refs_1_ = bf16[160,512]{1,0:T(8,128)(2,1)S(1)} collective-permute-done((bf16[160,512]{1,0:T(8,128)(2,1)S(1)}, bf16[160,512]{1,0:T(8,128)(2,1)S(1)}, u32[]{:S(2)}, u32[]{:S(2)}) %collective-permute-start.13) | collective-permute-done | bytes 163872 | tf_op jit(solution)/shard_map/ppermute | solution.py:192
  51.0 1.7 %collective-permute-start.16 = (bf16[4,448,128]{2,1,0:T(8,128)(2,1)S(1)}, bf16[4,448,128]{2,1,0:T(8,128)(2,1)S(1)}, u32[]{:S(2)}, u32[]{:S(2)}) collective-permute-start(bf16[4,448,128]{2,1,0:T(8,128)(2,1)S(1)} %collective-permute-done.12.refs_0_), channel_id=1, source_target_pairs={{0,16},{1,3},{2,18},{3,1},{16,0},{17,19},{18,2},{19,17},{4,20},{5,... | collective-permute-start | bytes 1376264 | tf_op jit(solution)/shard_map/ppermute | solution.py:545
  52.7 2.3 %collective-permute-start.15 = (bf16[4,448,128]{2,1,0:T(8,128)(2,1)S(1)}, bf16[4,448,128]{2,1,0:T(8,128)(2,1)S(1)}, u32[]{:S(2)}, u32[]{:S(2)}) collective-permute-start(bf16[4,448,128]{2,1,0:T(8,128)(2,1)S(1)} %collective-permute-done.12.refs_0_), channel_id=1, source_target_pairs={{0,2},{1,17},{2,0},{3,19},{16,18},{17,1},{18,16},{19,3},{4,6},{5,2... | collective-permute-start | bytes 1376264 | tf_op jit(solution)/shard_map/ppermute | solution.py:545
  55.1 1.2 project.6
  56.4 1.6 %collective-permute-done.11.come_ref = f32[160,512]{1,0:T(8,128)S(1)} collective-permute-done((f32[160,512]{1,0:T(8,128)S(1)}, f32[160,512]{1,0:T(8,128)S(1)}, u32[]{:S(2)}, u32[]{:S(2)}) %collective-permute-start.11) | collective-permute-done | bytes 327712 | tf_op jit(solution)/shard_map/ppermute | solution.py:536
  58.0 0.1 finish.6
  58.2 6.1 %collective-permute-done.16.refs_2_ = bf16[4,448,128]{2,1,0:T(8,128)(2,1)S(1)} collective-permute-done((bf16[4,448,128]{2,1,0:T(8,128)(2,1)S(1)}, bf16[4,448,128]{2,1,0:T(8,128)(2,1)S(1)}, u32[]{:S(2)}, u32[]{:S(2)}) %collective-permute-start.16) | collective-permute-done | bytes 458784 | tf_op jit(solution)/shard_map/ppermute | solution.py:545
  64.3 1.7 %collective-permute-start.17 = (bf16[4,448,128]{2,1,0:T(8,128)(2,1)S(1)}, bf16[4,448,128]{2,1,0:T(8,128)(2,1)S(1)}, u32[]{:S(2)}, u32[]{:S(2)}) collective-permute-start(bf16[4,448,128]{2,1,0:T(8,128)(2,1)S(1)} %collective-permute-done.15.refs_1_), channel_id=1, source_target_pairs={{0,16},{1,3},{2,18},{3,1},{16,0},{17,19},{18,2},{19,17},{4,20},{5,... | collective-permute-start | bytes 1376264 | tf_op jit(solution)/shard_map/ppermute | solution.py:545
  66.0 0.2 collective-permute-start.14
  66.2 8.6 %collective-permute-done.14.refs_2_ = bf16[160,512]{1,0:T(8,128)(2,1)S(1)} collective-permute-done((bf16[160,512]{1,0:T(8,128)(2,1)S(1)}, bf16[160,512]{1,0:T(8,128)(2,1)S(1)}, u32[]{:S(2)}, u32[]{:S(2)}) %collective-permute-start.14) | collective-permute-done | bytes 163872 | tf_op jit(solution)/shard_map/ppermute | solution.py:192
  74.8 1.2 project.7
  76.2 1.8 %collective-permute-start.23 = (bf16[480,256]{1,0:T(8,128)(2,1)S(1)}, bf16[480,256]{1,0:T(8,128)(2,1)S(1)}, u32[]{:S(2)}, u32[]{:S(2)}) collective-permute-start(bf16[480,256]{1,0:T(8,128)(2,1)S(1)} %pad_maximum_fusion.refs_4_), channel_id=1, source_target_pairs={{0,2},{2,0},{1,3},{3,1},{4,6},{6,4},{5,7},{7,5},{8,10},{10,8},{9,1... | collective-permute-start | bytes 737288 | tf_op jit(solution)/shard_map/ppermute | solution.py:545
  78.0 0.1 finish.7
  78.3 4.0 %collective-permute-start.24 = (bf16[160,256]{1,0:T(8,128)(2,1)S(1)}, bf16[160,256]{1,0:T(8,128)(2,1)S(1)}, u32[]{:S(2)}, u32[]{:S(2)}) collective-permute-start(bf16[160,256]{1,0:T(8,128)(2,1)S(1)} %get-tuple-element.87), channel_id=1, source_target_pairs={{0,6},{1,7},{2,4},{3,5},{4,10},{5,11},{6,8},{7,9},{8,14},{9,15},{1... | collective-permute-start | bytes 245768 | tf_op jit(solution)/shard_map/ppermute | solution.py:557
  82.3 2.3 %collective-permute-done.23.refs_8_ = bf16[480,256]{1,0:T(8,128)(2,1)S(1)} collective-permute-done((bf16[480,256]{1,0:T(8,128)(2,1)S(1)}, bf16[480,256]{1,0:T(8,128)(2,1)S(1)}, u32[]{:S(2)}, u32[]{:S(2)}) %collective-permute-start.23) | collective-permute-done | bytes 245792 | tf_op jit(solution)/shard_map/ppermute | solution.py:545
  84.6 0.7 collective-permute-done.19.refs_3_
  85.3 1.8 %collective-permute-done.20.refs_5_ = bf16[160,256]{1,0:T(8,128)(2,1)S(1)} collective-permute-done((bf16[160,256]{1,0:T(8,128)(2,1)S(1)}, bf16[160,256]{1,0:T(8,128)(2,1)S(1)}, u32[]{:S(2)}, u32[]{:S(2)}) %collective-permute-start.20) | collective-permute-done | bytes 81952 | tf_op jit(solution)/shard_map/ppermute | solution.py:192
  87.0 1.9 %collective-permute-done.24.refs_9_ = bf16[160,256]{1,0:T(8,128)(2,1)S(1)} collective-permute-done((bf16[160,256]{1,0:T(8,128)(2,1)S(1)}, bf16[160,256]{1,0:T(8,128)(2,1)S(1)}, u32[]{:S(2)}, u32[]{:S(2)}) %collective-permute-start.24) | collective-permute-done | bytes 81952 | tf_op jit(solution)/shard_map/ppermute | solution.py:557
  88.9 0.5 collective-permute-start.22
  89.4 1.1 collective-permute-done.22.refs_7_
  90.5 0.2 collective-permute-done.26.refs_11_
  90.7 8.8 %attention.1 = (bf16[640,128]{1,0:T(8,128)(2,1)S(1)}, f32[2,640,256]{2,1,0:T(8,128)S(1)}, bf16[2,640,256]{2,1,0:T(8,128)(2,1)S(1)}) custom-call(bf16[160,512]{1,0:T(8,128)(2,1)S(1)} %get-tuple-element.83.refs_0_, bf16[160,512]{1,0:T(8,128)(2,1)S(1)} %collective-permute-done.13.refs_1_, bf16[160,512]{1,0:T(8,128)(2,1)S(1)} %collective-permute-done.14.refs_2_, ...), custom_call_target="tpu_custom_call" | custom-call | tf_op jit(solution)/shard_map/attention/pallas_call | solution.py:212
  99.5 0.2 collective-permute-start.27
  99.8 1.9 %collective-permute-done.27 = bf16[2,640,256]{2,1,0:T(8,128)(2,1)S(1)} collective-permute-done((bf16[2,640,256]{2,1,0:T(8,128)(2,1)S(1)}, bf16[2,640,256]{2,1,0:T(8,128)(2,1)S(1)}, u32[]{:S(2)}, u32[]{:S(2)}) %collective-permute-start.27) | collective-permute-done | bytes 655392 | tf_op jit(solution)/shard_map/ppermute | solution.py:536
  101.7 0.1 convert_add_fusion
  101.9 0.7 collective-permute-start.28
  102.6 0.2 collective-permute-start.29
  102.8 1.2 collective-permute-start.30
  104.0 2.6 %collective-permute-start.31 = (bf16[160,128]{1,0:T(8,128)(2,1)S(1)}, bf16[160,128]{1,0:T(8,128)(2,1)S(1)}, u32[]{:S(2)}, u32[]{:S(2)}) collective-permute-start(bf16[160,128]{1,0:T(8,128)(2,1)S(1)} %get-tuple-element.107), channel_id=1, source_target_pairs={{0,12},{4,0},{8,4},{12,8},{1,13},{5,1},{9,5},{13,9},{2,14},{6,2},{... | collective-permute-start | bytes 122888 | tf_op jit(solution)/shard_map/ppermute | solution.py:192
  106.6 2.2 %collective-permute-done.29.refs_5_ = bf16[160,128]{1,0:T(8,128)(2,1)S(1)} collective-permute-done((bf16[160,128]{1,0:T(8,128)(2,1)S(1)}, bf16[160,128]{1,0:T(8,128)(2,1)S(1)}, u32[]{:S(2)}, u32[]{:S(2)}) %collective-permute-start.29) | collective-permute-done | bytes 40992 | tf_op jit(solution)/shard_map/ppermute | solution.py:192
  108.8 0.4 collective-permute-done.30.refs_6_
  109.3 2.4 %collective-permute-done.28 = bf16[640,256]{1,0:T(8,128)(2,1)S(1)} collective-permute-done((bf16[640,256]{1,0:T(8,128)(2,1)S(1)}, bf16[640,256]{1,0:T(8,128)(2,1)S(1)}, u32[]{:S(2)}, u32[]{:S(2)}) %collective-permute-start.28) | collective-permute-done | bytes 327712 | tf_op jit(solution)/shard_map/ppermute | solution.py:536
  111.9 1.3 collective-permute-start.33
  113.2 2.5 %collective-permute-start.34 = (bf16[160,256]{1,0:T(8,128)(2,1)S(1)}, bf16[160,256]{1,0:T(8,128)(2,1)S(1)}, u32[]{:S(2)}, u32[]{:S(2)}) collective-permute-start(bf16[160,256]{1,0:T(8,128)(2,1)S(1)} %get-tuple-element.103), channel_id=1, source_target_pairs={{0,12},{4,0},{8,4},{12,8},{1,13},{5,1},{9,5},{13,9},{2,14},{6,2},{... | collective-permute-start | bytes 245768 | tf_op jit(solution)/shard_map/ppermute | solution.py:192
  115.7 3.4 %collective-permute-done.32.refs_9_ = bf16[160,256]{1,0:T(8,128)(2,1)S(1)} collective-permute-done((bf16[160,256]{1,0:T(8,128)(2,1)S(1)}, bf16[160,256]{1,0:T(8,128)(2,1)S(1)}, u32[]{:S(2)}, u32[]{:S(2)}) %collective-permute-start.32) | collective-permute-done | bytes 81952 | tf_op jit(solution)/shard_map/ppermute | solution.py:192
  119.1 1.8 %collective-permute-done.33.refs_10_ = bf16[160,256]{1,0:T(8,128)(2,1)S(1)} collective-permute-done((bf16[160,256]{1,0:T(8,128)(2,1)S(1)}, bf16[160,256]{1,0:T(8,128)(2,1)S(1)}, u32[]{:S(2)}, u32[]{:S(2)}) %collective-permute-start.33) | collective-permute-done | bytes 81952 | tf_op jit(solution)/shard_map/ppermute | solution.py:192
  120.9 0.7 unfinish.1.grads
  121.7 1.9 %collective-permute-done.35.grads = bf16[160,1536]{1,0:T(8,128)(2,1)S(1)} collective-permute-done((bf16[160,1536]{1,0:T(8,128)(2,1)S(1)}, bf16[160,1536]{1,0:T(8,128)(2,1)S(1)}, u32[]{:S(2)}, u32[]{:S(2)}) %collective-permute-start.35) | collective-permute-done | bytes 491552 | tf_op jit(solution)/shard_map/ppermute | solution.py:536
  123.6 1.7 %back_project.3 = bf16[160,1792]{1,0:T(8,128)(2,1)S(1)} custom-call(bf16[160,1536]{1,0:T(8,128)(2,1)S(1)} %collective-permute-done.35.grads, bf16[1792,384]{1,0:T(8,128)(2,1)S(1)} %get-tuple-element.98.refs_0_, bf16[1792,384]{1,0:T(8,128)(2,1)S(1)} %get-tuple-element.99.refs_1_, bf16[1792,384]{1,0:T(8,128)(2,1)S(1)} %get-tuple-element.100.refs_2_, ...), custom_call_target="tpu_custom_call" | custom-call | tf_op jit(solution)/shard_map/back_project/pallas_call | solution.py:212
  125.3 0.2 collective-permute-start.36
  125.5 1.7 %back_project.2.own_ref = f32[160,1792]{1,0:T(8,128)S(1)} custom-call(bf16[160,1536]{1,0:T(8,128)(2,1)S(1)} %unfinish.1.grads, bf16[1792,384]{1,0:T(8,128)(2,1)S(1)} %get-tuple-element.98.refs_0_, bf16[1792,384]{1,0:T(8,128)(2,1)S(1)} %get-tuple-element.99.refs_1_, bf16[1792,384]{1,0:T(8,128)(2,1)S(1)} %get-tuple-element.100.refs_2_, ...), custom_call_target="tpu_custom_call" | custom-call | tf_op jit(solution)/shard_map/back_project/pallas_call | solution.py:212
  127.4 2.4 %close.1 = f32[160,3584]{1,0:T(8,128)} custom-call(f32[160,1792]{1,0:T(8,128)S(1)} %back_project.2.own_ref, bf16[160,1792]{1,0:T(8,128)(2,1)S(1)} %collective-permute-done.36.away_ref, bf16[160,3584]{1,0:T(8,128)(2,1)S(1)} %copy-done.1, bf16[160,3584]{1,0:T(8,128)(2,1)S(1)} %copy-done.3, f32[3,3584]{1,0:T(4,128)S(1)} %copy-done.5, ...), custom_call_target="tpu_custom_call" | custom-call | tf_op jit(solution)/shard_map/close/pallas_call | solution.py:212
  (50 shorter events, 0.9 us)
Async XLA Ops:
  0.0 5.1 %copy-start.1 = (bf16[160,3584]{1,0:T(8,128)(2,1)S(1)}, bf16[160,3584]{1,0:T(8,128)(2,1)}, u32[]{:S(2)}) copy-start(bf16[160,3584]{1,0:T(8,128)(2,1)} %x_ref.2) | copy-start | bytes 3440644
  0.0 5.1 %copy-start.5 = (f32[3,3584]{1,0:T(4,128)S(1)}, f32[3,3584]{1,0:T(4,128)}, u32[]{:S(2)}) copy-start(f32[3,3584]{1,0:T(4,128)} %mod_ref.3) | copy-start | bytes 129028
  0.0 20.7 %copy-start = (bf16[3584,3,128]{2,0,1:T(8,128)(2,1)S(1)}, bf16[3584,3,128]{2,0,1:T(8,128)(2,1)}, u32[]{:S(2)}) copy-start(bf16[3584,3,128]{2,0,1:T(8,128)(2,1)} %param.9) | copy-start | bytes 8257540
  2.1 15.8 %collective-permute-start = (bf16[4,448,128]{2,1,0:T(8,128)(2,1)}, bf16[4,448,128]{2,1,0:T(8,128)(2,1)S(1)}, u32[]{:S(2)}, u32[]{:S(2)}) collective-permute-start(bf16[4,448,128]{2,1,0:T(8,128)(2,1)} %pack.1), channel_id=1, source_target_pairs={{0,4},{4,8},{8,12},{12,0},{1,5},{5,9},{9,13},{13,1},{2,6},{6,10},{... | collective-permute-start | bytes 1376264 | tf_op jit(solution)/shard_map/ppermute | solution.py:192
  5.2 1.3 copy-start.2
  6.4 14.3 %copy-start.4 = (bf16[128,3584]{1,0:T(8,128)(2,1)S(1)}, bf16[128,3584]{1,0:T(8,128)(2,1)}, u32[]{:S(2)}) copy-start(bf16[128,3584]{1,0:T(8,128)(2,1)} %refs_1_.1) | copy-start | bytes 2752516
  17.9 2.8 %collective-permute-start.1 = (bf16[160,3584]{1,0:T(8,128)(2,1)S(1)}, bf16[160,3584]{1,0:T(8,128)(2,1)S(1)}, u32[]{:S(2)}, u32[]{:S(2)}) collective-permute-start(bf16[160,3584]{1,0:T(8,128)(2,1)S(1)} %get-tuple-element.57), channel_id=1, source_target_pairs={{0,1},{1,0},{2,3},{3,2},{4,5},{5,4},{6,7},{7,6},{8,9},{9,8},{10,11... | collective-permute-start | bytes 3440648 | tf_op jit(solution)/shard_map/ppermute | solution.py:536
  17.9 11.2 %copy-start.6 = (f32[2,128]{1,0:T(2,128)S(1)}, f32[2,128]{1,0:T(2,128)}, u32[]{:S(2)}) copy-start(f32[2,128]{1,0:T(2,128)} %gain_ref.9) | copy-start | bytes 3076
  17.9 17.1 %copy-start.7 = (bf16[4,448,128]{2,1,0:T(8,128)(2,1)S(1)}, bf16[4,448,128]{2,1,0:T(8,128)(2,1)}, u32[]{:S(2)}) copy-start(bf16[4,448,128]{2,1,0:T(8,128)(2,1)} %pack.1) | copy-start | bytes 1376260
  17.9 9.7 %collective-permute-start.3 = (bf16[4,448,128]{2,1,0:T(8,128)(2,1)S(1)}, bf16[4,448,128]{2,1,0:T(8,128)(2,1)S(1)}, u32[]{:S(2)}, u32[]{:S(2)}) collective-permute-start(bf16[4,448,128]{2,1,0:T(8,128)(2,1)S(1)} %collective-permute-done.refs_0_), channel_id=1, source_target_pairs={{0,2},{1,17},{2,0},{3,19},{16,18},{17,1},{18,16},{19,3},{4,6},{5,2... | collective-permute-start | bytes 1376264 | tf_op jit(solution)/shard_map/ppermute | solution.py:545
  19.5 14.4 %collective-permute-start.7 = (bf16[4,448,128]{2,1,0:T(8,128)(2,1)S(1)}, bf16[4,448,128]{2,1,0:T(8,128)(2,1)S(1)}, u32[]{:S(2)}, u32[]{:S(2)}) collective-permute-start(bf16[4,448,128]{2,1,0:T(8,128)(2,1)S(1)} %collective-permute-done.refs_0_), channel_id=1, source_target_pairs={{0,4},{4,8},{8,12},{12,0},{1,5},{5,9},{9,13},{13,1},{2,6},{6,10},{... | collective-permute-start | bytes 1376264 | tf_op jit(solution)/shard_map/ppermute | solution.py:192
  22.1 7.0 %collective-permute-start.2 = (f32[160,512]{1,0:T(8,128)S(1)}, f32[160,512]{1,0:T(8,128)S(1)}, u32[]{:S(2)}, u32[]{:S(2)}) collective-permute-start(f32[160,512]{1,0:T(8,128)S(1)} %get-tuple-element.59), channel_id=1, source_target_pairs={{0,1},{1,0},{2,3},{3,2},{4,5},{5,4},{6,7},{7,6},{8,9},{9,8},{10,11... | collective-permute-start | bytes 983048 | tf_op jit(solution)/shard_map/ppermute | solution.py:536
  22.3 12.7 %collective-permute-start.4 = (bf16[4,448,128]{2,1,0:T(8,128)(2,1)S(1)}, bf16[4,448,128]{2,1,0:T(8,128)(2,1)S(1)}, u32[]{:S(2)}, u32[]{:S(2)}) collective-permute-start(bf16[4,448,128]{2,1,0:T(8,128)(2,1)S(1)} %collective-permute-done.refs_0_), channel_id=1, source_target_pairs={{0,16},{1,3},{2,18},{3,1},{16,0},{17,19},{18,2},{19,17},{4,20},{5,... | collective-permute-start | bytes 1376264 | tf_op jit(solution)/shard_map/ppermute | solution.py:545
  27.6 8.9 %collective-permute-start.5 = (bf16[4,448,128]{2,1,0:T(8,128)(2,1)S(1)}, bf16[4,448,128]{2,1,0:T(8,128)(2,1)S(1)}, u32[]{:S(2)}, u32[]{:S(2)}) collective-permute-start(bf16[4,448,128]{2,1,0:T(8,128)(2,1)S(1)} %collective-permute-done.3.refs_1_), channel_id=1, source_target_pairs={{0,16},{1,3},{2,18},{3,1},{16,0},{17,19},{18,2},{19,17},{4,20},{5,... | collective-permute-start | bytes 1376264 | tf_op jit(solution)/shard_map/ppermute | solution.py:545
  33.9 9.9 %collective-permute-start.8 = (bf16[4,448,128]{2,1,0:T(8,128)(2,1)S(1)}, bf16[4,448,128]{2,1,0:T(8,128)(2,1)S(1)}, u32[]{:S(2)}, u32[]{:S(2)}) collective-permute-start(bf16[4,448,128]{2,1,0:T(8,128)(2,1)S(1)} %collective-permute-done.7.refs_0_), channel_id=1, source_target_pairs={{0,2},{1,17},{2,0},{3,19},{16,18},{17,1},{18,16},{19,3},{4,6},{5,2... | collective-permute-start | bytes 1376264 | tf_op jit(solution)/shard_map/ppermute | solution.py:545
  35.0 10.7 %collective-permute-start.12 = (bf16[4,448,128]{2,1,0:T(8,128)(2,1)S(1)}, bf16[4,448,128]{2,1,0:T(8,128)(2,1)S(1)}, u32[]{:S(2)}, u32[]{:S(2)}) collective-permute-start(bf16[4,448,128]{2,1,0:T(8,128)(2,1)S(1)} %copy-done.7), channel_id=1, source_target_pairs={{0,12},{4,0},{8,4},{12,8},{1,13},{5,1},{9,5},{13,9},{2,14},{6,2},{... | collective-permute-start | bytes 1376264 | tf_op jit(solution)/shard_map/ppermute | solution.py:192
  37.7 6.1 %collective-permute-start.6 = (f32[160,512]{1,0:T(8,128)S(1)}, f32[160,512]{1,0:T(8,128)S(1)}, u32[]{:S(2)}, u32[]{:S(2)}) collective-permute-start(f32[160,512]{1,0:T(8,128)S(1)} %get-tuple-element.63), channel_id=1, source_target_pairs={{0,1},{1,0},{2,3},{3,2},{4,5},{5,4},{6,7},{7,6},{8,9},{9,8},{10,11... | collective-permute-start | bytes 983048 | tf_op jit(solution)/shard_map/ppermute | solution.py:536
  37.8 10.0 %collective-permute-start.9 = (bf16[4,448,128]{2,1,0:T(8,128)(2,1)S(1)}, bf16[4,448,128]{2,1,0:T(8,128)(2,1)S(1)}, u32[]{:S(2)}, u32[]{:S(2)}) collective-permute-start(bf16[4,448,128]{2,1,0:T(8,128)(2,1)S(1)} %collective-permute-done.7.refs_0_), channel_id=1, source_target_pairs={{0,16},{1,3},{2,18},{3,1},{16,0},{17,19},{18,2},{19,17},{4,20},{5,... | collective-permute-start | bytes 1376264 | tf_op jit(solution)/shard_map/ppermute | solution.py:545
  43.8 11.3 %collective-permute-start.10 = (bf16[4,448,128]{2,1,0:T(8,128)(2,1)S(1)}, bf16[4,448,128]{2,1,0:T(8,128)(2,1)S(1)}, u32[]{:S(2)}, u32[]{:S(2)}) collective-permute-start(bf16[4,448,128]{2,1,0:T(8,128)(2,1)S(1)} %collective-permute-done.8.refs_1_), channel_id=1, source_target_pairs={{0,16},{1,3},{2,18},{3,1},{16,0},{17,19},{18,2},{19,17},{4,20},{5,... | collective-permute-start | bytes 1376264 | tf_op jit(solution)/shard_map/ppermute | solution.py:545
  45.7 5.3 %collective-permute-start.13 = (bf16[160,512]{1,0:T(8,128)(2,1)S(1)}, bf16[160,512]{1,0:T(8,128)(2,1)S(1)}, u32[]{:S(2)}, u32[]{:S(2)}) collective-permute-start(bf16[160,512]{1,0:T(8,128)(2,1)S(1)} %get-tuple-element.74), channel_id=1, source_target_pairs={{0,12},{4,0},{8,4},{12,8},{1,13},{5,1},{9,5},{13,9},{2,14},{6,2},{... | collective-permute-start | bytes 491528 | tf_op jit(solution)/shard_map/ppermute | solution.py:192
  51.0 13.3 %collective-permute-start.16 = (bf16[4,448,128]{2,1,0:T(8,128)(2,1)S(1)}, bf16[4,448,128]{2,1,0:T(8,128)(2,1)S(1)}, u32[]{:S(2)}, u32[]{:S(2)}) collective-permute-start(bf16[4,448,128]{2,1,0:T(8,128)(2,1)S(1)} %collective-permute-done.12.refs_0_), channel_id=1, source_target_pairs={{0,16},{1,3},{2,18},{3,1},{16,0},{17,19},{18,2},{19,17},{4,20},{5,... | collective-permute-start | bytes 1376264 | tf_op jit(solution)/shard_map/ppermute | solution.py:545
  52.7 11.5 %collective-permute-start.15 = (bf16[4,448,128]{2,1,0:T(8,128)(2,1)S(1)}, bf16[4,448,128]{2,1,0:T(8,128)(2,1)S(1)}, u32[]{:S(2)}, u32[]{:S(2)}) collective-permute-start(bf16[4,448,128]{2,1,0:T(8,128)(2,1)S(1)} %collective-permute-done.12.refs_0_), channel_id=1, source_target_pairs={{0,2},{1,17},{2,0},{3,19},{16,18},{17,1},{18,16},{19,3},{4,6},{5,2... | collective-permute-start | bytes 1376264 | tf_op jit(solution)/shard_map/ppermute | solution.py:545
  56.3 1.7 %collective-permute-start.11 = (f32[160,512]{1,0:T(8,128)S(1)}, f32[160,512]{1,0:T(8,128)S(1)}, u32[]{:S(2)}, u32[]{:S(2)}) collective-permute-start(f32[160,512]{1,0:T(8,128)S(1)} %get-tuple-element.69), channel_id=1, source_target_pairs={{0,1},{1,0},{2,3},{3,2},{4,5},{5,4},{6,7},{7,6},{8,9},{9,8},{10,11... | collective-permute-start | bytes 983048 | tf_op jit(solution)/shard_map/ppermute | solution.py:536
  64.3 10.5 %collective-permute-start.17 = (bf16[4,448,128]{2,1,0:T(8,128)(2,1)S(1)}, bf16[4,448,128]{2,1,0:T(8,128)(2,1)S(1)}, u32[]{:S(2)}, u32[]{:S(2)}) collective-permute-start(bf16[4,448,128]{2,1,0:T(8,128)(2,1)S(1)} %collective-permute-done.15.refs_1_), channel_id=1, source_target_pairs={{0,16},{1,3},{2,18},{3,1},{16,0},{17,19},{18,2},{19,17},{4,20},{5,... | collective-permute-start | bytes 1376264 | tf_op jit(solution)/shard_map/ppermute | solution.py:545
  66.0 8.8 %collective-permute-start.14 = (bf16[160,512]{1,0:T(8,128)(2,1)S(1)}, bf16[160,512]{1,0:T(8,128)(2,1)S(1)}, u32[]{:S(2)}, u32[]{:S(2)}) collective-permute-start(bf16[160,512]{1,0:T(8,128)(2,1)S(1)} %get-tuple-element.75), channel_id=1, source_target_pairs={{0,8},{4,12},{8,0},{12,4},{1,9},{5,13},{9,1},{13,5},{2,10},{6,14},... | collective-permute-start | bytes 491528 | tf_op jit(solution)/shard_map/ppermute | solution.py:192
  76.0 2.0 %collective-permute-start.18 = (f32[160,512]{1,0:T(8,128)S(1)}, f32[160,512]{1,0:T(8,128)S(1)}, u32[]{:S(2)}, u32[]{:S(2)}) collective-permute-start(f32[160,512]{1,0:T(8,128)S(1)} %get-tuple-element.81), channel_id=1, source_target_pairs={{0,1},{1,0},{2,3},{3,2},{4,5},{5,4},{6,7},{7,6},{8,9},{9,8},{10,11... | collective-permute-start | bytes 983048 | tf_op jit(solution)/shard_map/ppermute | solution.py:536
  76.2 8.4 %collective-permute-start.23 = (bf16[480,256]{1,0:T(8,128)(2,1)S(1)}, bf16[480,256]{1,0:T(8,128)(2,1)S(1)}, u32[]{:S(2)}, u32[]{:S(2)}) collective-permute-start(bf16[480,256]{1,0:T(8,128)(2,1)S(1)} %pad_maximum_fusion.refs_4_), channel_id=1, source_target_pairs={{0,2},{2,0},{1,3},{3,1},{4,6},{6,4},{5,7},{7,5},{8,10},{10,8},{9,1... | collective-permute-start | bytes 737288 | tf_op jit(solution)/shard_map/ppermute | solution.py:545
  78.2 7.1 %collective-permute-start.19 = (bf16[160,256]{1,0:T(8,128)(2,1)S(1)}, bf16[160,256]{1,0:T(8,128)(2,1)S(1)}, u32[]{:S(2)}, u32[]{:S(2)}) collective-permute-start(bf16[160,256]{1,0:T(8,128)(2,1)S(1)} %get-tuple-element.85), channel_id=1, source_target_pairs={{0,4},{4,8},{8,12},{12,0},{1,5},{5,9},{9,13},{13,1},{2,6},{6,10},{... | collective-permute-start | bytes 245768 | tf_op jit(solution)/shard_map/ppermute | solution.py:192
  78.2 8.8 %collective-permute-start.20 = (bf16[160,256]{1,0:T(8,128)(2,1)S(1)}, bf16[160,256]{1,0:T(8,128)(2,1)S(1)}, u32[]{:S(2)}, u32[]{:S(2)}) collective-permute-start(bf16[160,256]{1,0:T(8,128)(2,1)S(1)} %get-tuple-element.87), channel_id=1, source_target_pairs={{0,4},{4,8},{8,12},{12,0},{1,5},{5,9},{9,13},{13,1},{2,6},{6,10},{... | collective-permute-start | bytes 245768 | tf_op jit(solution)/shard_map/ppermute | solution.py:192
  78.3 10.6 %collective-permute-start.24 = (bf16[160,256]{1,0:T(8,128)(2,1)S(1)}, bf16[160,256]{1,0:T(8,128)(2,1)S(1)}, u32[]{:S(2)}, u32[]{:S(2)}) collective-permute-start(bf16[160,256]{1,0:T(8,128)(2,1)S(1)} %get-tuple-element.87), channel_id=1, source_target_pairs={{0,6},{1,7},{2,4},{3,5},{4,10},{5,11},{6,8},{7,9},{8,14},{9,15},{1... | collective-permute-start | bytes 245768 | tf_op jit(solution)/shard_map/ppermute | solution.py:557
  82.3 7.2 %collective-permute-start.21 = (bf16[480,256]{1,0:T(8,128)(2,1)S(1)}, bf16[480,256]{1,0:T(8,128)(2,1)S(1)}, u32[]{:S(2)}, u32[]{:S(2)}) collective-permute-start(bf16[480,256]{1,0:T(8,128)(2,1)S(1)} %pad_maximum_fusion.refs_4_), channel_id=1, source_target_pairs={{0,1},{1,0},{2,3},{3,2},{4,5},{5,4},{6,7},{7,6},{8,9},{9,8},{10,11... | collective-permute-start | bytes 737288 | tf_op jit(solution)/shard_map/ppermute | solution.py:536
  88.9 1.8 %collective-permute-start.25 = (bf16[480,256]{1,0:T(8,128)(2,1)S(1)}, bf16[480,256]{1,0:T(8,128)(2,1)S(1)}, u32[]{:S(2)}, u32[]{:S(2)}) collective-permute-start(bf16[480,256]{1,0:T(8,128)(2,1)S(1)} %collective-permute-done.23.refs_8_), channel_id=1, source_target_pairs={{0,1},{1,0},{2,3},{3,2},{4,5},{5,4},{6,7},{7,6},{8,9},{9,8},{10,11... | collective-permute-start | bytes 737288 | tf_op jit(solution)/shard_map/ppermute | solution.py:536
  88.9 1.6 %collective-permute-start.22 = (bf16[160,256]{1,0:T(8,128)(2,1)S(1)}, bf16[160,256]{1,0:T(8,128)(2,1)S(1)}, u32[]{:S(2)}, u32[]{:S(2)}) collective-permute-start(bf16[160,256]{1,0:T(8,128)(2,1)S(1)} %collective-permute-done.20.refs_5_), channel_id=1, source_target_pairs={{0,1},{1,0},{2,3},{3,2},{4,5},{5,4},{6,7},{7,6},{8,9},{9,8},{10,11... | collective-permute-start | bytes 245768 | tf_op jit(solution)/shard_map/ppermute | solution.py:536
  89.4 1.3 collective-permute-start.26
  99.5 2.2 %collective-permute-start.27 = (bf16[2,640,256]{2,1,0:T(8,128)(2,1)S(1)}, bf16[2,640,256]{2,1,0:T(8,128)(2,1)S(1)}, u32[]{:S(2)}, u32[]{:S(2)}) collective-permute-start(bf16[2,640,256]{2,1,0:T(8,128)(2,1)S(1)} %get-tuple-element.91), channel_id=1, source_target_pairs={{0,1},{1,0},{2,3},{3,2},{4,5},{5,4},{6,7},{7,6},{8,9},{9,8},{10,11... | collective-permute-start | bytes 1966088 | tf_op jit(solution)/shard_map/ppermute | solution.py:536
  101.9 9.8 %collective-permute-start.28 = (bf16[640,256]{1,0:T(8,128)(2,1)S(1)}, bf16[640,256]{1,0:T(8,128)(2,1)S(1)}, u32[]{:S(2)}, u32[]{:S(2)}) collective-permute-start(bf16[640,256]{1,0:T(8,128)(2,1)S(1)} %fusion.2), channel_id=1, source_target_pairs={{0,2},{2,0},{1,3},{3,1},{4,6},{6,4},{5,7},{7,5},{8,10},{10,8},{9,1... | collective-permute-start | bytes 983048 | tf_op jit(solution)/shard_map/ppermute | solution.py:536
  102.6 6.3 %collective-permute-start.29 = (bf16[160,128]{1,0:T(8,128)(2,1)S(1)}, bf16[160,128]{1,0:T(8,128)(2,1)S(1)}, u32[]{:S(2)}, u32[]{:S(2)}) collective-permute-start(bf16[160,128]{1,0:T(8,128)(2,1)S(1)} %get-tuple-element.109), channel_id=1, source_target_pairs={{0,4},{4,8},{8,12},{12,0},{1,5},{5,9},{9,13},{13,1},{2,6},{6,10},{... | collective-permute-start | bytes 122888 | tf_op jit(solution)/shard_map/ppermute | solution.py:192
  102.8 6.5 %collective-permute-start.30 = (bf16[160,128]{1,0:T(8,128)(2,1)S(1)}, bf16[160,128]{1,0:T(8,128)(2,1)S(1)}, u32[]{:S(2)}, u32[]{:S(2)}) collective-permute-start(bf16[160,128]{1,0:T(8,128)(2,1)S(1)} %get-tuple-element.108), channel_id=1, source_target_pairs={{0,8},{4,12},{8,0},{12,4},{1,9},{5,13},{9,1},{13,5},{2,10},{6,14},... | collective-permute-start | bytes 122888 | tf_op jit(solution)/shard_map/ppermute | solution.py:192
  104.0 5.2 %collective-permute-start.31 = (bf16[160,128]{1,0:T(8,128)(2,1)S(1)}, bf16[160,128]{1,0:T(8,128)(2,1)S(1)}, u32[]{:S(2)}, u32[]{:S(2)}) collective-permute-start(bf16[160,128]{1,0:T(8,128)(2,1)S(1)} %get-tuple-element.107), channel_id=1, source_target_pairs={{0,12},{4,0},{8,4},{12,8},{1,13},{5,1},{9,5},{13,9},{2,14},{6,2},{... | collective-permute-start | bytes 122888 | tf_op jit(solution)/shard_map/ppermute | solution.py:192
  111.8 7.2 %collective-permute-start.32 = (bf16[160,256]{1,0:T(8,128)(2,1)S(1)}, bf16[160,256]{1,0:T(8,128)(2,1)S(1)}, u32[]{:S(2)}, u32[]{:S(2)}) collective-permute-start(bf16[160,256]{1,0:T(8,128)(2,1)S(1)} %get-tuple-element.105), channel_id=1, source_target_pairs={{0,4},{4,8},{8,12},{12,0},{1,5},{5,9},{9,13},{13,1},{2,6},{6,10},{... | collective-permute-start | bytes 245768 | tf_op jit(solution)/shard_map/ppermute | solution.py:192
  111.9 9.0 %collective-permute-start.33 = (bf16[160,256]{1,0:T(8,128)(2,1)S(1)}, bf16[160,256]{1,0:T(8,128)(2,1)S(1)}, u32[]{:S(2)}, u32[]{:S(2)}) collective-permute-start(bf16[160,256]{1,0:T(8,128)(2,1)S(1)} %get-tuple-element.104), channel_id=1, source_target_pairs={{0,8},{4,12},{8,0},{12,4},{1,9},{5,13},{9,1},{13,5},{2,10},{6,14},... | collective-permute-start | bytes 245768 | tf_op jit(solution)/shard_map/ppermute | solution.py:192
  113.2 7.7 %collective-permute-start.34 = (bf16[160,256]{1,0:T(8,128)(2,1)S(1)}, bf16[160,256]{1,0:T(8,128)(2,1)S(1)}, u32[]{:S(2)}, u32[]{:S(2)}) collective-permute-start(bf16[160,256]{1,0:T(8,128)(2,1)S(1)} %get-tuple-element.103), channel_id=1, source_target_pairs={{0,12},{4,0},{8,4},{12,8},{1,13},{5,1},{9,5},{13,9},{2,14},{6,2},{... | collective-permute-start | bytes 245768 | tf_op jit(solution)/shard_map/ppermute | solution.py:192
  121.6 1.9 %collective-permute-start.35 = (bf16[160,1536]{1,0:T(8,128)(2,1)S(1)}, bf16[160,1536]{1,0:T(8,128)(2,1)S(1)}, u32[]{:S(2)}, u32[]{:S(2)}) collective-permute-start(bf16[160,1536]{1,0:T(8,128)(2,1)S(1)} %unfinish.1.grads), channel_id=1, source_target_pairs={{0,1},{1,0},{2,3},{3,2},{4,5},{5,4},{6,7},{7,6},{8,9},{9,8},{10,11... | collective-permute-start | bytes 1474568 | tf_op jit(solution)/shard_map/ppermute | solution.py:536
  125.3 2.1 %copy-start.3 = (bf16[160,3584]{1,0:T(8,128)(2,1)S(1)}, bf16[160,3584]{1,0:T(8,128)(2,1)}, u32[]{:S(2)}) copy-start(bf16[160,3584]{1,0:T(8,128)(2,1)} %c_ref.3) | copy-start | bytes 3440644
  125.3 2.0 %collective-permute-start.36 = (bf16[160,1792]{1,0:T(8,128)(2,1)S(1)}, bf16[160,1792]{1,0:T(8,128)(2,1)S(1)}, u32[]{:S(2)}, u32[]{:S(2)}) collective-permute-start(bf16[160,1792]{1,0:T(8,128)(2,1)S(1)} %back_project.3), channel_id=1, source_target_pairs={{0,1},{1,0},{2,3},{3,2},{4,5},{5,4},{6,7},{7,6},{8,9},{9,8},{10,11... | collective-permute-start | bytes 1720328 | tf_op jit(solution)/shard_map/ppermute | solution.py:536

commit v5 on v4

--- a/solution.py
+++ b/solution.py
@@ -226,21 +226,25 @@
 TN = (((0,), (0,)), ((), ()))
 
 
-def pack_kernel(w_in, w_out, packed, quarter, sems):
-    core, _, _, mine = place()
-    part, dim = packed.shape[1:]
+def pack_kernel(w_in, w_out, near, second, quarters, sems):
+    core = place()[0]
+    part, dim = near.shape[1:]
     half, tile = 4 * part, dim // 4
-    rows = pl.ds(pl.multiple_of(core * half + mine * part, tile), part)
-    copies = [pltpu.make_async_copy(w_in.at[j, rows, :], packed.at[j], sems.at[j]) for j in range(3)]
     lanes = pl.ds(pl.multiple_of(core * half, dim), half)
-    heads = pl.ds(pl.multiple_of(mine * tile, tile), tile)
-    copies.append(pltpu.make_async_copy(w_out.at[heads, lanes], quarter, sems.at[3]))
+    copies = []
+    for i, (packed, at) in enumerate(((near, arrivals()[0]), (second, arrivals()[2]))):
+        rows = pl.ds(pl.multiple_of(core * half + at * part, tile), part)
+        heads = pl.ds(pl.multiple_of(at * tile, tile), tile)
+        pairs = [(w_in.at[j, rows, :], packed.at[j]) for j in range(3)]
+        pairs.append((w_out.at[heads, lanes], quarters.at[i]))
+        copies += [pltpu.make_async_copy(s, d, sems.at[4 * i + j]) for j, (s, d) in enumerate(pairs)]
     for copy in copies:
         copy.start()
-    for copy in reversed(copies):
+    for copy in copies:
         copy.wait()
-    for i in range(part // tile):
-        packed[3, i * tile : (i + 1) * tile, :] = quarter[:, i * dim : (i + 1) * dim]
+    for i, packed in enumerate((near, second)):
+        for t in range(part // tile):
+            packed[3, t * tile : (t + 1) * tile, :] = quarters[i, :, t * dim : (t + 1) * dim]
 
 
 def pack(w_in, w_out):
@@ -249,12 +253,12 @@
     return call(
         pack_kernel,
         "pack",
-        [((4, part, dim), BF16)],
+        [((4, part, dim), BF16)] * 2,
         (w_in, w_out),
         60,
         far=(0, 1),
-        scratch=[pltpu.VMEM((dim // 4, 4 * part), BF16), pltpu.SemaphoreType.DMA((4,))],
-    )[0]
+        scratch=[pltpu.VMEM((2, dim // 4, 4 * part), BF16), pltpu.SemaphoreType.DMA((8,))],
+    )
 
 
 def front_kernel(x_ref, c_ref, mod_ref, keep_ref, send_ref, inv_ref):
@@ -366,81 +370,125 @@
     return call(finish_kernel, "finish", [((rows, 2 * dim), F32)] + ready, (own, come, gains), 6)
 
 
-def attention_kernel(scale, block, slots, *refs):
-    qgs, kvs = refs[:slots], refs[slots:-9]
-    dq_ref, stay_ref, send_ref, q_ref, g_ref, k_ref, v_ref, prob_ref, dprob_ref = refs[-9:]
-    total, dim = k_ref.shape
-    rows = q_ref.shape[0]
-    steps = total // block
+def key_terms(scale, at, rows, q_ref, g_ref, k_ref, prob_ref, dprob_ref, inverse, delta):
+    here = pl.ds(at, rows)
+    p = prob_ref[here, :] * inverse
+    ds = (p * (dprob_ref[here, :] - delta)).astype(BF16)
+    dk = jnp.dot(ds, q_ref[...], preferred_element_type=F32) * scale
+    dv = jnp.dot(p.astype(BF16), g_ref[...], preferred_element_type=F32)
+    dq = lax.dot_general(k_ref[here, :], ds, TN, preferred_element_type=F32)
+    return jnp.concatenate([dk, dv], axis=1), dq
+
+
+def attention_kernel(scale, slots, *refs):
+    qgs, kvs = refs[:slots], refs[slots:-15]
+    stay_ref, send_ref, q_ref, g_ref, near_k_ref, near_prob_ref, near_dprob_ref = refs[-15:-8]
+    stats_ref, dq_ref, near_v_ref, far_k_ref, far_v_ref, far_prob_ref, far_dprob_ref = refs[-8:-1]
+    top_ref = refs[-1]
+    rows, dim = q_ref.shape
     for i, qg in enumerate(qgs):
         at = pl.ds(i * qg.shape[0], qg.shape[0])
         q_ref[at, :] = qg[:, -2 * dim : -dim]
         g_ref[at, :] = qg[:, -dim:]
     at = 0
     for kv in kvs:
-        k_ref[pl.ds(at, kv.shape[0]), :] = kv[:, :dim]
-        v_ref[pl.ds(at, kv.shape[0]), :] = kv[:, dim:]
-        at += kv.shape[0]
-
-    def scores(i, top):
-        here = pl.ds(pl.multiple_of(i * block, block), block)
-        s = lax.dot_general(k_ref[here, :], q_ref[...], NT, preferred_element_type=F32) * scale
-        prob_ref[here, :] = s
-        dprob_ref[here, :] = lax.dot_general(
-            v_ref[here, :], g_ref[...], NT, preferred_element_type=F32
-        )
-        return jnp.maximum(top, jnp.max(s, axis=0, keepdims=True))
-
-    top = lax.fori_loop(0, steps, scores, jnp.full((1, rows), -jnp.inf, F32))
-
-    def weigh(i, carry):
-        norm, cross = carry
-        here = pl.ds(pl.multiple_of(i * block, block), block)
-        e = jnp.exp(prob_ref[here, :] - top)
-        prob_ref[here, :] = e
-        return (
-            norm + jnp.sum(e, axis=0, keepdims=True),
-            cross + jnp.sum(e * dprob_ref[here, :], axis=0, keepdims=True),
-        )
-
-    none = jnp.zeros((1, rows), F32)
-    norm, cross = lax.fori_loop(0, steps, weigh, (none, none))
+        size = kv.shape[0]
+        k_ref, v_ref = ((near_k_ref, near_v_ref), (far_k_ref, far_v_ref))[at // (2 * rows)]
+        to = pl.ds(at % (2 * rows), size)
+        k_ref[to, :] = kv[:, :dim]
+        v_ref[to, :] = kv[:, dim:]
+        at += size
+    near = (near_k_ref, near_v_ref, near_prob_ref, near_dprob_ref)
+    far = (far_k_ref, far_v_ref, far_prob_ref, far_dprob_ref)
+    top = jnp.full((1, rows), -jnp.inf, F32)
+    for k_ref, v_ref, prob_ref, dprob_ref in (near, far):
+
+        def scores(i, top):
+            here = pl.ds(pl.multiple_of(i * rows, rows), rows)
+            s = lax.dot_general(k_ref[here, :], q_ref[...], NT, preferred_element_type=F32)
+            prob_ref[here, :] = s
+            dprob_ref[here, :] = lax.dot_general(
+                v_ref[here, :], g_ref[...], NT, preferred_element_type=F32
+            )
+            return jnp.maximum(top, jnp.max(s, axis=0, keepdims=True))
+
+        top = lax.fori_loop(0, 2, scores, top)
+    power = scale * math.log2(math.e)
+    top_ref[...] = top * power
+    norm = cross = jnp.zeros((1, rows), F32)
+    for _, _, prob_ref, dprob_ref in (near, far):
+
+        def weigh(i, carry):
+            norm, cross = carry
+            here = pl.ds(pl.multiple_of(i * rows, rows), rows)
+            e = jnp.exp2(prob_ref[here, :] * power - top_ref[...])
+            prob_ref[here, :] = e
+            return (
+                norm + jnp.sum(e, axis=0, keepdims=True),
+                cross + jnp.sum(e * dprob_ref[here, :], axis=0, keepdims=True),
+            )
+
+        norm, cross = lax.fori_loop(0, 2, weigh, (norm, cross))
     inverse = 1.0 / norm
     delta = cross * inverse
+    stats_ref[0:1, :] = inverse
+    stats_ref[1:2, :] = delta
     dq = jnp.zeros((dim, rows), F32)
-    quarter = total // 4
-    for turn in range(4):
-        out_ref = (stay_ref, send_ref)[turn % 2]
-
-        def back(i, dq):
-            here = pl.ds(pl.multiple_of(turn * quarter + i * block, block), block)
-            to = pl.ds(pl.multiple_of(i * block, block), block)
-            p = prob_ref[here, :] * inverse
-            ds = (p * (dprob_ref[here, :] - delta)).astype(BF16)
-            dk = jnp.dot(ds, q_ref[...], preferred_element_type=F32) * scale
-            dv = jnp.dot(p.astype(BF16), g_ref[...], preferred_element_type=F32)
-            out_ref[turn // 2, to, :dim] = dk.astype(out_ref.dtype)
-            out_ref[turn // 2, to, dim:] = dv.astype(out_ref.dtype)
-            return dq + lax.dot_general(k_ref[here, :], ds, TN, preferred_element_type=F32)
-
-        dq = lax.fori_loop(0, quarter // block, back, dq)
-    dq_ref[...] = (dq.T * scale).astype(BF16)
+    for turn, out_ref in enumerate((stay_ref, send_ref)):
+        dkv, part = key_terms(
+            scale, turn * rows, rows, q_ref, g_ref, far_k_ref, far_prob_ref, far_dprob_ref, inverse, delta
+        )
+        out_ref[...] = dkv.astype(out_ref.dtype)
+        dq += part
+    dq_ref[...] = dq
 
 
 def attention(qgs, pieces):
     slots, dim = len(qgs), pieces[0][0].shape[1] // 2
     rows = sum(qg.shape[0] for qg in qgs)
-    total = 4 * rows
-    terms = (2, rows, 2 * dim)
+    keys, square = ((2 * rows, dim), BF16), ((2 * rows, rows), F32)
+    near = [((rows, dim), BF16)] * 2 + [keys, square, square, ((2, rows), F32), ((dim, rows), F32)]
+    stay, send, *near = call(
+        partial(attention_kernel, 1.0 / math.sqrt(dim), slots),
+        "attention",
+        [((rows, 2 * dim), F32), ((rows, 2 * dim), BF16), *near],
+        [*qgs, *[piece for some in pieces for piece in some]],
+        28,
+        scratch=[pltpu.VMEM(*kind) for kind in (keys, keys, keys, square, square, ((1, rows), F32))],
+    )
+    return stay, send, near
+
+
+def attention_near_kernel(scale, q_ref, g_ref, k_ref, prob_ref, dprob_ref, stats_ref, part_ref, *refs):
+    dq_ref, *terms = refs
+    rows = q_ref.shape[0]
+    dq = part_ref[...]
+    for turn, out_ref in enumerate(terms):
+        dkv, part = key_terms(
+            scale,
+            turn * rows,
+            rows,
+            q_ref,
+            g_ref,
+            k_ref,
+            prob_ref,
+            dprob_ref,
+            stats_ref[0:1, :],
+            stats_ref[1:2, :],
+        )
+        out_ref[...] = dkv.astype(out_ref.dtype)
+        dq += part
+    dq_ref[...] = (dq.T * scale).astype(BF16)
+
+
+def attention_near(near):
+    rows, dim = near[0].shape
     return call(
-        partial(attention_kernel, 1.0 / math.sqrt(dim), rows // 2, slots),
-        "attention",
-        [((rows, dim), BF16), (terms, F32), (terms, BF16)],
-        [*qgs, *[piece for some in pieces for piece in some]],
-        24,
-        scratch=[pltpu.VMEM((rows, dim), BF16)] * 2
-        + [pltpu.VMEM((total, dim), BF16)] * 2
-        + [pltpu.VMEM((total, rows), F32)] * 2,
+        partial(attention_near_kernel, 1.0 / math.sqrt(dim)),
+        "attention_near",
+        [((rows, dim), BF16), ((rows, 2 * dim), F32), ((rows, 2 * dim), BF16)],
+        near,
+        16,
     )
 
 
@@ -536,7 +584,7 @@
         return lax.ppermute(value, "seq", pairs)
 
     w_in = jnp.transpose(w_qkv, (1, 0, 2))
-    packed = pack(w_in, w_out)
+    packed, second = pack(w_in, w_out)
     keep, send, inv = front(after(tokens, packed), cotangent, modulation)
     came, swaps = packed, []
     raws, wholes, heads = [], [], []
@@ -562,21 +610,24 @@
             earlier = (heads[step][i],)
         return earlier
 
-    for step in range(1, count):
-        last = step == count - 1
-        came = around(after(packed, came), -1, count) if last else around(came, 1, count)
+    for step in range(1, count - 1):
+        came = around(came, 1, count)
         if step == 1:
             come = swap(after(send, came), CORE_SWAP)
         one = in_plane(came, PLANE, plane_swap(True), *([keep] if step == 1 else raws[: step - 1]))
-        sent = home(1, came) if last else ()
-        two = in_plane(came, PLANE, plane_swap(False), *sent)
-        far = in_plane(one, PLANE, plane_swap(False), *([two, raws[-1]] if last else ()))
+        two = in_plane(came, PLANE, plane_swap(False))
+        far = in_plane(one, PLANE, plane_swap(False))
         if step == 1:
             slot(0, [], (w_in, w_out))
-        if last:
-            for i in range(2, step):
-                sent = home(i, *sent)
-        slot(step, [came, one, two, far], (), *sent)
+        slot(step, [came, one, two, far], ())
+    near = around(after(packed, *swaps[:1]), -1, count)
+    one = in_plane(near, PLANE, plane_swap(True), *raws[: count - 2])
+    came = around(after(second, came), -1, count)
+    sent = home(1, near)
+    far = in_plane(came, PLANE, plane_swap(True), one, *sent)
+    for step in range(2, count - 1):
+        sent = home(step, *sent)
+    slot(count - 1, [near, one, came, far], (), *sent)
     kv, qg = after(heads[-1][0], *sent), after(heads[-1][1], *sent)
     turned = across(kv, 1 - count)
     heads[-1] = [around(kv, 1 - count, count), around(qg, 1 - count, count)]
@@ -590,12 +641,14 @@
     pieces = [[four[i] for four in pieces] for i in range(4)]
     qgs = [head[-1] for head in heads]
     slots = range(count)
-    dq, stay, send = attention(qgs, pieces)
+    stay, send, near = attention(qgs, pieces)
+    far = (stay + swap(send, CORE_SWAP).astype(F32)).astype(BF16)
+    dq, stay, send = attention_near(near)
     dq = dq.reshape(count, rows, dim)
     dqs = [around(dq[i], i, count) if i else dq[i] for i in slots]
     summed = stay + swap(send, CORE_SWAP).astype(F32)
-    came, *dqs = lax.optimization_barrier((swap(summed[1].astype(BF16), CHIP_SWAP), *dqs))
-    dkv = (summed[0] + came.astype(F32)).astype(BF16).reshape(count, rows, 2 * dim)
+    came, *dqs = lax.optimization_barrier((swap(far, CHIP_SWAP), *dqs))
+    dkv = (summed + came.astype(F32)).astype(BF16).reshape(count, rows, 2 * dim)
     dkvs = [around(dkv[i], i, count) if i else dkv[i] for i in slots]
 
     dqkv = unfinish(qk_gain, raws, dqs, dkvs)

time: 130 us -> 122 us (0.938)
  waiting for transfers between devices: 68.1 us -> 63.1 us
  starting transfers between devices: 35.3 us -> 32.4 us
  local copies, waits for them, and re-layouts: 1.38 us -> 3.43 us
  Pallas kernels: 24.4 us -> 22.7 us
    ppermute x13 -> x14, waiting for transfers between devices: 10.5 us -> 6.38 us  [swap(): return lax.ppermute(value, 'seq', pairs)]
    ppermute x1, starting transfers between devices: 3.96 us -> 0.71 us  [across(): return lax.ppermute(value, ('tensor', 'seq'), pairs)]
    ppermute x10 -> x9, waiting for transfers between devices: 17.1 us -> 19.5 us  [in_plane(): lax.ppermute(after(value, *swaps[:-2][-1:], *earlier), axes, pairs)]
    unnamed x16 -> x22, local copies, waits for them, and re-layouts: 1.29 us -> 3.37 us
    ppermute x1, waiting for transfers between devices: 1.87 us -> 0.01 us  [across(): return lax.ppermute(value, ('tensor', 'seq'), pairs)]
    pallas_call x15 -> x16, Pallas kernels: 24.4 us -> 22.7 us  [call(): pl.pallas_call(kernel, out_shape=out, in_specs=[hbm if i in far else vmem...]
    ppermute x10 -> x9, starting transfers between devices: 15.9 us -> 14.3 us  [in_plane(): lax.ppermute(after(value, *swaps[:-2][-1:], *earlier), axes, pairs)]
    ppermute x13 -> x14, waiting for transfers between devices: 38.7 us -> 37.2 us  [around(): lax.ppermute(value, 'tensor', [(i, (i + step) % count) for i in range(cou...]
  transfers between devices with their start and end apart: 37 -> 38, of which waited for: 25 -> 23; matrix products, arithmetic and copies ran while one was open for 0% -> 0% of each run, Pallas kernels for 6% -> 7%
where the time goes in v5:
time: 122 us
  waiting for transfers between devices  63.1 us (52%)
  starting transfers between devices  32.4 us (27%)
  Pallas kernels  22.7 us (19%)
  local copies, waits for them, and re-layouts  3.43 us (3%)
    ppermute x14, waiting for transfers between devices, around(): lax.ppermute(value, 'tensor', [(i, (i + step) % count) for i in range(cou...  37.2 us
    pallas_call x16, Pallas kernels, call(): pl.pallas_call(kernel, out_shape=out, in_specs=[hbm if i in far else vmem...  22.7 us
    ppermute x9, waiting for transfers between devices, in_plane(): lax.ppermute(after(value, *swaps[:-2][-1:], *earlier), axes, pairs)  19.5 us
    ppermute x14, starting transfers between devices, around(): lax.ppermute(value, 'tensor', [(i, (i + step) % count) for i in range(cou...  14.9 us
    ppermute x9, starting transfers between devices, in_plane(): lax.ppermute(after(value, *swaps[:-2][-1:], *earlier), axes, pairs)  14.3 us
    ppermute x14, waiting for transfers between devices, swap(): return lax.ppermute(value, 'seq', pairs)  6.38 us
    unnamed x22, local copies, waits for them, and re-layouts  3.37 us
    ppermute x14, starting transfers between devices, swap(): return lax.ppermute(value, 'seq', pairs)  2.56 us
  transfers between devices with their start and end apart: 38, of which 23 were waited for; matrix products, arithmetic and copies ran while one was open for 0% of the time, Pallas kernels for 7%

profile of v5, /device:TPU:0, one launch (start us, length us, event | category | flops | bytes accessed | tf_op | source)
XLA Modules:
  0.0 122.2 jit_solution(3337130045756390339)
XLA Ops:
  0.0 2.4 %pack.1 = (bf16[4,448,128]{2,1,0:T(8,128)(2,1)}, bf16[4,448,128]{2,1,0:T(8,128)(2,1)}) custom-call(bf16[3,3584,128]{2,1,0:T(8,128)(2,1)} %bitcast.1, bf16[128,3584]{1,0:T(8,128)(2,1)} %refs_1_.1), custom_call_target="tpu_custom_call" | custom-call | tf_op jit(solution)/shard_map/pack/pallas_call | solution.py:212
  2.5 3.1 %collective-permute-start = (bf16[4,448,128]{2,1,0:T(8,128)(2,1)}, bf16[4,448,128]{2,1,0:T(8,128)(2,1)S(1)}, u32[]{:S(2)}, u32[]{:S(2)}) collective-permute-start(bf16[4,448,128]{2,1,0:T(8,128)(2,1)} %get-tuple-element.85), channel_id=1, source_target_pairs={{0,4},{4,8},{8,12},{12,0},{1,5},{5,9},{9,13},{13,1},{2,6},{6,10},{... | collective-permute-start | bytes 1376264 | tf_op jit(solution)/shard_map/ppermute | solution.py:192
  5.5 1.3 %copy-done.1 = bf16[160,3584]{1,0:T(8,128)(2,1)S(1)} copy-done((bf16[160,3584]{1,0:T(8,128)(2,1)S(1)}, bf16[160,3584]{1,0:T(8,128)(2,1)}, u32[]{:S(2)}) %copy-start.1) | copy-done | bytes 1146904
  6.8 1.3 %copy-done.3 = bf16[160,3584]{1,0:T(8,128)(2,1)S(1)} copy-done((bf16[160,3584]{1,0:T(8,128)(2,1)S(1)}, bf16[160,3584]{1,0:T(8,128)(2,1)}, u32[]{:S(2)}) %copy-start.3) | copy-done | bytes 1146904
  8.1 0.8 copy-done.6
  8.9 1.3 %front.1 = (bf16[160,3584]{1,0:T(8,128)(2,1)S(1)}, bf16[160,3584]{1,0:T(8,128)(2,1)S(1)}, f32[160,1]{1,0:T(8,128)S(1)}) custom-call(bf16[160,3584]{1,0:T(8,128)(2,1)S(1)} %copy-done.1, bf16[160,3584]{1,0:T(8,128)(2,1)S(1)} %copy-done.3, f32[3,3584]{1,0:T(4,128)S(1)} %copy-done.6), custom_call_target="tpu_custom_call" | custom-call | tf_op jit(solution)/shard_map/front/pallas_call | solution.py:212
  10.2 8.1 %collective-permute-done.refs_0_ = bf16[4,448,128]{2,1,0:T(8,128)(2,1)S(1)} collective-permute-done((bf16[4,448,128]{2,1,0:T(8,128)(2,1)}, bf16[4,448,128]{2,1,0:T(8,128)(2,1)S(1)}, u32[]{:S(2)}, u32[]{:S(2)}) %collective-permute-start) | collective-permute-done | bytes 458784 | tf_op jit(solution)/shard_map/ppermute | solution.py:192
  18.3 1.6 %collective-permute-start.3 = (bf16[4,448,128]{2,1,0:T(8,128)(2,1)S(1)}, bf16[4,448,128]{2,1,0:T(8,128)(2,1)S(1)}, u32[]{:S(2)}, u32[]{:S(2)}) collective-permute-start(bf16[4,448,128]{2,1,0:T(8,128)(2,1)S(1)} %collective-permute-done.refs_0_), channel_id=1, source_target_pairs={{0,2},{1,17},{2,0},{3,19},{16,18},{17,1},{18,16},{19,3},{4,6},{5,2... | collective-permute-start | bytes 1376264 | tf_op jit(solution)/shard_map/ppermute | solution.py:593
  19.9 1.2 %collective-permute-done.1.come_ref = bf16[160,3584]{1,0:T(8,128)(2,1)S(1)} collective-permute-done((bf16[160,3584]{1,0:T(8,128)(2,1)S(1)}, bf16[160,3584]{1,0:T(8,128)(2,1)S(1)}, u32[]{:S(2)}, u32[]{:S(2)}) %collective-permute-start.1) | collective-permute-done | bytes 1146912 | tf_op jit(solution)/shard_map/ppermute | solution.py:584
  21.1 1.4 %project.4 = (f32[160,512]{1,0:T(8,128)S(1)}, f32[160,512]{1,0:T(8,128)S(1)}, bf16[1792,384]{1,0:T(8,128)(2,1)S(1)}) custom-call(bf16[160,3584]{1,0:T(8,128)(2,1)S(1)} %get-tuple-element.88.keep_ref, bf16[160,3584]{1,0:T(8,128)(2,1)S(1)} %collective-permute-done.1.come_ref, bf16[3,3584,128]{2,1,0:T(8,128)(2,1)S(1)} %bitcast.2, bf16[128,3584]{1,0:T(8,128)(2,1)S(1)} %copy-done.5), custom_call_target="tpu_custom_call" | custom-call | tf_op jit(solution)/shard_map/project/pallas_call | solution.py:212
  22.5 0.2 collective-permute-start.2
  22.7 1.5 %collective-permute-start.4 = (bf16[4,448,128]{2,1,0:T(8,128)(2,1)S(1)}, bf16[4,448,128]{2,1,0:T(8,128)(2,1)S(1)}, u32[]{:S(2)}, u32[]{:S(2)}) collective-permute-start(bf16[4,448,128]{2,1,0:T(8,128)(2,1)S(1)} %collective-permute-done.refs_0_), channel_id=1, source_target_pairs={{0,16},{1,3},{2,18},{3,1},{16,0},{17,19},{18,2},{19,17},{4,20},{5,... | collective-permute-start | bytes 1376264 | tf_op jit(solution)/shard_map/ppermute | solution.py:593
  24.2 3.8 %collective-permute-done.3.refs_1_ = bf16[4,448,128]{2,1,0:T(8,128)(2,1)S(1)} collective-permute-done((bf16[4,448,128]{2,1,0:T(8,128)(2,1)S(1)}, bf16[4,448,128]{2,1,0:T(8,128)(2,1)S(1)}, u32[]{:S(2)}, u32[]{:S(2)}) %collective-permute-start.3) | collective-permute-done | bytes 458784 | tf_op jit(solution)/shard_map/ppermute | solution.py:593
  28.0 1.5 %collective-permute-start.5 = (bf16[4,448,128]{2,1,0:T(8,128)(2,1)S(1)}, bf16[4,448,128]{2,1,0:T(8,128)(2,1)S(1)}, u32[]{:S(2)}, u32[]{:S(2)}) collective-permute-start(bf16[4,448,128]{2,1,0:T(8,128)(2,1)S(1)} %collective-permute-done.3.refs_1_), channel_id=1, source_target_pairs={{0,16},{1,3},{2,18},{3,1},{16,0},{17,19},{18,2},{19,17},{4,20},{5,... | collective-permute-start | bytes 1376264 | tf_op jit(solution)/shard_map/ppermute | solution.py:593
  29.5 0.1 finish.4
  29.6 4.6 %collective-permute-done.7.refs_0_ = bf16[4,448,128]{2,1,0:T(8,128)(2,1)S(1)} collective-permute-done((bf16[4,448,128]{2,1,0:T(8,128)(2,1)S(1)}, bf16[4,448,128]{2,1,0:T(8,128)(2,1)S(1)}, u32[]{:S(2)}, u32[]{:S(2)}) %collective-permute-start.7) | collective-permute-done | bytes 458784 | tf_op jit(solution)/shard_map/ppermute | solution.py:192
  34.3 1.1 collective-permute-start.8
  35.4 1.4 %collective-permute-done.5.refs_3_ = bf16[4,448,128]{2,1,0:T(8,128)(2,1)S(1)} collective-permute-done((bf16[4,448,128]{2,1,0:T(8,128)(2,1)S(1)}, bf16[4,448,128]{2,1,0:T(8,128)(2,1)S(1)}, u32[]{:S(2)}, u32[]{:S(2)}) %collective-permute-start.5) | collective-permute-done | bytes 458784 | tf_op jit(solution)/shard_map/ppermute | solution.py:593
  36.8 1.3 %project.5 = (f32[160,512]{1,0:T(8,128)S(1)}, f32[160,512]{1,0:T(8,128)S(1)}, bf16[1792,384]{1,0:T(8,128)(2,1)S(1)}) custom-call(bf16[160,3584]{1,0:T(8,128)(2,1)S(1)} %get-tuple-element.88.keep_ref, bf16[160,3584]{1,0:T(8,128)(2,1)S(1)} %collective-permute-done.1.come_ref, bf16[4,448,128]{2,1,0:T(8,128)(2,1)S(1)} %collective-permute-done.refs_0_, ...), custom_call_target="tpu_custom_call" | custom-call | tf_op jit(solution)/shard_map/project/pallas_call | solution.py:212
  38.2 2.5 %collective-permute-start.9 = (bf16[4,448,128]{2,1,0:T(8,128)(2,1)S(1)}, bf16[4,448,128]{2,1,0:T(8,128)(2,1)S(1)}, u32[]{:S(2)}, u32[]{:S(2)}) collective-permute-start(bf16[4,448,128]{2,1,0:T(8,128)(2,1)S(1)} %collective-permute-done.7.refs_0_), channel_id=1, source_target_pairs={{0,16},{1,3},{2,18},{3,1},{16,0},{17,19},{18,2},{19,17},{4,20},{5,... | collective-permute-start | bytes 1376264 | tf_op jit(solution)/shard_map/ppermute | solution.py:593
  40.7 3.4 %collective-permute-done.8.refs_1_ = bf16[4,448,128]{2,1,0:T(8,128)(2,1)S(1)} collective-permute-done((bf16[4,448,128]{2,1,0:T(8,128)(2,1)S(1)}, bf16[4,448,128]{2,1,0:T(8,128)(2,1)S(1)}, u32[]{:S(2)}, u32[]{:S(2)}) %collective-permute-start.8) | collective-permute-done | bytes 458784 | tf_op jit(solution)/shard_map/ppermute | solution.py:593
  44.2 1.1 collective-permute-start.16
  45.3 0.1 finish.5
  45.4 1.3 %collective-permute-done.12.refs_0_ = bf16[4,448,128]{2,1,0:T(8,128)(2,1)S(1)} collective-permute-done((bf16[4,448,128]{2,1,0:T(8,128)(2,1)S(1)}, bf16[4,448,128]{2,1,0:T(8,128)(2,1)S(1)}, u32[]{:S(2)}, u32[]{:S(2)}) %collective-permute-start.12) | collective-permute-done | bytes 458784 | tf_op jit(solution)/shard_map/ppermute | solution.py:192
  46.7 3.0 %collective-permute-start.15 = (bf16[4,448,128]{2,1,0:T(8,128)(2,1)S(1)}, bf16[4,448,128]{2,1,0:T(8,128)(2,1)S(1)}, u32[]{:S(2)}, u32[]{:S(2)}) collective-permute-start(bf16[4,448,128]{2,1,0:T(8,128)(2,1)S(1)} %collective-permute-done.12.refs_0_), channel_id=1, source_target_pairs={{0,2},{1,17},{2,0},{3,19},{16,18},{17,1},{18,16},{19,3},{4,6},{5,2... | collective-permute-start | bytes 1376264 | tf_op jit(solution)/shard_map/ppermute | solution.py:593
  49.8 0.5 collective-permute-start.13
  50.3 7.1 %collective-permute-done.10.refs_3_ = bf16[4,448,128]{2,1,0:T(8,128)(2,1)S(1)} collective-permute-done((bf16[4,448,128]{2,1,0:T(8,128)(2,1)S(1)}, bf16[4,448,128]{2,1,0:T(8,128)(2,1)S(1)}, u32[]{:S(2)}, u32[]{:S(2)}) %collective-permute-start.10) | collective-permute-done | bytes 458784 | tf_op jit(solution)/shard_map/ppermute | solution.py:593
  57.4 1.3 %project.6 = (f32[160,512]{1,0:T(8,128)S(1)}, f32[160,512]{1,0:T(8,128)S(1)}, bf16[1792,384]{1,0:T(8,128)(2,1)S(1)}) custom-call(bf16[160,3584]{1,0:T(8,128)(2,1)S(1)} %get-tuple-element.88.keep_ref, bf16[160,3584]{1,0:T(8,128)(2,1)S(1)} %collective-permute-done.1.come_ref, bf16[4,448,128]{2,1,0:T(8,128)(2,1)S(1)} %collective-permute-done.7.refs_0_, ...), custom_call_target="tpu_custom_call" | custom-call | tf_op jit(solution)/shard_map/project/pallas_call | solution.py:212
  58.8 0.7 collective-permute-done.13.refs_1_
  59.5 1.9 %collective-permute-start.17 = (bf16[4,448,128]{2,1,0:T(8,128)(2,1)S(1)}, bf16[4,448,128]{2,1,0:T(8,128)(2,1)S(1)}, u32[]{:S(2)}, u32[]{:S(2)}) collective-permute-start(bf16[4,448,128]{2,1,0:T(8,128)(2,1)S(1)} %collective-permute-done.16.refs_2_), channel_id=1, source_target_pairs={{0,2},{1,17},{2,0},{3,19},{16,18},{17,1},{18,16},{19,3},{4,6},{5,2... | collective-permute-start | bytes 1376264 | tf_op jit(solution)/shard_map/ppermute | solution.py:593
  61.3 0.1 finish.6
  61.5 1.1 collective-permute-start.14
  62.6 8.7 %collective-permute-done.14.refs_2_ = bf16[160,512]{1,0:T(8,128)(2,1)S(1)} collective-permute-done((bf16[160,512]{1,0:T(8,128)(2,1)S(1)}, bf16[160,512]{1,0:T(8,128)(2,1)S(1)}, u32[]{:S(2)}, u32[]{:S(2)}) %collective-permute-start.14) | collective-permute-done | bytes 163872 | tf_op jit(solution)/shard_map/ppermute | solution.py:192
  71.3 1.3 %project.7 = (f32[160,512]{1,0:T(8,128)S(1)}, f32[160,512]{1,0:T(8,128)S(1)}, bf16[1792,384]{1,0:T(8,128)(2,1)S(1)}) custom-call(bf16[160,3584]{1,0:T(8,128)(2,1)S(1)} %get-tuple-element.88.keep_ref, bf16[160,3584]{1,0:T(8,128)(2,1)S(1)} %collective-permute-done.1.come_ref, bf16[4,448,128]{2,1,0:T(8,128)(2,1)S(1)} %collective-permute-done.12.refs_0_, ...), custom_call_target="tpu_custom_call" | custom-call | tf_op jit(solution)/shard_map/project/pallas_call | solution.py:212
  72.7 1.1 collective-permute-start.23
  73.8 0.4 collective-permute-done.18.come_ref
  74.2 0.1 finish.7
  74.4 0.7 collective-permute-start.24
  75.1 3.9 %collective-permute-start.19 = (bf16[160,256]{1,0:T(8,128)(2,1)S(1)}, bf16[160,256]{1,0:T(8,128)(2,1)S(1)}, u32[]{:S(2)}, u32[]{:S(2)}) collective-permute-start(bf16[160,256]{1,0:T(8,128)(2,1)S(1)} %get-tuple-element.98), channel_id=1, source_target_pairs={{0,4},{4,8},{8,12},{12,0},{1,5},{5,9},{9,13},{13,1},{2,6},{6,10},{... | collective-permute-start | bytes 245768 | tf_op jit(solution)/shard_map/ppermute | solution.py:192
  79.1 3.8 %collective-permute-done.23.refs_8_ = bf16[480,256]{1,0:T(8,128)(2,1)S(1)} collective-permute-done((bf16[480,256]{1,0:T(8,128)(2,1)S(1)}, bf16[480,256]{1,0:T(8,128)(2,1)S(1)}, u32[]{:S(2)}, u32[]{:S(2)}) %collective-permute-start.23) | collective-permute-done | bytes 245792 | tf_op jit(solution)/shard_map/ppermute | solution.py:593
  82.9 0.9 collective-permute-done.20.refs_5_
  83.8 1.0 collective-permute-done.19.refs_3_
  84.8 0.5 collective-permute-start.26
  85.3 1.1 collective-permute-done.26.refs_11_
  86.4 0.2 collective-permute-done.22.refs_7_
  86.5 5.3 %attention.1 = (f32[640,256]{1,0:T(8,128)S(1)}, bf16[640,256]{1,0:T(8,128)(2,1)S(1)}, bf16[640,128]{1,0:T(8,128)(2,1)S(1)}, bf16[640,128]{1,0:T(8,128)(2,1)S(1)}...) custom-call(bf16[160,512]{1,0:T(8,128)(2,1)S(1)} %get-tuple-element., ...), custom_call_target="tpu_custom_call" | custom-call | tf_op jit(solution)/shard_map/attention/pallas_call | solution.py:212
  91.9 0.2 collective-permute-start.27
  92.1 1.5 %collective-permute-done.27 = bf16[640,256]{1,0:T(8,128)(2,1)S(1)} collective-permute-done((bf16[640,256]{1,0:T(8,128)(2,1)S(1)}, bf16[640,256]{1,0:T(8,128)(2,1)S(1)}, u32[]{:S(2)}, u32[]{:S(2)}) %collective-permute-start.27) | collective-permute-done | bytes 327712 | tf_op jit(solution)/shard_map/ppermute | solution.py:584
  93.6 1.1 collective-permute-start.28
  94.7 1.4 %attention_near.1 = (bf16[640,128]{1,0:T(8,128)(2,1)S(1)}, f32[640,256]{1,0:T(8,128)S(1)}, bf16[640,256]{1,0:T(8,128)(2,1)S(1)}) custom-call(bf16[640,128]{1,0:T(8,128)(2,1)S(1)} %get-tuple-element.105.q_ref, bf16[640,128]{1,0:T(8,128)(2,1)S(1)} %get-tuple-element.106.g_ref, bf16[1280,128]{1,0:T(8,128)(2,1)S(1)} %get-tuple-element.107.k_ref, ...), custom_call_target="tpu_custom_call" | custom-call | tf_op jit(solution)/shard_map/attention_near/pallas_call | solution.py:212
  96.2 1.7 %collective-permute-start.31 = (bf16[160,128]{1,0:T(8,128)(2,1)S(1)}, bf16[160,128]{1,0:T(8,128)(2,1)S(1)}, u32[]{:S(2)}, u32[]{:S(2)}) collective-permute-start(bf16[160,128]{1,0:T(8,128)(2,1)S(1)} %get-tuple-element.129), channel_id=1, source_target_pairs={{0,12},{4,0},{8,4},{12,8},{1,13},{5,1},{9,5},{13,9},{2,14},{6,2},{... | collective-permute-start | bytes 122888 | tf_op jit(solution)/shard_map/ppermute | solution.py:192
  97.9 0.6 collective-permute-start.29
  98.5 1.7 %collective-permute-done.31.refs_7_ = bf16[160,128]{1,0:T(8,128)(2,1)S(1)} collective-permute-done((bf16[160,128]{1,0:T(8,128)(2,1)S(1)}, bf16[160,128]{1,0:T(8,128)(2,1)S(1)}, u32[]{:S(2)}, u32[]{:S(2)}) %collective-permute-start.31) | collective-permute-done | bytes 40992 | tf_op jit(solution)/shard_map/ppermute | solution.py:192
  100.2 3.8 %collective-permute-done.30.refs_6_ = bf16[160,128]{1,0:T(8,128)(2,1)S(1)} collective-permute-done((bf16[160,128]{1,0:T(8,128)(2,1)S(1)}, bf16[160,128]{1,0:T(8,128)(2,1)S(1)}, u32[]{:S(2)}, u32[]{:S(2)}) %collective-permute-start.30) | collective-permute-done | bytes 40992 | tf_op jit(solution)/shard_map/ppermute | solution.py:192
  104.2 1.1 collective-permute-start.35
  105.3 1.7 %collective-permute-start.33 = (bf16[160,256]{1,0:T(8,128)(2,1)S(1)}, bf16[160,256]{1,0:T(8,128)(2,1)S(1)}, u32[]{:S(2)}, u32[]{:S(2)}) collective-permute-start(bf16[160,256]{1,0:T(8,128)(2,1)S(1)} %get-tuple-element.127), channel_id=1, source_target_pairs={{0,4},{4,8},{8,12},{12,0},{1,5},{5,9},{9,13},{13,1},{2,6},{6,10},{... | collective-permute-start | bytes 245768 | tf_op jit(solution)/shard_map/ppermute | solution.py:192
  107.0 2.5 %collective-permute-done.35.refs_11_ = bf16[160,256]{1,0:T(8,128)(2,1)S(1)} collective-permute-done((bf16[160,256]{1,0:T(8,128)(2,1)S(1)}, bf16[160,256]{1,0:T(8,128)(2,1)S(1)}, u32[]{:S(2)}, u32[]{:S(2)}) %collective-permute-start.35) | collective-permute-done | bytes 81952 | tf_op jit(solution)/shard_map/ppermute | solution.py:192
  109.6 3.7 %collective-permute-done.34.refs_10_ = bf16[160,256]{1,0:T(8,128)(2,1)S(1)} collective-permute-done((bf16[160,256]{1,0:T(8,128)(2,1)S(1)}, bf16[160,256]{1,0:T(8,128)(2,1)S(1)}, u32[]{:S(2)}, u32[]{:S(2)}) %collective-permute-start.34) | collective-permute-done | bytes 81952 | tf_op jit(solution)/shard_map/ppermute | solution.py:192
  113.3 0.7 unfinish.1.grads
  114.1 1.9 %collective-permute-done.36.grads = bf16[160,1536]{1,0:T(8,128)(2,1)S(1)} collective-permute-done((bf16[160,1536]{1,0:T(8,128)(2,1)S(1)}, bf16[160,1536]{1,0:T(8,128)(2,1)S(1)}, u32[]{:S(2)}, u32[]{:S(2)}) %collective-permute-start.36) | collective-permute-done | bytes 491552 | tf_op jit(solution)/shard_map/ppermute | solution.py:584
  116.0 1.7 %back_project.3 = bf16[160,1792]{1,0:T(8,128)(2,1)S(1)} custom-call(bf16[160,1536]{1,0:T(8,128)(2,1)S(1)} %collective-permute-done.36.grads, bf16[1792,384]{1,0:T(8,128)(2,1)S(1)} %get-tuple-element.120.refs_0_, bf16[1792,384]{1,0:T(8,128)(2,1)S(1)} %get-tuple-element.121.refs_1_, bf16[1792,384]{1,0:T(8,128)(2,1)S(1)} %get-tuple-element.122.refs_2_, ...), custom_call_target="tpu_custom_call" | custom-call | tf_op jit(solution)/shard_map/back_project/pallas_call | solution.py:212
  117.8 0.2 collective-permute-start.37
  118.0 1.7 %back_project.2.own_ref = f32[160,1792]{1,0:T(8,128)S(1)} custom-call(bf16[160,1536]{1,0:T(8,128)(2,1)S(1)} %unfinish.1.grads, bf16[1792,384]{1,0:T(8,128)(2,1)S(1)} %get-tuple-element.120.refs_0_, bf16[1792,384]{1,0:T(8,128)(2,1)S(1)} %get-tuple-element.121.refs_1_, bf16[1792,384]{1,0:T(8,128)(2,1)S(1)} %get-tuple-element.122.refs_2_, ...), custom_call_target="tpu_custom_call" | custom-call | tf_op jit(solution)/shard_map/back_project/pallas_call | solution.py:212
  119.8 2.4 %close.1 = f32[160,3584]{1,0:T(8,128)} custom-call(f32[160,1792]{1,0:T(8,128)S(1)} %back_project.2.own_ref, bf16[160,1792]{1,0:T(8,128)(2,1)S(1)} %collective-permute-done.37.away_ref, bf16[160,3584]{1,0:T(8,128)(2,1)S(1)} %copy-done.2, bf16[160,3584]{1,0:T(8,128)(2,1)S(1)} %copy-done.4, f32[3,3584]{1,0:T(4,128)S(1)} %copy-done.7, ...), custom_call_target="tpu_custom_call" | custom-call | tf_op jit(solution)/shard_map/close/pallas_call | solution.py:212
  (58 shorter events, 0.9 us)
Async XLA Ops:
  0.0 21.1 %copy-start = (bf16[3584,3,128]{2,0,1:T(8,128)(2,1)S(1)}, bf16[3584,3,128]{2,0,1:T(8,128)(2,1)}, u32[]{:S(2)}) copy-start(bf16[3584,3,128]{2,0,1:T(8,128)(2,1)} %param.9) | copy-start | bytes 8257540
  0.0 21.1 %copy-start.5 = (bf16[128,3584]{1,0:T(8,128)(2,1)S(1)}, bf16[128,3584]{1,0:T(8,128)(2,1)}, u32[]{:S(2)}) copy-start(bf16[128,3584]{1,0:T(8,128)(2,1)} %refs_1_.1) | copy-start | bytes 2752516
  2.5 15.8 %collective-permute-start = (bf16[4,448,128]{2,1,0:T(8,128)(2,1)}, bf16[4,448,128]{2,1,0:T(8,128)(2,1)S(1)}, u32[]{:S(2)}, u32[]{:S(2)}) collective-permute-start(bf16[4,448,128]{2,1,0:T(8,128)(2,1)} %get-tuple-element.85), channel_id=1, source_target_pairs={{0,4},{4,8},{8,12},{12,0},{1,5},{5,9},{9,13},{13,1},{2,6},{6,10},{... | collective-permute-start | bytes 1376264 | tf_op jit(solution)/shard_map/ppermute | solution.py:192
  5.5 1.3 %copy-start.1 = (bf16[160,3584]{1,0:T(8,128)(2,1)S(1)}, bf16[160,3584]{1,0:T(8,128)(2,1)}, u32[]{:S(2)}) copy-start(bf16[160,3584]{1,0:T(8,128)(2,1)} %x_ref.2) | copy-start | bytes 3440644
  6.8 1.3 %copy-start.3 = (bf16[160,3584]{1,0:T(8,128)(2,1)S(1)}, bf16[160,3584]{1,0:T(8,128)(2,1)}, u32[]{:S(2)}) copy-start(bf16[160,3584]{1,0:T(8,128)(2,1)} %c_ref.3) | copy-start | bytes 3440644
  8.1 0.8 copy-start.6
  18.3 2.8 %collective-permute-start.1 = (bf16[160,3584]{1,0:T(8,128)(2,1)S(1)}, bf16[160,3584]{1,0:T(8,128)(2,1)S(1)}, u32[]{:S(2)}, u32[]{:S(2)}) collective-permute-start(bf16[160,3584]{1,0:T(8,128)(2,1)S(1)} %get-tuple-element.69), channel_id=1, source_target_pairs={{0,1},{1,0},{2,3},{3,2},{4,5},{5,4},{6,7},{7,6},{8,9},{9,8},{10,11... | collective-permute-start | bytes 3440648 | tf_op jit(solution)/shard_map/ppermute | solution.py:584
  18.3 11.2 %copy-start.8 = (f32[2,128]{1,0:T(2,128)S(1)}, f32[2,128]{1,0:T(2,128)}, u32[]{:S(2)}) copy-start(f32[2,128]{1,0:T(2,128)} %gain_ref.9) | copy-start | bytes 3076
  18.3 17.1 %copy-start.10 = (bf16[4,448,128]{2,1,0:T(8,128)(2,1)S(1)}, bf16[4,448,128]{2,1,0:T(8,128)(2,1)}, u32[]{:S(2)}) copy-start(bf16[4,448,128]{2,1,0:T(8,128)(2,1)} %get-tuple-element.85) | copy-start | bytes 1376260
  18.3 9.7 %collective-permute-start.3 = (bf16[4,448,128]{2,1,0:T(8,128)(2,1)S(1)}, bf16[4,448,128]{2,1,0:T(8,128)(2,1)S(1)}, u32[]{:S(2)}, u32[]{:S(2)}) collective-permute-start(bf16[4,448,128]{2,1,0:T(8,128)(2,1)S(1)} %collective-permute-done.refs_0_), channel_id=1, source_target_pairs={{0,2},{1,17},{2,0},{3,19},{16,18},{17,1},{18,16},{19,3},{4,6},{5,2... | collective-permute-start | bytes 1376264 | tf_op jit(solution)/shard_map/ppermute | solution.py:593
  19.9 14.4 %collective-permute-start.7 = (bf16[4,448,128]{2,1,0:T(8,128)(2,1)S(1)}, bf16[4,448,128]{2,1,0:T(8,128)(2,1)S(1)}, u32[]{:S(2)}, u32[]{:S(2)}) collective-permute-start(bf16[4,448,128]{2,1,0:T(8,128)(2,1)S(1)} %collective-permute-done.refs_0_), channel_id=1, source_target_pairs={{0,4},{4,8},{8,12},{12,0},{1,5},{5,9},{9,13},{13,1},{2,6},{6,10},{... | collective-permute-start | bytes 1376264 | tf_op jit(solution)/shard_map/ppermute | solution.py:192
  22.5 7.0 %collective-permute-start.2 = (f32[160,512]{1,0:T(8,128)S(1)}, f32[160,512]{1,0:T(8,128)S(1)}, u32[]{:S(2)}, u32[]{:S(2)}) collective-permute-start(f32[160,512]{1,0:T(8,128)S(1)} %get-tuple-element.71), channel_id=1, source_target_pairs={{0,1},{1,0},{2,3},{3,2},{4,5},{5,4},{6,7},{7,6},{8,9},{9,8},{10,11... | collective-permute-start | bytes 983048 | tf_op jit(solution)/shard_map/ppermute | solution.py:584
  22.7 12.7 %collective-permute-start.4 = (bf16[4,448,128]{2,1,0:T(8,128)(2,1)S(1)}, bf16[4,448,128]{2,1,0:T(8,128)(2,1)S(1)}, u32[]{:S(2)}, u32[]{:S(2)}) collective-permute-start(bf16[4,448,128]{2,1,0:T(8,128)(2,1)S(1)} %collective-permute-done.refs_0_), channel_id=1, source_target_pairs={{0,16},{1,3},{2,18},{3,1},{16,0},{17,19},{18,2},{19,17},{4,20},{5,... | collective-permute-start | bytes 1376264 | tf_op jit(solution)/shard_map/ppermute | solution.py:593
  28.0 8.9 %collective-permute-start.5 = (bf16[4,448,128]{2,1,0:T(8,128)(2,1)S(1)}, bf16[4,448,128]{2,1,0:T(8,128)(2,1)S(1)}, u32[]{:S(2)}, u32[]{:S(2)}) collective-permute-start(bf16[4,448,128]{2,1,0:T(8,128)(2,1)S(1)} %collective-permute-done.3.refs_1_), channel_id=1, source_target_pairs={{0,16},{1,3},{2,18},{3,1},{16,0},{17,19},{18,2},{19,17},{4,20},{5,... | collective-permute-start | bytes 1376264 | tf_op jit(solution)/shard_map/ppermute | solution.py:593
  34.3 9.9 %copy-start.9 = (bf16[4,448,128]{2,1,0:T(8,128)(2,1)S(1)}, bf16[4,448,128]{2,1,0:T(8,128)(2,1)}, u32[]{:S(2)}) copy-start(bf16[4,448,128]{2,1,0:T(8,128)(2,1)} %get-tuple-element.91) | copy-start | bytes 1376260
  34.3 9.9 %collective-permute-start.8 = (bf16[4,448,128]{2,1,0:T(8,128)(2,1)S(1)}, bf16[4,448,128]{2,1,0:T(8,128)(2,1)S(1)}, u32[]{:S(2)}, u32[]{:S(2)}) collective-permute-start(bf16[4,448,128]{2,1,0:T(8,128)(2,1)S(1)} %collective-permute-done.7.refs_0_), channel_id=1, source_target_pairs={{0,2},{1,17},{2,0},{3,19},{16,18},{17,1},{18,16},{19,3},{4,6},{5,2... | collective-permute-start | bytes 1376264 | tf_op jit(solution)/shard_map/ppermute | solution.py:593
  35.4 11.3 %collective-permute-start.12 = (bf16[4,448,128]{2,1,0:T(8,128)(2,1)S(1)}, bf16[4,448,128]{2,1,0:T(8,128)(2,1)S(1)}, u32[]{:S(2)}, u32[]{:S(2)}) collective-permute-start(bf16[4,448,128]{2,1,0:T(8,128)(2,1)S(1)} %copy-done.10), channel_id=1, source_target_pairs={{0,12},{4,0},{8,4},{12,8},{1,13},{5,1},{9,5},{13,9},{2,14},{6,2},{... | collective-permute-start | bytes 1376264 | tf_op jit(solution)/shard_map/ppermute | solution.py:192
  38.1 7.1 %collective-permute-start.6 = (f32[160,512]{1,0:T(8,128)S(1)}, f32[160,512]{1,0:T(8,128)S(1)}, u32[]{:S(2)}, u32[]{:S(2)}) collective-permute-start(f32[160,512]{1,0:T(8,128)S(1)} %get-tuple-element.75), channel_id=1, source_target_pairs={{0,1},{1,0},{2,3},{3,2},{4,5},{5,4},{6,7},{7,6},{8,9},{9,8},{10,11... | collective-permute-start | bytes 983048 | tf_op jit(solution)/shard_map/ppermute | solution.py:584
  38.2 12.1 %collective-permute-start.9 = (bf16[4,448,128]{2,1,0:T(8,128)(2,1)S(1)}, bf16[4,448,128]{2,1,0:T(8,128)(2,1)S(1)}, u32[]{:S(2)}, u32[]{:S(2)}) collective-permute-start(bf16[4,448,128]{2,1,0:T(8,128)(2,1)S(1)} %collective-permute-done.7.refs_0_), channel_id=1, source_target_pairs={{0,16},{1,3},{2,18},{3,1},{16,0},{17,19},{18,2},{19,17},{4,20},{5,... | collective-permute-start | bytes 1376264 | tf_op jit(solution)/shard_map/ppermute | solution.py:593
  44.2 13.3 %collective-permute-start.10 = (bf16[4,448,128]{2,1,0:T(8,128)(2,1)S(1)}, bf16[4,448,128]{2,1,0:T(8,128)(2,1)S(1)}, u32[]{:S(2)}, u32[]{:S(2)}) collective-permute-start(bf16[4,448,128]{2,1,0:T(8,128)(2,1)S(1)} %collective-permute-done.8.refs_1_), channel_id=1, source_target_pairs={{0,16},{1,3},{2,18},{3,1},{16,0},{17,19},{18,2},{19,17},{4,20},{5,... | collective-permute-start | bytes 1376264 | tf_op jit(solution)/shard_map/ppermute | solution.py:593
  44.2 14.6 %collective-permute-start.16 = (bf16[4,448,128]{2,1,0:T(8,128)(2,1)S(1)}, bf16[4,448,128]{2,1,0:T(8,128)(2,1)S(1)}, u32[]{:S(2)}, u32[]{:S(2)}) collective-permute-start(bf16[4,448,128]{2,1,0:T(8,128)(2,1)S(1)} %copy-done.9), channel_id=1, source_target_pairs={{0,12},{4,0},{8,4},{12,8},{1,13},{5,1},{9,5},{13,9},{2,14},{6,2},{... | collective-permute-start | bytes 1376264 | tf_op jit(solution)/shard_map/ppermute | solution.py:192
  46.7 12.7 %collective-permute-start.15 = (bf16[4,448,128]{2,1,0:T(8,128)(2,1)S(1)}, bf16[4,448,128]{2,1,0:T(8,128)(2,1)S(1)}, u32[]{:S(2)}, u32[]{:S(2)}) collective-permute-start(bf16[4,448,128]{2,1,0:T(8,128)(2,1)S(1)} %collective-permute-done.12.refs_0_), channel_id=1, source_target_pairs={{0,2},{1,17},{2,0},{3,19},{16,18},{17,1},{18,16},{19,3},{4,6},{5,2... | collective-permute-start | bytes 1376264 | tf_op jit(solution)/shard_map/ppermute | solution.py:593
  49.8 9.7 %collective-permute-start.13 = (bf16[160,512]{1,0:T(8,128)(2,1)S(1)}, bf16[160,512]{1,0:T(8,128)(2,1)S(1)}, u32[]{:S(2)}, u32[]{:S(2)}) collective-permute-start(bf16[160,512]{1,0:T(8,128)(2,1)S(1)} %get-tuple-element.86), channel_id=1, source_target_pairs={{0,12},{4,0},{8,4},{12,8},{1,13},{5,1},{9,5},{13,9},{2,14},{6,2},{... | collective-permute-start | bytes 491528 | tf_op jit(solution)/shard_map/ppermute | solution.py:192
  58.7 2.7 %collective-permute-start.11 = (f32[160,512]{1,0:T(8,128)S(1)}, f32[160,512]{1,0:T(8,128)S(1)}, u32[]{:S(2)}, u32[]{:S(2)}) collective-permute-start(f32[160,512]{1,0:T(8,128)S(1)} %get-tuple-element.81), channel_id=1, source_target_pairs={{0,1},{1,0},{2,3},{3,2},{4,5},{5,4},{6,7},{7,6},{8,9},{9,8},{10,11... | collective-permute-start | bytes 983048 | tf_op jit(solution)/shard_map/ppermute | solution.py:584
  59.5 11.8 %collective-permute-start.17 = (bf16[4,448,128]{2,1,0:T(8,128)(2,1)S(1)}, bf16[4,448,128]{2,1,0:T(8,128)(2,1)S(1)}, u32[]{:S(2)}, u32[]{:S(2)}) collective-permute-start(bf16[4,448,128]{2,1,0:T(8,128)(2,1)S(1)} %collective-permute-done.16.refs_2_), channel_id=1, source_target_pairs={{0,2},{1,17},{2,0},{3,19},{16,18},{17,1},{18,16},{19,3},{4,6},{5,2... | collective-permute-start | bytes 1376264 | tf_op jit(solution)/shard_map/ppermute | solution.py:593
  61.5 9.8 %collective-permute-start.14 = (bf16[160,512]{1,0:T(8,128)(2,1)S(1)}, bf16[160,512]{1,0:T(8,128)(2,1)S(1)}, u32[]{:S(2)}, u32[]{:S(2)}) collective-permute-start(bf16[160,512]{1,0:T(8,128)(2,1)S(1)} %get-tuple-element.87), channel_id=1, source_target_pairs={{0,8},{4,12},{8,0},{12,4},{1,9},{5,13},{9,1},{13,5},{2,10},{6,14},... | collective-permute-start | bytes 491528 | tf_op jit(solution)/shard_map/ppermute | solution.py:192
  72.6 1.7 %collective-permute-start.18 = (f32[160,512]{1,0:T(8,128)S(1)}, f32[160,512]{1,0:T(8,128)S(1)}, u32[]{:S(2)}, u32[]{:S(2)}) collective-permute-start(f32[160,512]{1,0:T(8,128)S(1)} %get-tuple-element.94), channel_id=1, source_target_pairs={{0,1},{1,0},{2,3},{3,2},{4,5},{5,4},{6,7},{7,6},{8,9},{9,8},{10,11... | collective-permute-start | bytes 983048 | tf_op jit(solution)/shard_map/ppermute | solution.py:584
  72.7 10.2 %collective-permute-start.23 = (bf16[480,256]{1,0:T(8,128)(2,1)S(1)}, bf16[480,256]{1,0:T(8,128)(2,1)S(1)}, u32[]{:S(2)}, u32[]{:S(2)}) collective-permute-start(bf16[480,256]{1,0:T(8,128)(2,1)S(1)} %pad_maximum_fusion.refs_4_), channel_id=1, source_target_pairs={{0,2},{2,0},{1,3},{3,1},{4,6},{6,4},{5,7},{7,5},{8,10},{10,8},{9,1... | collective-permute-start | bytes 737288 | tf_op jit(solution)/shard_map/ppermute | solution.py:593
  74.4 8.5 %collective-permute-start.24 = (bf16[160,256]{1,0:T(8,128)(2,1)S(1)}, bf16[160,256]{1,0:T(8,128)(2,1)S(1)}, u32[]{:S(2)}, u32[]{:S(2)}) collective-permute-start(bf16[160,256]{1,0:T(8,128)(2,1)S(1)} %get-tuple-element.100), channel_id=1, source_target_pairs={{0,6},{1,7},{2,4},{3,5},{4,10},{5,11},{6,8},{7,9},{8,14},{9,15},{1... | collective-permute-start | bytes 245768 | tf_op jit(solution)/shard_map/ppermute | solution.py:605
  75.1 8.7 %collective-permute-start.20 = (bf16[160,256]{1,0:T(8,128)(2,1)S(1)}, bf16[160,256]{1,0:T(8,128)(2,1)S(1)}, u32[]{:S(2)}, u32[]{:S(2)}) collective-permute-start(bf16[160,256]{1,0:T(8,128)(2,1)S(1)} %get-tuple-element.100), channel_id=1, source_target_pairs={{0,4},{4,8},{8,12},{12,0},{1,5},{5,9},{9,13},{13,1},{2,6},{6,10},{... | collective-permute-start | bytes 245768 | tf_op jit(solution)/shard_map/ppermute | solution.py:192
  75.1 9.6 %collective-permute-start.19 = (bf16[160,256]{1,0:T(8,128)(2,1)S(1)}, bf16[160,256]{1,0:T(8,128)(2,1)S(1)}, u32[]{:S(2)}, u32[]{:S(2)}) collective-permute-start(bf16[160,256]{1,0:T(8,128)(2,1)S(1)} %get-tuple-element.98), channel_id=1, source_target_pairs={{0,4},{4,8},{8,12},{12,0},{1,5},{5,9},{9,13},{13,1},{2,6},{6,10},{... | collective-permute-start | bytes 245768 | tf_op jit(solution)/shard_map/ppermute | solution.py:192
  79.0 6.2 %collective-permute-start.21 = (bf16[480,256]{1,0:T(8,128)(2,1)S(1)}, bf16[480,256]{1,0:T(8,128)(2,1)S(1)}, u32[]{:S(2)}, u32[]{:S(2)}) collective-permute-start(bf16[480,256]{1,0:T(8,128)(2,1)S(1)} %pad_maximum_fusion.refs_4_), channel_id=1, source_target_pairs={{0,1},{1,0},{2,3},{3,2},{4,5},{5,4},{6,7},{7,6},{8,9},{9,8},{10,11... | collective-permute-start | bytes 737288 | tf_op jit(solution)/shard_map/ppermute | solution.py:584
  84.8 1.8 %collective-permute-start.25 = (bf16[480,256]{1,0:T(8,128)(2,1)S(1)}, bf16[480,256]{1,0:T(8,128)(2,1)S(1)}, u32[]{:S(2)}, u32[]{:S(2)}) collective-permute-start(bf16[480,256]{1,0:T(8,128)(2,1)S(1)} %collective-permute-done.23.refs_8_), channel_id=1, source_target_pairs={{0,1},{1,0},{2,3},{3,2},{4,5},{5,4},{6,7},{7,6},{8,9},{9,8},{10,11... | collective-permute-start | bytes 737288 | tf_op jit(solution)/shard_map/ppermute | solution.py:584
  84.8 1.6 %collective-permute-start.26 = (bf16[160,256]{1,0:T(8,128)(2,1)S(1)}, bf16[160,256]{1,0:T(8,128)(2,1)S(1)}, u32[]{:S(2)}, u32[]{:S(2)}) collective-permute-start(bf16[160,256]{1,0:T(8,128)(2,1)S(1)} %collective-permute-done.24.refs_9_), channel_id=1, source_target_pairs={{0,1},{1,0},{2,3},{3,2},{4,5},{5,4},{6,7},{7,6},{8,9},{9,8},{10,11... | collective-permute-start | bytes 245768 | tf_op jit(solution)/shard_map/ppermute | solution.py:584
  85.3 1.3 %collective-permute-start.22 = (bf16[160,256]{1,0:T(8,128)(2,1)S(1)}, bf16[160,256]{1,0:T(8,128)(2,1)S(1)}, u32[]{:S(2)}, u32[]{:S(2)}) collective-permute-start(bf16[160,256]{1,0:T(8,128)(2,1)S(1)} %collective-permute-done.20.refs_5_), channel_id=1, source_target_pairs={{0,1},{1,0},{2,3},{3,2},{4,5},{5,4},{6,7},{7,6},{8,9},{9,8},{10,11... | collective-permute-start | bytes 245768 | tf_op jit(solution)/shard_map/ppermute | solution.py:584
  91.9 1.7 %collective-permute-start.27 = (bf16[640,256]{1,0:T(8,128)(2,1)S(1)}, bf16[640,256]{1,0:T(8,128)(2,1)S(1)}, u32[]{:S(2)}, u32[]{:S(2)}) collective-permute-start(bf16[640,256]{1,0:T(8,128)(2,1)S(1)} %get-tuple-element.104), channel_id=1, source_target_pairs={{0,1},{1,0},{2,3},{3,2},{4,5},{5,4},{6,7},{7,6},{8,9},{9,8},{10,11... | collective-permute-start | bytes 983048 | tf_op jit(solution)/shard_map/ppermute | solution.py:584
  93.6 10.4 %collective-permute-start.28 = (bf16[640,256]{1,0:T(8,128)(2,1)S(1)}, bf16[640,256]{1,0:T(8,128)(2,1)S(1)}, u32[]{:S(2)}, u32[]{:S(2)}) collective-permute-start(bf16[640,256]{1,0:T(8,128)(2,1)S(1)} %add_convert_fusion.1), channel_id=1, source_target_pairs={{0,2},{2,0},{1,3},{3,1},{4,6},{6,4},{5,7},{7,5},{8,10},{10,8},{9,1... | collective-permute-start | bytes 983048 | tf_op jit(solution)/shard_map/ppermute | solution.py:584
  96.1 8.0 %collective-permute-start.32 = (bf16[640,256]{1,0:T(8,128)(2,1)S(1)}, bf16[640,256]{1,0:T(8,128)(2,1)S(1)}, u32[]{:S(2)}, u32[]{:S(2)}) collective-permute-start(bf16[640,256]{1,0:T(8,128)(2,1)S(1)} %get-tuple-element.118), channel_id=1, source_target_pairs={{0,1},{1,0},{2,3},{3,2},{4,5},{5,4},{6,7},{7,6},{8,9},{9,8},{10,11... | collective-permute-start | bytes 983048 | tf_op jit(solution)/shard_map/ppermute | solution.py:584
  96.2 4.1 %collective-permute-start.31 = (bf16[160,128]{1,0:T(8,128)(2,1)S(1)}, bf16[160,128]{1,0:T(8,128)(2,1)S(1)}, u32[]{:S(2)}, u32[]{:S(2)}) collective-permute-start(bf16[160,128]{1,0:T(8,128)(2,1)S(1)} %get-tuple-element.129), channel_id=1, source_target_pairs={{0,12},{4,0},{8,4},{12,8},{1,13},{5,1},{9,5},{13,9},{2,14},{6,2},{... | collective-permute-start | bytes 122888 | tf_op jit(solution)/shard_map/ppermute | solution.py:192
  97.9 6.2 %collective-permute-start.30 = (bf16[160,128]{1,0:T(8,128)(2,1)S(1)}, bf16[160,128]{1,0:T(8,128)(2,1)S(1)}, u32[]{:S(2)}, u32[]{:S(2)}) collective-permute-start(bf16[160,128]{1,0:T(8,128)(2,1)S(1)} %get-tuple-element.130), channel_id=1, source_target_pairs={{0,8},{4,12},{8,0},{12,4},{1,9},{5,13},{9,1},{13,5},{2,10},{6,14},... | collective-permute-start | bytes 122888 | tf_op jit(solution)/shard_map/ppermute | solution.py:192
  97.9 6.2 %collective-permute-start.29 = (bf16[160,128]{1,0:T(8,128)(2,1)S(1)}, bf16[160,128]{1,0:T(8,128)(2,1)S(1)}, u32[]{:S(2)}, u32[]{:S(2)}) collective-permute-start(bf16[160,128]{1,0:T(8,128)(2,1)S(1)} %get-tuple-element.131), channel_id=1, source_target_pairs={{0,4},{4,8},{8,12},{12,0},{1,5},{5,9},{9,13},{13,1},{2,6},{6,10},{... | collective-permute-start | bytes 122888 | tf_op jit(solution)/shard_map/ppermute | solution.py:192
  104.2 5.4 %collective-permute-start.35 = (bf16[160,256]{1,0:T(8,128)(2,1)S(1)}, bf16[160,256]{1,0:T(8,128)(2,1)S(1)}, u32[]{:S(2)}, u32[]{:S(2)}) collective-permute-start(bf16[160,256]{1,0:T(8,128)(2,1)S(1)} %get-tuple-element.125), channel_id=1, source_target_pairs={{0,12},{4,0},{8,4},{12,8},{1,13},{5,1},{9,5},{13,9},{2,14},{6,2},{... | collective-permute-start | bytes 245768 | tf_op jit(solution)/shard_map/ppermute | solution.py:192
  105.3 8.0 %collective-permute-start.34 = (bf16[160,256]{1,0:T(8,128)(2,1)S(1)}, bf16[160,256]{1,0:T(8,128)(2,1)S(1)}, u32[]{:S(2)}, u32[]{:S(2)}) collective-permute-start(bf16[160,256]{1,0:T(8,128)(2,1)S(1)} %get-tuple-element.126), channel_id=1, source_target_pairs={{0,8},{4,12},{8,0},{12,4},{1,9},{5,13},{9,1},{13,5},{2,10},{6,14},... | collective-permute-start | bytes 245768 | tf_op jit(solution)/shard_map/ppermute | solution.py:192
  105.3 8.0 %collective-permute-start.33 = (bf16[160,256]{1,0:T(8,128)(2,1)S(1)}, bf16[160,256]{1,0:T(8,128)(2,1)S(1)}, u32[]{:S(2)}, u32[]{:S(2)}) collective-permute-start(bf16[160,256]{1,0:T(8,128)(2,1)S(1)} %get-tuple-element.127), channel_id=1, source_target_pairs={{0,4},{4,8},{8,12},{12,0},{1,5},{5,9},{9,13},{13,1},{2,6},{6,10},{... | collective-permute-start | bytes 245768 | tf_op jit(solution)/shard_map/ppermute | solution.py:192
  114.0 1.9 %collective-permute-start.36 = (bf16[160,1536]{1,0:T(8,128)(2,1)S(1)}, bf16[160,1536]{1,0:T(8,128)(2,1)S(1)}, u32[]{:S(2)}, u32[]{:S(2)}) collective-permute-start(bf16[160,1536]{1,0:T(8,128)(2,1)S(1)} %unfinish.1.grads), channel_id=1, source_target_pairs={{0,1},{1,0},{2,3},{3,2},{4,5},{5,4},{6,7},{7,6},{8,9},{9,8},{10,11... | collective-permute-start | bytes 1474568 | tf_op jit(solution)/shard_map/ppermute | solution.py:584
  117.7 2.1 %copy-start.2 = (bf16[160,3584]{1,0:T(8,128)(2,1)S(1)}, bf16[160,3584]{1,0:T(8,128)(2,1)}, u32[]{:S(2)}) copy-start(bf16[160,3584]{1,0:T(8,128)(2,1)} %x_ref.2) | copy-start | bytes 3440644
  117.7 2.1 %copy-start.4 = (bf16[160,3584]{1,0:T(8,128)(2,1)S(1)}, bf16[160,3584]{1,0:T(8,128)(2,1)}, u32[]{:S(2)}) copy-start(bf16[160,3584]{1,0:T(8,128)(2,1)} %c_ref.3) | copy-start | bytes 3440644
  117.7 2.1 %copy-start.7 = (f32[3,3584]{1,0:T(4,128)S(1)}, f32[3,3584]{1,0:T(4,128)}, u32[]{:S(2)}) copy-start(f32[3,3584]{1,0:T(4,128)} %mod_ref.3) | copy-start | bytes 129028
  117.8 2.0 %collective-permute-start.37 = (bf16[160,1792]{1,0:T(8,128)(2,1)S(1)}, bf16[160,1792]{1,0:T(8,128)(2,1)S(1)}, u32[]{:S(2)}, u32[]{:S(2)}) collective-permute-start(bf16[160,1792]{1,0:T(8,128)(2,1)S(1)} %back_project.3), channel_id=1, source_target_pairs={{0,1},{1,0},{2,3},{3,2},{4,5},{5,4},{6,7},{7,6},{8,9},{9,8},{10,11... | collective-permute-start | bytes 1720328 | tf_op jit(solution)/shard_map/ppermute | solution.py:584
